TPU v7x, 128 devices: a whole 4x4x4 slice. The times are simulated.
128 devices in a mesh: row: 8 (over x, core), col: 16 (over z, y).
Axes of the slice: x: 4, y: 4, z: 4, core: 2. Of those that a mesh axis runs over, the one named last changes fastest.
Arguments:
- features: bfloat16 [131072, 128], P(('row', 'col')), may hold values from -6 to 6
- cotangent: bfloat16 [131072, 256], P(('row', 'col')), may hold values from -6 to 6
- w_self: bfloat16 [128, 256], replicated, may hold values from -0.5 to 0.5
- w_neigh: bfloat16 [128, 256], replicated, may hold values from -0.5 to 0.5
- bias: float32 [256], replicated, may hold values from -4 to 4
- src_slot: int32 [1048576], P(('row', 'col')), may hold values from 0 to 2047, as said below
- dst_slot: int32 [1048576], P(('row', 'col')), may hold values from 0 to 2047, as said below
- edge_live: int32 [128], P(('row', 'col')), may hold values from 2048 to 8192, as said below
- mirror_list: int32 [128, 128, 8], P(('row', 'col')), may hold values from -1 to 1023, as said below
Outputs:
- activation: bfloat16 [131072, 256], P(('row', 'col'))
- grad_features: bfloat16 [131072, 128], P(('row', 'col'))
- grad_w_self: float32 [128, 256], replicated
- grad_w_neigh: float32 [128, 256], replicated
- grad_bias: float32 [256], replicated
Inputs may be any that keep to these rules, and one draw needn't show every extreme that they name: In each list mirror_list[q, p, :] the entries other than -1 come first, number 1 to 8, and are distinct; some device p receives 8 rows from every device q. `src_slot`: each slot is below 1024 or names a mirror slot 1024 + q * 8 + j of its device p with mirror_list[q, p, j] not -1. `dst_slot`: each slot is below 1024 or names a mirror slot 1024 + q * 8 + j of its device p with mirror_list[q, p, j] not -1. `edge_live`: some device has all 8192 edges live.
All inputs are finite; a program needn't handle non-finite values.
Results may differ from a plain program's by a relative error of at most 0.0075.
Values may be sent and summed in bfloat16 or wider, within the bound.
No kernel may reach another device: no remote copies, remote signals or barrier semaphores. Data moves between devices by JAX's collectives and lax.ppermute only.
A program may use at most 64 MiB of HBM per device.

v0:
```python
import jax
import jax.numpy as jnp
from jax import lax
from jax.sharding import PartitionSpec as P


def pull_rows(rows, safe_list, used):
    peers, slots = safe_list.shape
    width = rows.shape[1]
    outgoing = jnp.where(used[:, :, None], rows[safe_list], jnp.zeros((), rows.dtype))
    arrived = lax.all_to_all(outgoing, ("row", "col"), split_axis=0, concat_axis=0, tiled=True)
    return jnp.concatenate([rows, arrived.reshape(peers * slots, width)], axis=0)


def edge_spread(table, take, put, live, total):
    width = table.shape[1]
    edges = take.shape[0]
    turns = 16
    block = edges // turns
    rows = jnp.where(live[:, None], table[take], jnp.zeros((), table.dtype)).reshape(
        turns, block, width
    )
    places = put.reshape(turns, block)
    flags = live.reshape(turns, block)
    columns = jnp.arange(total, dtype=jnp.int32)

    def one_block(carry, items):
        piece, where, alive = items
        hot = ((where[:, None] == columns[None, :]) & alive[:, None]).astype(jnp.bfloat16)
        added = lax.dot_general(
            hot, piece, (((0,), (0,)), ((), ())), preferred_element_type=jnp.float32
        )
        counted = jnp.sum(hot, axis=0, dtype=jnp.float32)
        return ((carry[0] + added, carry[1] + counted), None)

    start = (jnp.zeros((total, width), jnp.float32), jnp.zeros((total,), jnp.float32))
    result, _ = lax.scan(one_block, start, (rows, places, flags))
    return result


def master_add(received, safe_list, used, vdev):
    width = received.shape[-1]
    kept = received.reshape(-1, width)
    hot = (
        (safe_list.reshape(-1)[:, None] == jnp.arange(vdev, dtype=jnp.int32)[None, :])
        & used.reshape(-1)[:, None]
    ).astype(jnp.float32)
    return lax.dot_general(
        hot,
        kept,
        (((0,), (0,)), ((), ())),
        precision=lax.Precision.HIGHEST,
        preferred_element_type=jnp.float32,
    )


def local(features, cotangent, w_self, w_neigh, bias, src_slot, dst_slot, edge_live, mirror_list):
    vdev, width = features.shape
    lists = mirror_list[0]
    peers, slots = lists.shape
    used = lists >= 0
    safe_list = jnp.where(used, lists, 0)
    total = vdev + peers * slots
    live = jnp.arange(src_slot.shape[0], dtype=jnp.int32) < edge_live[0]
    table = pull_rows(features, safe_list, used)
    sums, tallies = edge_spread(table, src_slot, dst_slot, live, total)
    mirror_sums = sums[vdev:].reshape(peers, slots, width)
    mirror_tallies = tallies[vdev:].reshape(peers, slots)
    got_sums, got_tallies = (
        lax.all_to_all(
            mirror_sums.astype(jnp.bfloat16),
            ("row", "col"),
            split_axis=0,
            concat_axis=0,
            tiled=True,
        ).astype(mirror_sums.dtype),
        lax.all_to_all(
            mirror_tallies.astype(jnp.bfloat16),
            ("row", "col"),
            split_axis=0,
            concat_axis=0,
            tiled=True,
        ).astype(mirror_tallies.dtype),
    )
    joined = jnp.concatenate([got_sums, got_tallies[:, :, None]], axis=2)
    folded = master_add(joined, safe_list, used, vdev)
    neighbour = sums[:vdev] + folded[:, :width]
    degree = tallies[:vdev] + folded[:, width]
    inverse = 1.0 / jnp.maximum(degree, 1.0)
    aggregate = (neighbour * inverse[:, None]).astype(jnp.bfloat16)
    pre = (
        jnp.dot(features, w_self, preferred_element_type=jnp.float32)
        + jnp.dot(aggregate, w_neigh, preferred_element_type=jnp.float32)
        + bias
    )
    sig = jax.nn.sigmoid(pre)
    activation = (pre * sig).astype(jnp.bfloat16)
    grad_pre = (cotangent.astype(jnp.float32) * sig * (1.0 + pre * (1.0 - sig))).astype(
        jnp.bfloat16
    )
    term_self = lax.dot_general(
        features, grad_pre, (((0,), (0,)), ((), ())), preferred_element_type=jnp.float32
    )
    term_neigh = lax.dot_general(
        aggregate, grad_pre, (((0,), (0,)), ((), ())), preferred_element_type=jnp.float32
    )
    term_bias = jnp.sum(grad_pre.astype(jnp.float32), axis=0)
    grad_w_self, grad_w_neigh, grad_bias = lax.psum(
        (term_self, term_neigh, term_bias), ("row", "col")
    )
    message = (
        lax.dot_general(
            grad_pre, w_neigh, (((1,), (1,)), ((), ())), preferred_element_type=jnp.float32
        )
        * inverse[:, None]
    ).astype(jnp.bfloat16)
    back_table = pull_rows(message, safe_list, used)
    spread, _ = edge_spread(back_table, dst_slot, src_slot, live, total)
    mirror_spread = spread[vdev:].reshape(peers, slots, width)
    got_spread = lax.all_to_all(
        mirror_spread.astype(jnp.bfloat16), ("row", "col"), split_axis=0, concat_axis=0, tiled=True
    ).astype(mirror_spread.dtype)
    own_grad = lax.dot_general(
        grad_pre, w_self, (((1,), (1,)), ((), ())), preferred_element_type=jnp.float32
    )
    grad_features = (
        own_grad + spread[:vdev] + master_add(got_spread, safe_list, used, vdev)
    ).astype(jnp.bfloat16)
    return (activation, grad_features, grad_w_self, grad_w_neigh, grad_bias)


def solution(mesh):
    placed = (
        P(("row", "col"), None),
        P(("row", "col"), None),
        P(),
        P(),
        P(),
        P(("row", "col")),
        P(("row", "col")),
        P(("row", "col")),
        P(("row", "col"), None, None),
    )
    return jax.shard_map(
        local,
        mesh=mesh,
        in_specs=placed,
        out_specs=(P(("row", "col"), None), P(("row", "col"), None), P(), P(), P()),
        check_vma=False,
    )
```

profile of v0, /device:TPU:1, one launch (start us, length us, event | category | flops | bytes accessed | tf_op | source)
XLA Modules:
  0.0 446.1 jit_solution(16063865505967131727)
XLA Ops:
  9.0 3.9 gather_fusion
  13.8 11.5 %all-to-all-start = ((bf16[128,8,128]{2,1,0:T(8,128)(2,1)}), bf16[128,8,128]{2,1,0:T(8,128)(2,1)S(1)}, u32[]{:S(2)}, u32[]{:S(2)}) async-start(bf16[128,8,128]{2,1,0:T(8,128)(2,1)} %bitcast_select_fusion.1), calls=%async_computation | async-start | bytes 524288 | tf_op jit(solution)/shard_map/all_to_all | solution.py:11
  26.8 9.9 %all-to-all-done = bf16[128,8,128]{2,1,0:T(8,128)(2,1)S(1)} async-done(((bf16[128,8,128]{2,1,0:T(8,128)(2,1)}), bf16[128,8,128]{2,1,0:T(8,128)(2,1)S(1)}, u32[]{:S(2)}, u32[]{:S(2)}) %all-to-all-start) | async-done | bytes 262176 | tf_op jit(solution)/shard_map/all_to_all | solution.py:11
  36.8 24.0 %gather_fusion.1 = bf16[8192,128]{1,0:T(8,128)(2,1)S(1)} fusion(bf16[2048,128]{1,0:T(8,128)(2,1)S(1)} %pad_maximum_fusion, s32[8192]{0:T(1024)S(1)} %fusion.52), kind=kCustom, calls=%fused_computation.1 | custom fusion | bytes 4227072 | tf_op jit(solution)/shard_map/gather | solution.py:20
  63.5 59.1 %while.24 = (s32[]{:T(128)}, f32[2048,128]{1,0:T(8,128)S(1)}, f32[2048]{0:T(1024)S(1)}, s32[16,512]{1,0:T(8,128)S(1)}, pred[16,512]{1,0:T(8,128)(4,1)S(1)}, /*in...) while((s32[]{:T(128)}, f32[2048,128]{1,0:T(8,128)S(1)}, f32[2048]{0:T(1024)S(1)}, ...), condition=%wide.region_2.3_spmd.clone, body=%wide.region_0.2_spmd.clone.sunk | while | flops 276301824 | bytes 2271848 | solution.py:37
  63.6 2.7 fusion.77
  71.0 2.7 fusion.77
  74.7 2.7 fusion.77
  78.4 2.7 fusion.77
  82.1 2.7 fusion.77
  85.8 2.7 fusion.77
  89.5 2.7 fusion.77
  93.2 2.7 fusion.77
  96.9 2.7 fusion.77
  100.6 2.7 fusion.77
  104.3 2.7 fusion.77
  108.0 2.7 fusion.77
  111.6 2.7 fusion.77
  115.3 2.7 fusion.77
  119.0 2.7 fusion.77
  123.5 4.0 all-to-all-start.2
  128.2 9.0 %all-to-all-done.2 = bf16[128,1,8]{2,1,0:T(2,128)(2,1)S(1)} async-done(((bf16[128,1,8]{2,1,0:T(2,128)(2,1)}), bf16[128,1,8]{2,1,0:T(2,128)(2,1)S(1)}, u32[]{:S(2)}, u32[]{:S(2)}) %all-to-all-start.2) | async-done | bytes 2080 | tf_op jit(solution)/shard_map/all_to_all | solution.py:77
  137.2 5.2 %all-to-all-start.1 = ((bf16[128,8,128]{2,1,0:T(8,128)(2,1)}), bf16[128,8,128]{2,1,0:T(8,128)(2,1)}, u32[]{:S(2)}, u32[]{:S(2)}) async-start(bf16[128,8,128]{2,1,0:T(8,128)(2,1)} %fusion.49), calls=%async_computation.1 | async-start | bytes 524288 | tf_op jit(solution)/shard_map/all_to_all | solution.py:70
  144.7 9.0 %all-to-all-done.1 = bf16[128,8,128]{2,1,0:T(8,128)(2,1)} async-done(((bf16[128,8,128]{2,1,0:T(8,128)(2,1)}), bf16[128,8,128]{2,1,0:T(8,128)(2,1)}, u32[]{:S(2)}, u32[]{:S(2)}) %all-to-all-start.1) | async-done | bytes 262176 | tf_op jit(solution)/shard_map/all_to_all | solution.py:70
  159.0 3.2 gather_fusion.2
  163.1 4.0 all-to-all-start.3
  168.2 67.4 %psum.23 = f32[256]{0:T(256)} all-reduce(f32[256]{0:T(256)S(1)} %get-tuple-element.165), channel_id=1, replica_groups=mesh['row'=8,'col'=16] {'row','col'}, use_global_device_ids=true, to_apply=%region_8.9 | all-reduce | flops 256 | bytes 2048 | tf_op jit(solution)/shard_map/psum | solution.py:108
  235.7 81.3 %all-reduce.3.cloned.1.call-done = (f32[128,256]{0,1:T(8,128)}, f32[128,256]{1,0:T(8,128)}) async-done(((f32[128,256]{0,1:T(8,128)}, f32[128,256]{1,0:T(8,128)}), (f32[128,256]{0,1:T(8,128)}, f32[128,256]{1,0:T(8,128)})) %all-reduce.3.cloned.1.call-update) | async-done | bytes 262160 | tf_op jit(solution)/shard_map/psum | solution.py:108
  319.1 24.0 %gather_fusion.3 = bf16[8192,128]{1,0:T(8,128)(2,1)S(1)} fusion(bf16[2048,128]{1,0:T(8,128)(2,1)S(1)} %copy.53, s32[8192]{0:T(1024)S(1)} %fusion.53), kind=kCustom, calls=%fused_computation.3 | custom fusion | bytes 4227072 | tf_op jit(solution)/shard_map/gather | solution.py:20
  345.9 71.2 %while.25 = (s32[]{:T(128)}, f32[2048,128]{1,0:T(8,128)}, s32[16,512]{1,0:T(8,128)}, pred[16,512]{1,0:T(8,128)(4,1)S(1)}, bf16[16,512,128]{2,1,0:T(8,128)(2,1)}, /*index=5*/s32[]{:T(128)}, s32[]{:T(128)}) while((s32[]{:T(128)}, f32[2048,128]{1,0:T(8,128)}, s32[16,512]{1,0:T(8,128)}, pred[16,512]{1,0:T(8,128)(4,1)S(1)}, ...), condition=%wide.region_4.5_spmd.clone, body=%wide.region_3.4_spmd.clone.sunk | while | flops 271056896 | bytes 2236511 | solution.py:37
  346.7 3.3 fusion.80
  350.7 3.7 fusion.80
  355.2 3.7 fusion.80
  359.7 3.7 fusion.80
  364.2 3.7 fusion.80
  368.6 3.7 fusion.80
  373.1 3.7 fusion.80
  377.6 3.7 fusion.80
  382.1 3.7 fusion.80
  386.5 3.7 fusion.80
  391.0 3.7 fusion.80
  395.5 3.7 fusion.80
  399.9 3.7 fusion.80
  404.4 3.7 fusion.80
  408.9 3.7 fusion.80
  413.4 3.7 fusion.80
  418.9 6.0 %all-to-all-start.4 = ((bf16[128,8,128]{2,1,0:T(8,128)(2,1)}), bf16[128,8,128]{2,1,0:T(8,128)(2,1)S(1)}, u32[]{:S(2)}, u32[]{:S(2)}) async-start(bf16[128,8,128]{2,1,0:T(8,128)(2,1)} %fusion.50), calls=%async_computation.4 | async-start | bytes 524288 | tf_op jit(solution)/shard_map/all_to_all | solution.py:120
  426.2 10.1 %all-to-all-done.4 = bf16[128,8,128]{2,1,0:T(8,128)(2,1)S(1)} async-done(((bf16[128,8,128]{2,1,0:T(8,128)(2,1)}), bf16[128,8,128]{2,1,0:T(8,128)(2,1)S(1)}, u32[]{:S(2)}, u32[]{:S(2)}) %all-to-all-start.4) | async-done | bytes 262176 | tf_op jit(solution)/shard_map/all_to_all | solution.py:120
  (185 shorter events, 57.4 us)
Async XLA Ops:
  7.2 148.9 %copy-start = (bf16[128,256]{1,0:T(8,128)(2,1)S(1)}, bf16[128,256]{1,0:T(8,128)(2,1)}, u32[]{:S(2)}) copy-start(bf16[128,256]{1,0:T(8,128)(2,1)} %param.16) | copy-start | bytes 196612
  7.2 18.1 %copy-start.14 = (s32[1,128,8]{1,2,0:T(8,128)S(1)}, s32[1,128,8]{1,2,0:T(8,128)}, u32[]{:S(2)}) copy-start(s32[1,128,8]{1,2,0:T(8,128)} %param.21) | copy-start | bytes 12292
  7.2 29.6 %copy-start.1 = (bf16[1024,128]{1,0:T(8,128)(2,1)S(1)}, bf16[1024,128]{1,0:T(8,128)(2,1)}, u32[]{:S(2)}) copy-start(bf16[1024,128]{1,0:T(8,128)(2,1)} %param.13) | copy-start | bytes 786436
  7.2 19.6 %copy-start.12 = (s32[8192]{0:T(1024)S(1)}, s32[8192]{0:T(1024)}, u32[]{:S(2)}) copy-start(s32[8192]{0:T(1024)} %param.19) | copy-start | bytes 98308
  7.2 19.6 %copy-start.10 = (s32[8192]{0:T(1024)S(1)}, s32[8192]{0:T(1024)}, u32[]{:S(2)}) copy-start(s32[8192]{0:T(1024)} %param.18) | copy-start | bytes 98308
  9.0 4.8 %copy-start.7 = (pred[128,8]{1,0:T(8,128)(4,1)}, pred[128,8]{1,0:T(8,128)(4,1)S(1)}, u32[]{:S(2)}) copy-start(pred[128,8]{1,0:T(8,128)(4,1)S(1)} %copy.44) | copy-start | bytes 3076
  13.8 22.9 %all-to-all-start = ((bf16[128,8,128]{2,1,0:T(8,128)(2,1)}), bf16[128,8,128]{2,1,0:T(8,128)(2,1)S(1)}, u32[]{:S(2)}, u32[]{:S(2)}) async-start(bf16[128,8,128]{2,1,0:T(8,128)(2,1)} %bitcast_select_fusion.1), calls=%async_computation | async-start | bytes 524288 | tf_op jit(solution)/shard_map/all_to_all | solution.py:11
  60.8 2.7 copy-start.2
  63.5 79.5 %copy-start.11 = (s32[8192]{0:T(1024)S(1)}, s32[8192]{0:T(1024)}, u32[]{:S(2)}) copy-start(s32[8192]{0:T(1024)} %param.18) | copy-start | bytes 98308
  63.5 80.1 %copy-start.3 = (bf16[128,256]{1,0:T(8,128)(2,1)S(1)}, bf16[128,256]{1,0:T(8,128)(2,1)}, u32[]{:S(2)}) copy-start(bf16[128,256]{1,0:T(8,128)(2,1)} %param.15) | copy-start | bytes 196612
  122.7 0.8 copy-start.5
  123.5 13.7 %all-to-all-start.2 = ((bf16[128,1,8]{2,1,0:T(2,128)(2,1)}), bf16[128,1,8]{2,1,0:T(2,128)(2,1)S(1)}, u32[]{:S(2)}, u32[]{:S(2)}) async-start(bf16[128,1,8]{2,1,0:T(2,128)(2,1)} %all_to_all.24), calls=%async_computation.2 | async-start | bytes 131072 | tf_op jit(solution)/shard_map/all_to_all | solution.py:77
  137.2 16.5 %all-to-all-start.1 = ((bf16[128,8,128]{2,1,0:T(8,128)(2,1)}), bf16[128,8,128]{2,1,0:T(8,128)(2,1)}, u32[]{:S(2)}, u32[]{:S(2)}) async-start(bf16[128,8,128]{2,1,0:T(8,128)(2,1)} %fusion.49), calls=%async_computation.1 | async-start | bytes 524288 | tf_op jit(solution)/shard_map/all_to_all | solution.py:70
  143.0 10.6 %copy-start.15 = (s32[1024]{0:T(1024)S(1)}, s32[1024]{0:T(1024)}, u32[]{:S(2)}) copy-start(s32[1024]{0:T(1024)} %broadcast_select_fusion.2) | copy-start | bytes 12292
  153.7 2.4 copy-start.17
  153.7 2.4 copy-start.18
  158.5 3.7 copy-start.8
  159.0 9.2 %copy-start.13 = (s32[8192]{0:T(1024)S(1)}, s32[8192]{0:T(1024)}, u32[]{:S(2)}) copy-start(s32[8192]{0:T(1024)} %param.19) | copy-start | bytes 98308
  163.1 155.5 %all-to-all-start.3 = ((bf16[128,8,128]{2,1,0:T(8,128)(2,1)}), bf16[128,8,128]{2,1,0:T(8,128)(2,1)S(1)}, u32[]{:S(2)}, u32[]{:S(2)}) async-start(bf16[128,8,128]{2,1,0:T(8,128)(2,1)} %bitcast_select_fusion), calls=%async_computation.3 | async-start | bytes 524288 | tf_op jit(solution)/shard_map/all_to_all | solution.py:11
  167.1 149.8 %all-reduce.3.cloned.1.call-start = ((), (), s32[]{:S(2)}) async-start(), calls=%async_computation.5 | async-start | bytes 524288 | tf_op jit(solution)/shard_map/psum | solution.py:108
  319.1 24.1 %copy-start.6 = (pred[16,512]{1,0:T(8,128)(4,1)S(1)}, pred[16,512]{1,0:T(8,128)(4,1)}, u32[]{:S(2)}) copy-start(pred[16,512]{1,0:T(8,128)(4,1)} %copy-done.5) | copy-start | bytes 24580
  345.9 79.0 %copy-start.4 = (bf16[128,256]{1,0:T(8,128)(2,1)S(1)}, bf16[128,256]{1,0:T(8,128)(2,1)}, u32[]{:S(2)}) copy-start(bf16[128,256]{1,0:T(8,128)(2,1)} %param.15) | copy-start | bytes 196612
  417.1 19.2 %copy-start.16 = (pred[1024]{0:T(1024)(128)(4,1)S(1)}, pred[1024]{0:T(1024)(128)(4,1)}, u32[]{:S(2)}) copy-start(pred[1024]{0:T(1024)(128)(4,1)} %broadcast_compare_fusion) | copy-start | bytes 3076
  418.9 17.4 %all-to-all-start.4 = ((bf16[128,8,128]{2,1,0:T(8,128)(2,1)}), bf16[128,8,128]{2,1,0:T(8,128)(2,1)S(1)}, u32[]{:S(2)}, u32[]{:S(2)}) async-start(bf16[128,8,128]{2,1,0:T(8,128)(2,1)} %fusion.50), calls=%async_computation.4 | async-start | bytes 524288 | tf_op jit(solution)/shard_map/all_to_all | solution.py:120
  424.8 13.7 %copy-start.9 = (f32[128,256]{1,0:T(8,128)S(1)}, f32[128,256]{1,0:T(8,128)}, u32[]{:S(2)}) copy-start(f32[128,256]{1,0:T(8,128)} %get-tuple-element.284) | copy-start | bytes 393220
Sparse Core Ops, SparseCore 0:
  173.5 143.4 all-reduce.2
where the time goes:
time: 448 us; the launch traced here: 446 us
  waiting for transfers between devices  119 us (27%)
  matrix products  113 us (25%)
  local copies, waits for them, and re-layouts  75.8 us (17%)
  blocking collectives  67.4 us (15%)
  starting transfers between devices  30.7 us (7%)
  other arithmetic  24.1 us (5%)
  between operations  15.1 us (3%)
    dot_general x32, matrix products, one_block(): lax.dot_general(hot, piece, (((0,), (0,)), ((), ())), preferred_element_t...  103 us
    psum x1, waiting for transfers between devices, local(): lax.psum((term_self, term_neigh, term_bias), ('row', 'col'))  81.3 us
    psum x1, blocking collectives, local(): lax.psum((term_self, term_neigh, term_bias), ('row', 'col'))  67.4 us
    gather x2, local copies, waits for them, and re-layouts, edge_spread(): table[take]  48.1 us
    all_to_all x2, starting transfers between devices, pull_rows(): lax.all_to_all(outgoing, ('row', 'col'), split_axis=0, concat_axis=0, til...  15.5 us
    reduce_sum x16, other arithmetic, one_block(): counted = jnp.sum(hot, axis=0, dtype=jnp.float32)  13.7 us
    dynamic_slice x64, local copies, waits for them, and re-layouts, edge_spread(): result, _ = lax.scan(one_block, start, (rows, places, flags))  12.7 us
    all_to_all x1, waiting for transfers between devices, local(): lax.all_to_all(mirror_spread.astype(jnp.bfloat16), ('row', 'col'), split_...  10.1 us
  transfers between devices with their start and end apart: 6, of which 5 were waited for; matrix products, arithmetic and copies ran while one was open for 2% of the time, Pallas kernels for 0%

commit v1 on v0

v1 whole, which is shorter than its diff:
```python
import jax
import jax.numpy as jnp
from jax import lax
from jax.experimental import pallas as pl
from jax.experimental.pallas import tpu as pltpu
from jax.sharding import PartitionSpec as P

F32 = jnp.float32
BF16 = jnp.bfloat16
AXES = ("row", "col")

MASTERS = 1024
MIRRORS = 1024
SLOTS = MASTERS + MIRRORS
EDGES = 8192
PEERS = 128
F = 128
H = 256
LANES = 128
COPIES = 4
TURN = 64
WORDS = SLOTS * (SLOTS // 512)


def dot(a, b):
    return jnp.dot(a, b, preferred_element_type=F32)


def dot_nt(a, b):
    return lax.dot_general(a, b, (((1,), (1,)), ((), ())), preferred_element_type=F32)


def dot_tn(a, b):
    return lax.dot_general(a, b, (((0,), (0,)), ((), ())), preferred_element_type=F32)


def gather_matrix(column):
    places = lax.broadcasted_iota(jnp.int32, (MIRRORS, MASTERS), 1)
    return jnp.where(places == column, 1.0, 0.0).astype(BF16)


def scatter_matrix(line):
    places = lax.broadcasted_iota(jnp.int32, (MASTERS, MIRRORS), 0)
    return jnp.where(places == line, 1.0, 0.0).astype(BF16)


def pull_kernel(column_ref, rows_ref, out_ref):
    picked = dot(gather_matrix(column_ref[...]), rows_ref[...])
    out_ref[...] = picked.reshape(PEERS, 8, F).astype(BF16)


def build_kernel(live_ref, place_ref, lane_ref, rows_ref, a_ref, part_ref, hot3, *tables3):
    hot = hot3.reshape(4 * LANES, LANES)
    tables = [t.reshape(WORDS, LANES) for t in tables3]
    r = lax.broadcasted_iota(jnp.int32, (4 * LANES, LANES), 0)
    c = lax.broadcasted_iota(jnp.int32, (4 * LANES, LANES), 1)
    value = jnp.zeros((4 * LANES, LANES), jnp.int32)
    for q in range(4):
        value = jnp.where(r == c + LANES * q, 1 << (8 * q), value)
    hot[...] = value

    def clear(i, carry):
        for t in tables:
            t[pl.ds(pl.multiple_of(i * 256, 256), 256), :] = jnp.zeros((256, LANES), jnp.int32)
        return carry

    lax.fori_loop(0, WORDS // 256, clear, 0)
    n = live_ref[0]

    def turn(i, carry):
        for g in range(TURN // COPIES):
            at = [pl.ds(g * COPIES + k, EDGES - TURN + 1) for k in range(COPIES)]
            where = [place_ref.at[s][i * TURN] for s in at]
            hots = [hot3[lane_ref.at[s][i * TURN]] for s in at]
            olds = [tables3[k][where[k]] for k in range(COPIES)]
            for k in range(COPIES):
                tables3[k][where[k]] = olds[k] + hots[k]
        return carry

    turns = n // TURN
    lax.fori_loop(0, turns, turn, 0)

    def rest(e, carry):
        tables3[0][place_ref[e]] = tables3[0][place_ref[e]] + hot3[lane_ref[e]]
        return carry

    lax.fori_loop(turns * TURN, n, rest, 0)

    ones = jnp.ones((MASTERS, LANES), BF16)
    wide = jnp.concatenate([rows_ref[...], ones], axis=1)

    def widen(read, carry):
        def block(i, carry):
            d = pl.multiple_of(i * 128, 128)
            for j in range(4):
                for q, counts in enumerate(read(pl.ds(pl.multiple_of(j * SLOTS + d, 128), 128))):
                    left = q * 512 + j * LANES
                    a_ref[pl.ds(d, 128), left : left + LANES] = counts.astype(F32).astype(BF16)
            own = dot(a_ref[pl.ds(d, 128), :MASTERS], wide)
            far = dot(a_ref[pl.ds(d, 128), MASTERS:], ones)
            part_ref[pl.ds(d, 128), :F] = own[:, :F]
            part_ref[pl.ds(d, 128), F:] = own[:, F:] + far
            return carry

        return lax.fori_loop(0, SLOTS // 128, block, carry)

    def read_bytes(at):
        x = tables[0][at, :]
        for t in tables[1:]:
            x = x + t[at, :]
        yield x & 255
        for q in range(1, 4):
            yield lax.shift_right_logical(x, 8 * q) & 255

    widen(read_bytes, 0)

    found = jnp.sum(part_ref[:, F : F + 1])

    @pl.when(found != n.astype(F32))
    def _():
        lax.fori_loop(0, WORDS // 256, clear, 0)

        def edge(e, carry):
            at = place_ref[e]
            lane = lane_ref[e]
            q = lane // LANES
            one = jnp.where(
                lax.broadcasted_iota(jnp.int32, (1, LANES), 1) == lane % LANES,
                jnp.where(q % 2 == 1, 65536, 1),
                0,
            )
            tables3[0][at] = tables3[0][at] + jnp.where(q < 2, one, 0)
            tables3[1][at] = tables3[1][at] + jnp.where(q < 2, 0, one)
            return carry

        lax.fori_loop(0, n, edge, 0)

        def read_halves(at):
            for t in tables[:2]:
                x = t[at, :]
                yield x & 65535
                yield lax.shift_right_logical(x, 16)

        widen(read_halves, 0)


def split(x):
    high = x.astype(BF16).astype(F32)
    return high, (x - high).astype(BF16).astype(F32)


def low_half(shape):
    return lax.broadcasted_iota(jnp.int32, shape, len(shape) - 1) < shape[-1] // 2


def push_kernel(a_ref, part_ref, got_ref, out_ref):
    rows = got_ref[...].reshape(MIRRORS, F)
    sums = part_ref[:, :F] + dot(a_ref[...], rows)
    high, low = split(part_ref[:, F:])
    tally = jnp.where(low_half((MIRRORS, LANES)), high, low)
    both = jnp.concatenate([sums.reshape(PEERS, 8, F), tally.reshape(PEERS, 8, F)], axis=1)
    out_ref[...] = both.astype(BF16)


def local_kernel(a_ref, part_ref, got_ref, rows_ref, w_ref, bias_ref, part_out, pre_out):
    part_out[:, :F] = part_ref[:, :F] + dot(a_ref[...], got_ref[...].reshape(MIRRORS, F))
    part_out[:, F:] = part_ref[:, F:]
    pre_out[...] = dot(rows_ref[...], w_ref[...]) + bias_ref[...]


def dense_kernel(
    got_ref, part_ref, pre_ref, line_ref, column_ref, rows_ref, w_ref, cot_ref,
    act_ref, grad_ref, msg_ref, out_ref, bias_ref,
):
    got = got_ref[...].astype(F32)
    wide = jnp.concatenate(
        [got[:, :8].reshape(MIRRORS, F), got[:, 8:].reshape(MIRRORS, LANES)], axis=1
    ).astype(BF16)
    folded = dot(scatter_matrix(line_ref[...]), wide)
    tally = folded[:, F:]
    degree = part_ref[:, F:] + (tally + pltpu.roll(tally, LANES // 2, 1))
    inverse = 1.0 / jnp.maximum(degree, 1.0)
    aggregate = ((part_ref[:, :F] + folded[:, :F]) * inverse).astype(BF16)
    w = w_ref[...]
    pre = pre_ref[...] + dot(aggregate, w)
    sig = jax.nn.sigmoid(pre)
    act_ref[...] = (pre * sig).astype(BF16)
    grad = (cot_ref[...].astype(F32) * sig * (1.0 + pre * (1.0 - sig))).astype(BF16)
    grad_ref[...] = grad
    msg = (dot_nt(grad, w) * inverse).astype(BF16)
    msg_ref[...] = msg
    picked = dot(gather_matrix(column_ref[...]), msg).reshape(PEERS, 8, F)
    terms = dot_tn(jnp.concatenate([rows_ref[...], aggregate], axis=1), grad)
    flat = jnp.concatenate([terms[:, :F], terms[:, F:]], axis=0).reshape(PEERS // 2, 8, F)
    high, low = split(flat)
    first = lax.broadcasted_iota(jnp.int32, (PEERS // 2, 8, F), 1) < 4
    even = jnp.where(first, high, pltpu.roll(low, 4, 1))
    odd = jnp.where(first, pltpu.roll(high, 4, 1), low)
    mixed = jnp.stack([even, odd], axis=1).reshape(PEERS, 8, F)
    out_ref[...] = jnp.concatenate([picked, mixed], axis=1).astype(BF16)
    total = dot(jnp.ones((8, MASTERS), BF16), grad)
    high, low = split(total)
    sub = lax.broadcasted_iota(jnp.int32, (8, F), 0)
    tile = jnp.where(sub == 4, high[:, :F], 0.0)
    tile = jnp.where(sub == 5, high[:, F:], tile)
    tile = jnp.where(sub == 6, low[:, :F], tile)
    bias_ref[...] = jnp.where(sub == 7, low[:, F:], tile)


def back_local_kernel(a_ref, msg_ref, grad_ref, w_ref, base_ref, mirror_ref):
    spread = dot_tn(msg_ref[...], a_ref[...])
    base_ref[...] = spread[:, :MASTERS].T + dot_nt(grad_ref[...], w_ref[...])
    mirror_ref[...] = spread[:, MASTERS:]


def back_push_kernel(a_ref, mirror_ref, got_ref, bias_ref, out_ref):
    got = got_ref[...].astype(F32)
    rows = got[:, :8].reshape(MIRRORS, F).astype(BF16)
    spread = (mirror_ref[...] + dot_tn(rows, a_ref[...])).T
    total = jnp.sum(got[:, 8:], axis=0)
    total = total + pltpu.roll(total, 4, 0)
    sub = lax.broadcasted_iota(jnp.int32, (8, F), 0)
    tile = jnp.where(sub < 4, total, bias_ref[...])
    tile = jnp.broadcast_to(tile[None], (PEERS, 8, F))
    both = jnp.concatenate([spread.reshape(PEERS, 8, F), tile], axis=1)
    out_ref[...] = both.astype(BF16)


def back_mirror_kernel(a_ref, base_ref, got_ref, out_ref):
    got = got_ref[...].astype(F32)
    rows = got[:, :8].reshape(MIRRORS, F).astype(BF16)
    out_ref[...] = base_ref[...] + dot_tn(rows, a_ref[...]).T


def last_kernel(base_ref, got_ref, line_ref, grad_ref, self_ref, neigh_ref, bias_ref):
    got = got_ref[...].astype(F32)
    rows = got[:, :8].reshape(MIRRORS, F).astype(BF16)
    grad_ref[...] = (base_ref[...] + dot(scatter_matrix(line_ref[...]), rows)).astype(BF16)
    tiles = got[:, 8:]
    pairs = tiles.reshape(PEERS // 2, 2, 8, F)
    first = lax.broadcasted_iota(jnp.int32, (PEERS // 2, 8, F), 1) < 4
    flat = jnp.where(first, pairs[:, 0], pltpu.roll(pairs[:, 1], 4, 1)).reshape(2 * H, F)
    self_ref[:, :F] = flat[:F]
    self_ref[:, F:] = flat[H : H + F]
    neigh_ref[:, :F] = flat[F:H]
    neigh_ref[:, F:] = flat[H + F :]
    total = jnp.sum(tiles, axis=0)
    bias_ref[...] = total + pltpu.roll(total, 6, 0)


def vmem(shape=None, index=None):
    if shape is None:
        return pl.BlockSpec(memory_space=pltpu.VMEM)
    return pl.BlockSpec(shape, lambda i: index, memory_space=pltpu.VMEM, pipeline_mode=pl.Buffered(1))


def call(kernel, ins, outs, specs, name, mib=32, scratch=(), flops=0, moved=0):
    return pl.pallas_call(
        kernel,
        grid=(1,),
        out_shape=[jax.ShapeDtypeStruct(s, t) for s, t in outs],
        in_specs=specs,
        out_specs=[vmem() for _ in outs],
        scratch_shapes=list(scratch),
        compiler_params=pltpu.CompilerParams(vmem_limit_bytes=mib * 1024 * 1024),
        cost_estimate=pl.CostEstimate(flops=flops, bytes_accessed=moved, transcendentals=0),
        name=name,
    )(*ins)


def exchange(x):
    return lax.all_to_all(x, AXES, split_axis=0, concat_axis=0, tiled=True)


def local(features, cotangent, w_self, w_neigh, bias, src_slot, dst_slot, edge_live, mirror_list):
    line = mirror_list.reshape(1, MIRRORS)
    column = mirror_list.reshape(MIRRORS, 1)
    place = ((src_slot >> 7) & 3) * SLOTS + dst_slot
    lane = (src_slot & 127) | ((src_slot >> 9) << 7)
    smem = pl.BlockSpec(memory_space=pltpu.SMEM)
    corner = {
        (i, j): vmem((1024, 1024), (i, j)) for i in range(2) for j in range(2)
    }

    (out1,) = call(
        pull_kernel, (column, features), [((PEERS, 8, F), BF16)], [vmem()] * 2, "pull"
    )
    got1 = exchange(out1)

    a, part = call(
        build_kernel,
        (edge_live, place, lane, features),
        [((SLOTS, SLOTS), BF16), ((SLOTS, 2 * F), F32)],
        [smem, smem, smem, vmem()],
        "build",
        mib=40,
        scratch=[pltpu.VMEM((4 * LANES, 1, LANES), jnp.int32)]
        + [pltpu.VMEM((WORDS, 1, LANES), jnp.int32) for _ in range(COPIES)],
        flops=20_000_000_000,
        moved=20_000_000,
    )
    (out2,) = call(
        push_kernel,
        (a, part, got1),
        [((PEERS, 16, F), BF16)],
        [corner[1, 1], vmem((1024, 2 * F), (1, 0)), vmem()],
        "push",
    )
    got2 = exchange(out2)
    part_m, pre = call(
        local_kernel,
        (a, part, got1, features, w_self, bias.reshape(1, H)),
        [((MASTERS, 2 * F), F32), ((MASTERS, H), F32)],
        [corner[0, 1], vmem((1024, 2 * F), (0, 0)), vmem(), vmem(), vmem(), vmem()],
        "local",
        flops=2_000_000_000,
        moved=6_000_000,
    )
    act, grad, msg, out3, bias_tile = call(
        dense_kernel,
        (got2, part_m, pre, line, column, features, w_neigh, cotangent),
        [
            ((MASTERS, H), BF16),
            ((MASTERS, H), BF16),
            ((MASTERS, F), BF16),
            ((PEERS, 16, F), BF16),
            ((8, F), F32),
        ],
        [vmem()] * 8,
        "dense",
    )
    got3 = exchange(out3)
    base, mirror = call(
        back_local_kernel,
        (a, msg, grad, w_self),
        [((MASTERS, F), F32), ((F, MIRRORS), F32)],
        [vmem((1024, 2048), (0, 0)), vmem(), vmem(), vmem()],
        "back_local",
        flops=2_000_000_000,
        moved=6_000_000,
    )
    (out4,) = call(
        back_push_kernel,
        (a, mirror, got3, bias_tile),
        [((PEERS, 16, F), BF16)],
        [corner[1, 1], vmem(), vmem(), vmem()],
        "back_push",
    )
    got4 = exchange(out4)
    (base2,) = call(
        back_mirror_kernel,
        (a, base, got3),
        [((MASTERS, F), F32)],
        [corner[1, 0], vmem(), vmem()],
        "back_mirror",
        flops=2_000_000_000,
        moved=6_000_000,
    )
    grad_features, grad_self, grad_neigh, bias_out = call(
        last_kernel,
        (base2, got4, line),
        [((MASTERS, F), BF16), ((F, H), F32), ((F, H), F32), ((8, F), F32)],
        [vmem()] * 3,
        "last",
    )
    return act, grad_features, grad_self, grad_neigh, bias_out[4:6].reshape(H)


def solution(mesh):
    placed = (
        P(AXES, None),
        P(AXES, None),
        P(),
        P(),
        P(),
        P(AXES),
        P(AXES),
        P(AXES),
        P(AXES, None, None),
    )
    return jax.shard_map(
        local,
        mesh=mesh,
        in_specs=placed,
        out_specs=(P(AXES, None), P(AXES, None), P(), P(), P()),
        check_vma=False,
    )
```

time: 448 us -> 122 us (0.27)
  matrix products: 113 us -> 0 us
  waiting for transfers between devices: 119 us -> 27.5 us
  blocking collectives: 67.4 us -> 0 us
  local copies, waits for them, and re-layouts: 75.8 us -> 30 us
  Pallas kernels: 0 us -> 29.7 us
  other arithmetic: 24.1 us -> 0.79 us
  between operations: 15.1 us -> 1.46 us
    dot_general x40 -> x0, matrix products: 113 us -> none  [the longest x32 103 us: one_block(): lax.dot_general(hot, piece, (((0,), (0,)), ((), ())), preferred_element_t...]
    psum x1 -> x0, waiting for transfers between devices: 81.3 us -> none  [local(): lax.psum((term_self, term_neigh, term_bias), ('row', 'col'))]
    psum x1 -> x0, blocking collectives: 67.4 us -> none  [local(): lax.psum((term_self, term_neigh, term_bias), ('row', 'col'))]
    gather x4 -> x0, local copies, waits for them, and re-layouts: 55.1 us -> none  [the longest x2 48.1 us: edge_spread(): table[take]]
    pallas_call x0 -> x9, Pallas kernels: none -> 29.7 us  [call(): pl.pallas_call(kernel, grid=(1,), out_shape=[jax.ShapeDtypeStruct(s, t) f...]
    unnamed x41 -> x37, local copies, waits for them, and re-layouts: 2.51 us -> 29.2 us
    reduce_sum x16 -> x0, other arithmetic: 13.7 us -> none  [one_block(): counted = jnp.sum(hot, axis=0, dtype=jnp.float32)]
    dynamic_slice x64 -> x0, local copies, waits for them, and re-layouts: 12.7 us -> none  [edge_spread(): result, _ = lax.scan(one_block, start, (rows, places, flags))]
  transfers between devices with their start and end apart: 6 -> 4, of which waited for: 5 -> 3; matrix products, arithmetic and copies ran while one was open for 2% -> 1% of each run, Pallas kernels for 0% -> 16%
where the time goes in v1:
time: 122 us; the launch traced here: 121 us
  starting transfers between devices  31.6 us (26%)
  local copies, waits for them, and re-layouts  30 us (25%)
  Pallas kernels  29.7 us (24%)
  waiting for transfers between devices  27.5 us (23%)
  between operations  1.46 us (1%)
    all_to_all x4, starting transfers between devices, exchange(): return lax.all_to_all(x, AXES, split_axis=0, concat_axis=0, tiled=True)  31.6 us
    pallas_call x9, Pallas kernels, call(): pl.pallas_call(kernel, grid=(1,), out_shape=[jax.ShapeDtypeStruct(s, t) f...  29.7 us
    unnamed x37, local copies, waits for them, and re-layouts  29.2 us
    all_to_all x4, waiting for transfers between devices, exchange(): return lax.all_to_all(x, AXES, split_axis=0, concat_axis=0, tiled=True)  27.5 us
  transfers between devices with their start and end apart: 4, of which 3 were waited for; matrix products, arithmetic and copies ran while one was open for 1% of the time, Pallas kernels for 16%

profile of v1, /device:TPU:1, one launch (start us, length us, event | category | flops | bytes accessed | tf_op | source)
XLA Modules:
  0.0 121.0 jit_solution(7453984288974046661)
XLA Ops:
  0.6 0.8 copy.16
  1.4 0.2 reshape.26.column_ref
  1.6 0.0 copy-start.6
  1.6 0.9 copy-done.6
  2.6 1.5 %pull.1 = bf16[128,8,128]{2,1,0:T(8,128)(2,1)} custom-call(s32[1024,1]{1,0:T(8,128)S(1)} %reshape.26.column_ref, bf16[1024,128]{1,0:T(8,128)(2,1)S(1)} %copy-done.6), custom_call_target="tpu_custom_call" | custom-call | tf_op jit(solution)/shard_map/pull/pallas_call | solution.py:258
  4.0 11.5 %all-to-all-start = ((bf16[128,8,128]{2,1,0:T(8,128)(2,1)}), bf16[128,8,128]{2,1,0:T(8,128)(2,1)S(1)}, u32[]{:S(2)}, u32[]{:S(2)}) async-start(bf16[128,8,128]{2,1,0:T(8,128)(2,1)} %pull.1), calls=%async_computation | async-start | bytes 524288 | tf_op jit(solution)/shard_map/all_to_all | solution.py:272
  16.2 0.8 shift-left_or_fusion
  17.0 0.0 copy-start.7
  17.0 0.9 copy-done.7
  17.9 17.5 %build.1 = (bf16[2048,2048]{1,0:T(8,128)(2,1)S(1)}, f32[2048,256]{1,0:T(8,128)S(1)}) custom-call(s32[1]{0:T(128)S(6)} %copy.20.live_ref, s32[8192]{0:T(1024)S(1)} %get-tuple-element.36.place_ref, s32[8192]{0:T(1024)S(1)} %get-tuple-element.35.lane_ref, bf16[1024,128]{1,0:T(8,128)(2,1)S(1)} %copy-done.7), custom_call_target="tpu_custom_call" | custom-call | flops 20000000000 | bytes 20000000 | tf_op jit(solution)/shard_map/build/pallas_call | solution.py:258
  35.4 0.0 copy-start
  35.4 3.3 %copy-done = bf16[2048,2048]{1,0:T(8,128)(2,1)} copy-done((bf16[2048,2048]{1,0:T(8,128)(2,1)}, bf16[2048,2048]{1,0:T(8,128)(2,1)S(1)}, u32[]{:S(2)}) %copy-start) | copy-done | bytes 8388632
  38.7 0.0 all-to-all-done.got_ref
  38.7 3.4 %copy-done.1 = bf16[2048,2048]{1,0:T(8,128)(2,1)S(1)} copy-done((bf16[2048,2048]{1,0:T(8,128)(2,1)S(1)}, bf16[2048,2048]{1,0:T(8,128)(2,1)}, u32[]{:S(2)}) %copy-start.1) | copy-done | bytes 8388632
  42.0 0.7 push.1
  42.8 0.0 copy-start.9
  42.8 0.8 copy-done.9
  43.6 12.1 %all-to-all-start.1 = ((bf16[128,16,128]{2,1,0:T(8,128)(2,1)}), bf16[128,16,128]{2,1,0:T(8,128)(2,1)}, u32[]{:S(2)}, u32[]{:S(2)}) async-start(bf16[128,16,128]{2,1,0:T(8,128)(2,1)} %copy-done.9), calls=%async_computation.1 | async-start | bytes 1048576 | tf_op jit(solution)/shard_map/all_to_all | solution.py:272
  55.6 0.1 reshape.24.line_ref
  55.7 0.0 copy-done.8
  55.7 0.0 copy-done.15
  55.8 0.0 copy-done.17
  55.8 0.0 copy-start.2
  55.8 3.4 %copy-done.2 = bf16[2048,2048]{1,0:T(8,128)(2,1)S(1)} copy-done((bf16[2048,2048]{1,0:T(8,128)(2,1)S(1)}, bf16[2048,2048]{1,0:T(8,128)(2,1)}, u32[]{:S(2)}) %copy-start.2) | copy-done | bytes 8388632
  59.1 0.9 local.1
  60.0 0.0 copy-start.10
  60.0 1.0 copy-done.10
  61.0 1.0 copy-done.12
  62.0 7.3 %all-to-all-done.1.got_ref = bf16[128,16,128]{2,1,0:T(8,128)(2,1)} async-done(((bf16[128,16,128]{2,1,0:T(8,128)(2,1)}), bf16[128,16,128]{2,1,0:T(8,128)(2,1)}, u32[]{:S(2)}, u32[]{:S(2)}) %all-to-all-start.1) | async-done | bytes 524320 | tf_op jit(solution)/shard_map/all_to_all | solution.py:272
  69.4 0.0 copy-done.16
  69.4 1.2 %copy-done.11 = f32[1024,256]{1,0:T(8,128)S(1)} copy-done((f32[1024,256]{1,0:T(8,128)S(1)}, f32[1024,256]{1,0:T(8,128)}, u32[]{:S(2)}) %copy-start.11) | copy-done | bytes 1048600
  70.6 1.2 %copy-done.13 = f32[1024,256]{1,0:T(8,128)S(1)} copy-done((f32[1024,256]{1,0:T(8,128)S(1)}, f32[1024,256]{1,0:T(8,128)}, u32[]{:S(2)}) %copy-start.13) | copy-done | bytes 1048600
  71.8 1.0 copy-done.14
  72.9 4.9 %dense.1 = (bf16[1024,256]{1,0:T(8,128)(2,1)}, bf16[1024,256]{1,0:T(8,128)(2,1)S(1)}, bf16[1024,128]{1,0:T(8,128)(2,1)S(1)}, bf16[128,16,128]{2,1,0:T(8,128)(2,1)}, f32[8,128]{1,0:T(8,128)S(1)}) custom-call(bf16[128,16,128]{2,1,0:T(8,128)(2,1)} %all-to-all-done.1.got_ref, f32[1024,256]{1,0:T(8,128)S(1)} %copy-done.11, f32[1024,256]{1,0:T(8,128)S(1)} %copy-done.13, ...), custom_call_target="tpu_custom_call" | custom-call | tf_op jit(solution)/shard_map/dense/pallas_call | solution.py:258
  77.8 4.0 %all-to-all-start.2 = ((bf16[128,16,128]{2,1,0:T(8,128)(2,1)}), bf16[128,16,128]{2,1,0:T(8,128)(2,1)S(1)}, u32[]{:S(2)}, u32[]{:S(2)}) async-start(bf16[128,16,128]{2,1,0:T(8,128)(2,1)} %get-tuple-element.28), calls=%async_computation.2 | async-start | bytes 1048576 | tf_op jit(solution)/shard_map/all_to_all | solution.py:272
  81.8 0.0 copy-start.3
  81.8 3.4 %copy-done.3 = bf16[2048,2048]{1,0:T(8,128)(2,1)S(1)} copy-done((bf16[2048,2048]{1,0:T(8,128)(2,1)S(1)}, bf16[2048,2048]{1,0:T(8,128)(2,1)}, u32[]{:S(2)}) %copy-start.3) | copy-done | bytes 8388632
  85.2 0.9 back_local.1
  86.0 10.0 %all-to-all-done.2.got_ref = bf16[128,16,128]{2,1,0:T(8,128)(2,1)S(1)} async-done(((bf16[128,16,128]{2,1,0:T(8,128)(2,1)}), bf16[128,16,128]{2,1,0:T(8,128)(2,1)S(1)}, u32[]{:S(2)}, u32[]{:S(2)}) %all-to-all-start.2) | async-done | bytes 524320 | tf_op jit(solution)/shard_map/all_to_all | solution.py:272
  96.0 3.4 %copy-done.4 = bf16[2048,2048]{1,0:T(8,128)(2,1)S(1)} copy-done((bf16[2048,2048]{1,0:T(8,128)(2,1)S(1)}, bf16[2048,2048]{1,0:T(8,128)(2,1)}, u32[]{:S(2)}) %copy-start.4) | copy-done | bytes 8388632
  99.4 1.4 %back_push.1 = bf16[128,16,128]{2,1,0:T(8,128)(2,1)} custom-call(bf16[2048,2048]{1,0:T(8,128)(2,1)S(1)} %copy-done.4, f32[128,1024]{1,0:T(8,128)S(1)} %get-tuple-element.29.mirror_ref, bf16[128,16,128]{2,1,0:T(8,128)(2,1)S(1)} %all-to-all-done.2.got_ref, f32[8,128]{1,0:T(8,128)S(1)} %get-tuple-element.30.bias_ref), custom_call_target="tpu_custom_call" | custom-call | tf_op jit(solution)/shard_map/back_push/pallas_call | solution.py:258
  100.8 4.0 %all-to-all-start.3 = ((bf16[128,16,128]{2,1,0:T(8,128)(2,1)}), bf16[128,16,128]{2,1,0:T(8,128)(2,1)S(1)}, u32[]{:S(2)}, u32[]{:S(2)}) async-start(bf16[128,16,128]{2,1,0:T(8,128)(2,1)} %back_push.1), calls=%async_computation.3 | async-start | bytes 1048576 | tf_op jit(solution)/shard_map/all_to_all | solution.py:272
  104.8 0.0 copy-start.5
  104.8 3.4 %copy-done.5 = bf16[2048,2048]{1,0:T(8,128)(2,1)S(1)} copy-done((bf16[2048,2048]{1,0:T(8,128)(2,1)S(1)}, bf16[2048,2048]{1,0:T(8,128)(2,1)}, u32[]{:S(2)}) %copy-start.5) | copy-done | bytes 8388632
  108.2 0.6 back_mirror.1.base_ref
  108.8 10.3 %all-to-all-done.3.got_ref = bf16[128,16,128]{2,1,0:T(8,128)(2,1)S(1)} async-done(((bf16[128,16,128]{2,1,0:T(8,128)(2,1)}), bf16[128,16,128]{2,1,0:T(8,128)(2,1)S(1)}, u32[]{:S(2)}, u32[]{:S(2)}) %all-to-all-start.3) | async-done | bytes 524320 | tf_op jit(solution)/shard_map/all_to_all | solution.py:272
  119.0 1.5 %last.1 = (bf16[1024,128]{1,0:T(8,128)(2,1)}, f32[128,256]{1,0:T(8,128)}, f32[128,256]{1,0:T(8,128)}, f32[8,128]{1,0:T(8,128)S(1)}) custom-call(f32[1024,128]{1,0:T(8,128)S(1)} %back_mirror.1.base_ref, bf16[128,16,128]{2,1,0:T(8,128)(2,1)S(1)} %all-to-all-done.3.got_ref, s32[1,1024]{1,0:T(1,128)S(1)} %reshape.24.line_ref), custom_call_target="tpu_custom_call" | custom-call | tf_op jit(solution)/shard_map/last/pallas_call | solution.py:258
  120.5 0.6 slice_bitcast_fusion
  (10 shorter events, 0.0 us)
Async XLA Ops:
  1.6 1.0 copy-start.6
  4.0 34.6 %all-to-all-start = ((bf16[128,8,128]{2,1,0:T(8,128)(2,1)}), bf16[128,8,128]{2,1,0:T(8,128)(2,1)S(1)}, u32[]{:S(2)}, u32[]{:S(2)}) async-start(bf16[128,8,128]{2,1,0:T(8,128)(2,1)} %pull.1), calls=%async_computation | async-start | bytes 524288 | tf_op jit(solution)/shard_map/all_to_all | solution.py:272
  17.0 1.0 copy-start.7
  17.9 37.8 %copy-start.8 = (bf16[1024,128]{1,0:T(8,128)(2,1)S(1)}, bf16[1024,128]{1,0:T(8,128)(2,1)}, u32[]{:S(2)}) copy-start(bf16[1024,128]{1,0:T(8,128)(2,1)} %rows_ref.7) | copy-start | bytes 786436
  17.9 37.8 %copy-start.15 = (bf16[128,256]{1,0:T(8,128)(2,1)S(1)}, bf16[128,256]{1,0:T(8,128)(2,1)}, u32[]{:S(2)}) copy-start(bf16[128,256]{1,0:T(8,128)(2,1)} %w_ref.5) | copy-start | bytes 196612
  35.4 3.3 %copy-start = (bf16[2048,2048]{1,0:T(8,128)(2,1)}, bf16[2048,2048]{1,0:T(8,128)(2,1)S(1)}, u32[]{:S(2)}) copy-start(bf16[2048,2048]{1,0:T(8,128)(2,1)S(1)} %get-tuple-element.20.a_ref) | copy-start | bytes 25165828
  38.7 17.1 %copy-start.17 = (f32[256]{0:T(256)S(1)}, f32[256]{0:T(256)}, u32[]{:S(2)}) copy-start(f32[256]{0:T(256)} %param.13) | copy-start | bytes 3076
  38.7 3.4 %copy-start.1 = (bf16[2048,2048]{1,0:T(8,128)(2,1)S(1)}, bf16[2048,2048]{1,0:T(8,128)(2,1)}, u32[]{:S(2)}) copy-start(bf16[2048,2048]{1,0:T(8,128)(2,1)} %copy-done) | copy-start | bytes 25165828
  42.8 0.8 copy-start.9
  43.6 25.8 %copy-start.16 = (bf16[128,256]{1,0:T(8,128)(2,1)S(1)}, bf16[128,256]{1,0:T(8,128)(2,1)}, u32[]{:S(2)}) copy-start(bf16[128,256]{1,0:T(8,128)(2,1)} %w_ref.4) | copy-start | bytes 196612
  43.6 25.8 %all-to-all-start.1 = ((bf16[128,16,128]{2,1,0:T(8,128)(2,1)}), bf16[128,16,128]{2,1,0:T(8,128)(2,1)}, u32[]{:S(2)}, u32[]{:S(2)}) async-start(bf16[128,16,128]{2,1,0:T(8,128)(2,1)} %copy-done.9), calls=%async_computation.1 | async-start | bytes 1048576 | tf_op jit(solution)/shard_map/all_to_all | solution.py:272
  55.8 3.4 %copy-start.2 = (bf16[2048,2048]{1,0:T(8,128)(2,1)S(1)}, bf16[2048,2048]{1,0:T(8,128)(2,1)}, u32[]{:S(2)}) copy-start(bf16[2048,2048]{1,0:T(8,128)(2,1)} %copy-done) | copy-start | bytes 25165828
  60.0 1.0 copy-start.10
  61.0 1.0 copy-start.12
  69.4 1.2 %copy-start.11 = (f32[1024,256]{1,0:T(8,128)S(1)}, f32[1024,256]{1,0:T(8,128)}, u32[]{:S(2)}) copy-start(f32[1024,256]{1,0:T(8,128)} %copy-done.10) | copy-start | bytes 3145732
  70.6 1.2 %copy-start.13 = (f32[1024,256]{1,0:T(8,128)S(1)}, f32[1024,256]{1,0:T(8,128)}, u32[]{:S(2)}) copy-start(f32[1024,256]{1,0:T(8,128)} %copy-done.12) | copy-start | bytes 3145732
  71.8 1.0 copy-start.14
  77.8 18.2 %all-to-all-start.2 = ((bf16[128,16,128]{2,1,0:T(8,128)(2,1)}), bf16[128,16,128]{2,1,0:T(8,128)(2,1)S(1)}, u32[]{:S(2)}, u32[]{:S(2)}) async-start(bf16[128,16,128]{2,1,0:T(8,128)(2,1)} %get-tuple-element.28), calls=%async_computation.2 | async-start | bytes 1048576 | tf_op jit(solution)/shard_map/all_to_all | solution.py:272
  81.8 3.4 %copy-start.3 = (bf16[2048,2048]{1,0:T(8,128)(2,1)S(1)}, bf16[2048,2048]{1,0:T(8,128)(2,1)}, u32[]{:S(2)}) copy-start(bf16[2048,2048]{1,0:T(8,128)(2,1)} %copy-done) | copy-start | bytes 25165828
  96.0 3.4 %copy-start.4 = (bf16[2048,2048]{1,0:T(8,128)(2,1)S(1)}, bf16[2048,2048]{1,0:T(8,128)(2,1)}, u32[]{:S(2)}) copy-start(bf16[2048,2048]{1,0:T(8,128)(2,1)} %copy-done) | copy-start | bytes 25165828
  100.8 18.2 %all-to-all-start.3 = ((bf16[128,16,128]{2,1,0:T(8,128)(2,1)}), bf16[128,16,128]{2,1,0:T(8,128)(2,1)S(1)}, u32[]{:S(2)}, u32[]{:S(2)}) async-start(bf16[128,16,128]{2,1,0:T(8,128)(2,1)} %back_push.1), calls=%async_computation.3 | async-start | bytes 1048576 | tf_op jit(solution)/shard_map/all_to_all | solution.py:272
  104.8 3.4 %copy-start.5 = (bf16[2048,2048]{1,0:T(8,128)(2,1)S(1)}, bf16[2048,2048]{1,0:T(8,128)(2,1)}, u32[]{:S(2)}) copy-start(bf16[2048,2048]{1,0:T(8,128)(2,1)} %copy-done) | copy-start | bytes 25165828

commit v2 on v1

v2 whole, which is shorter than its diff:
```python
import jax
import jax.numpy as jnp
from jax import lax
from jax.experimental import pallas as pl
from jax.experimental.pallas import tpu as pltpu
from jax.sharding import PartitionSpec as P

F32 = jnp.float32
BF16 = jnp.bfloat16
AXES = ("row", "col")

MASTERS = 1024
MIRRORS = 1024
SLOTS = MASTERS + MIRRORS
EDGES = 8192
PEERS = 128
F = 128
H = 256
LANES = 128
COPIES = 6
TURN = 128
PARTS = 4
WORDS = SLOTS * (SLOTS // 512)


def part_of(size, k):
    return pl.ds(k * (size // PARTS), size // PARTS)


def dot(a, b):
    return jnp.dot(a, b, preferred_element_type=F32)


def dot_nt(a, b):
    return lax.dot_general(a, b, (((1,), (1,)), ((), ())), preferred_element_type=F32)


def gather_matrix(column):
    places = lax.broadcasted_iota(jnp.int32, (MIRRORS, MASTERS), 1)
    return jnp.where(places == column, 1.0, 0.0).astype(BF16)


def scatter_matrix(line):
    places = lax.broadcasted_iota(jnp.int32, (MASTERS, MIRRORS), 0)
    return jnp.where(places == line, 1.0, 0.0).astype(BF16)


def as_column(lists):
    turned = jnp.transpose(lists.astype(F32))
    shape = (PEERS, 8, 8)
    spread = jnp.broadcast_to(turned[:, None, :], shape)
    here = lax.broadcasted_iota(jnp.int32, shape, 1) == lax.broadcasted_iota(jnp.int32, shape, 2)
    column = jnp.sum(jnp.where(here, spread, 0.0), axis=2, keepdims=True)
    return column.reshape(MIRRORS, 1).astype(jnp.int32)


def pull_kernel(lists_ref, rows_ref, out_ref):
    matrix = gather_matrix(as_column(lists_ref[...]))
    rows = rows_ref[...]
    for c in range(2):
        picked = dot(matrix[c * 512 : (c + 1) * 512], rows).reshape(PEERS // 2, 8, F)
        half = pl.ds(c * (PEERS // 2), PEERS // 2)
        out_ref[half] = picked.astype(BF16)
        out_ref.send(half)


def build_kernel(
    live_ref, src_ref, dst_ref, rows_ref, mm_ref, mg_ref, gm_ref, gg_ref, sums_ref, tally_ref,
    code_ref, codes, sem, *tables3
):
    tables = [t.reshape(WORDS, LANES) for t in tables3]
    n = live_ref[0]

    def clear(i, carry):
        for t in tables:
            t[pl.ds(pl.multiple_of(i * 256, 256), 256), :] = jnp.zeros((256, LANES), jnp.int32)
        return carry

    lax.fori_loop(0, WORDS // 512, clear, 0)
    src, dst = src_ref[...], dst_ref[...]
    shape = (EDGES // LANES, LANES)
    number = lax.broadcasted_iota(jnp.int32, shape, 0) * LANES
    number = number + lax.broadcasted_iota(jnp.int32, shape, 1)
    place = ((src >> 7) & 3) * SLOTS + dst
    code = place | ((src & 127) << 13) | ((src >> 9) << 24)
    code_ref[...] = jnp.where(number < n, code, 128 << 13)
    move = pltpu.make_async_copy(code_ref, codes, sem)
    move.start()
    lax.fori_loop(WORDS // 512, WORDS // 256, clear, 0)
    move.wait()

    lanes = lax.broadcasted_iota(jnp.int32, (1, LANES), 1) << 13
    one = jnp.ones((1, LANES), jnp.int32)

    def turn(i, carry):
        for start in range(0, TURN, COPIES):
            count = min(COPIES, TURN - start)
            words = [codes[i, start + k] for k in range(count)]
            where = [w & (WORDS - 1) for w in words]
            adds = []
            for w in words:
                w = jnp.full((1, LANES), w, jnp.int32)
                bit = lax.shift_left(one, lax.shift_right_logical(w, 21))
                adds.append(jnp.where(lanes == (w & (255 << 13)), bit, 0))
            olds = [tables3[k][where[k]] for k in range(count)]
            for k in range(count):
                tables3[k][where[k]] = olds[k] + adds[k]
        return carry

    turns = (n + TURN - 1) // TURN
    lax.fori_loop(0, turns, turn, 0)

    def put(near_ref, far_ref, to, at, read, seen):
        for j in range(4):
            words = read(pl.ds(pl.multiple_of(j * SLOTS + at, 128), 128))
            for q, counts in enumerate(words):
                half = near_ref if q < 2 else far_ref
                left = (q % 2) * 512 + j * LANES
                half[pl.ds(to, 128), pl.ds(left, LANES)] = counts.astype(F32).astype(BF16)
                seen = seen + jnp.sum(counts.reshape(16, 8, LANES), axis=0)
        return seen

    ones = jnp.ones((MASTERS, LANES), BF16)
    wide = jnp.concatenate([rows_ref[...], ones], axis=1)

    def widen(read):
        def mirrors(i, seen):
            d = pl.multiple_of(i * 128, 128)
            return put(gm_ref, gg_ref, d, MASTERS + d, read, seen)

        def masters(i, seen):
            e = pl.multiple_of(i * 256, 256)
            own = dot(gm_ref[pl.ds(e, 256), :], wide)
            far = dot(gg_ref[pl.ds(e, 256), :], ones)
            sums_ref[pl.ds(e, 256), :] = own[:, :F]
            tally_ref[pl.ds(e, 256), :] = two_parts(own[:, F:] + far)
            for h in range(2):
                d = pl.multiple_of(i * 256 + h * 128, 128)
                seen = put(mm_ref, mg_ref, d, d, read, seen)
            mm_ref.send(pl.ds(e, 256))
            mg_ref.send(pl.ds(e, 256))
            return seen

        seen = lax.fori_loop(0, MIRRORS // 128, mirrors, jnp.zeros((8, LANES), jnp.int32))
        gg_ref.send()
        gm_ref.send()
        seen = lax.fori_loop(0, MASTERS // 256, masters, seen)
        sums_ref.send()
        tally_ref.send()
        return seen

    def finish():
        for ref in (mm_ref, mg_ref, gm_ref, gg_ref, sums_ref, tally_ref):
            ref.wait()

    def read_bytes(at):
        x = tables[0][at, :]
        for t in tables[1:]:
            x = x + t[at, :]
        yield x & 255
        yield lax.shift_right_logical(x, 8) & 255
        yield lax.shift_right_logical(x, 16) & 255
        yield lax.shift_right_logical(x, 24)

    found = jnp.sum(widen(read_bytes).astype(F32))
    finish()

    @pl.when(found != n.astype(F32))
    def _():
        lax.fori_loop(0, WORDS // 256, clear, 0)

        def edge(e, carry):
            word = codes[e // LANES, e % LANES]
            at = word & (WORDS - 1)
            q = word >> 24
            one = jnp.where(
                lanes == (word & (127 << 13)), jnp.where(q % 2 == 1, 65536, 1), 0
            )
            tables3[0][at] = tables3[0][at] + jnp.where(q < 2, one, 0)
            tables3[1][at] = tables3[1][at] + jnp.where(q < 2, 0, one)
            return carry

        lax.fori_loop(0, n, edge, 0)

        def read_halves(at):
            for t in tables[:2]:
                x = t[at, :]
                yield x & 65535
                yield lax.shift_right_logical(x, 16)

        widen(read_halves)
        finish()


def split(x):
    high = x.astype(BF16).astype(F32)
    return high, (x - high).astype(BF16).astype(F32)


def two_parts(x):
    high, low = split(x)
    left = lax.broadcasted_iota(jnp.int32, x.shape, 1) < LANES // 2
    return jnp.where(left, high, low).astype(BF16)


def push_kernel(got_ref, sums_ref, gg_ref, tally_ref, out_ref):
    got = got_ref[...].reshape(MIRRORS, F)
    for c in range(PARTS):
        rows, peers = part_of(MIRRORS, c), part_of(PEERS, c)
        sums = dot(gg_ref.part(c), got) + sums_ref[rows]
        tally = tally_ref[rows].astype(F32)
        shape = (PEERS // PARTS, 8, F)
        both = jnp.concatenate([sums.reshape(shape), tally.reshape(shape)], axis=1)
        out_ref[peers] = both.astype(BF16)
        out_ref.send(peers)


def local_kernel(
    rows_ref, lists_ref, mm_ref, got_ref, mg_ref, gather_ref, turned_ref, sums_ref, tally_ref
):
    gather_ref[...] = gather_matrix(as_column(lists_ref[...]))
    gather_ref.send()
    rows = rows_ref[...]
    turned_ref[...] = rows.astype(F32).T.astype(BF16)
    turned_ref.send()
    ones = jnp.ones((MASTERS, LANES), BF16)
    got = got_ref[...].reshape(MIRRORS, F)
    both = dot(mm_ref[...], jnp.concatenate([rows, ones], axis=1)) + dot(
        mg_ref[...], jnp.concatenate([got, ones], axis=1)
    )
    sums_ref[...] = both[:, :F]
    sums_ref.send()
    tally_ref[...] = two_parts(both[:, F:])
    tally_ref.send()


def dense_kernel(
    line_ref, got_ref, tally_ref, sums_ref, self_ref, bias_ref, rows_ref, neigh_ref, cot_ref,
    gather_ref, turned_ref,
    act_ref, grad_ref, msg_ref, out_ref, total_ref,
):
    scatter = scatter_matrix(line_ref[...])
    got = got_ref[...].astype(F32)
    wide = jnp.concatenate(
        [got[:, :8].reshape(MIRRORS, F), got[:, 8:].reshape(MIRRORS, LANES)], axis=1
    ).astype(BF16)
    folded = dot(scatter, wide)
    tally = folded[:, F:] + tally_ref[...].astype(F32)
    degree = tally + pltpu.roll(tally, LANES // 2, 1)
    inverse = 1.0 / jnp.maximum(degree, 1.0)
    mean = (sums_ref[...] + folded[:, :F]) * inverse
    w = neigh_ref[...]
    pre = dot(rows_ref[...], self_ref[...]) + dot(mean.astype(BF16), w) + bias_ref[...]
    sig = jax.nn.sigmoid(pre)
    act_ref[...] = (pre * sig).astype(BF16)
    act_ref.send()
    grad = (cot_ref[...].astype(F32) * sig * (1.0 + pre * (1.0 - sig))).astype(BF16)
    grad_ref[...] = grad
    grad_ref.send()
    msg = (dot_nt(grad, w) * inverse).astype(BF16)
    msg_ref[...] = msg
    msg_ref.send()
    picked = dot(gather_ref[...], msg).reshape(PEERS, 8, F)
    turned = jnp.concatenate([turned_ref[...], mean.T.astype(BF16)], axis=0)
    terms = dot(turned, grad)
    flat = jnp.concatenate([terms[:, :F], terms[:, F:]], axis=0).reshape(PEERS // 2, 8, F)
    high, low = split(flat)
    first = lax.broadcasted_iota(jnp.int32, (PEERS // 2, 8, F), 1) < 4
    even = jnp.where(first, high, pltpu.roll(low, 4, 1))
    odd = jnp.where(first, pltpu.roll(high, 4, 1), low)
    mixed = jnp.stack([even, odd], axis=1).reshape(PEERS, 8, F)
    out_ref[...] = jnp.concatenate([picked, mixed], axis=1).astype(BF16)
    out_ref.send()
    total = dot(jnp.ones((8, MASTERS), BF16), grad)
    high, low = split(total)
    sub = lax.broadcasted_iota(jnp.int32, (8, F), 0)
    tile = jnp.where(sub == 4, high[:, :F], 0.0)
    tile = jnp.where(sub == 5, high[:, F:], tile)
    tile = jnp.where(sub == 6, low[:, :F], tile)
    total_ref[...] = jnp.where(sub == 7, low[:, F:], tile)
    total_ref.send()


def back_local_kernel(
    gg_ref, msg_ref, mg_ref, mm_ref, grad_ref, w_ref, _, turned_ref, mirror_ref, base_ref
):
    turned_ref[...] = gg_ref[...].T
    turned_ref.send()
    msg = msg_ref[...].astype(F32).T.astype(BF16)
    mirror_ref[...] = dot(msg, mg_ref[...]).T
    mirror_ref.send()
    base_ref[...] = dot(msg, mm_ref[...]).T + dot_nt(grad_ref[...], w_ref[...])
    base_ref.send()


def back_push_kernel(got_ref, mirror_ref, total_ref, turned_ref, out_ref):
    got = got_ref[...].astype(F32)
    rows = got[:, :8].reshape(MIRRORS, F).astype(BF16)
    total = jnp.sum(got[:, 8:], axis=0)
    total = total + pltpu.roll(total, 4, 0)
    sub = lax.broadcasted_iota(jnp.int32, (8, F), 0)
    tile = jnp.where(sub < 4, total, total_ref[...])
    shape = (PEERS // PARTS, 8, F)
    tiles = jnp.broadcast_to(tile[None], shape)
    for c in range(PARTS):
        peers = part_of(PEERS, c)
        spread = dot(turned_ref.part(c), rows) + mirror_ref[part_of(MIRRORS, c)]
        out_ref[peers] = jnp.concatenate([spread.reshape(shape), tiles], axis=1).astype(BF16)
        out_ref.send(peers)


def back_mirror_kernel(got_ref, gm_ref, base_ref, out_ref):
    turned = got_ref[...].astype(F32)[:, :8].reshape(MIRRORS, F).T.astype(BF16)
    out_ref[...] = dot(turned, gm_ref[...]).T + base_ref[...]
    out_ref.send()


def last_kernel(line_ref, got_ref, base_ref, grad_ref, self_ref, neigh_ref, bias_ref):
    got = got_ref[...].astype(F32)
    rows = got[:, :8].reshape(MIRRORS, F).astype(BF16)
    grad_ref[...] = (dot(scatter_matrix(line_ref[...]), rows) + base_ref[...]).astype(BF16)
    grad_ref.send()
    tiles = got[:, 8:]
    pairs = tiles.reshape(PEERS // 2, 2, 8, F)
    first = lax.broadcasted_iota(jnp.int32, (PEERS // 2, 8, F), 1) < 4
    flat = jnp.where(first, pairs[:, 0], pltpu.roll(pairs[:, 1], 4, 1)).reshape(2 * H, F)
    self_ref[:, :F] = flat[:F]
    self_ref[:, F:] = flat[H : H + F]
    neigh_ref[:, :F] = flat[F:H]
    neigh_ref[:, F:] = flat[H + F :]
    total = jnp.sum(tiles, axis=0)
    bias_ref[...] = total[4:6] + total[6:8]
    for ref in (self_ref, neigh_ref, bias_ref):
        ref.send()


VMEM = pl.BlockSpec(memory_space=pltpu.VMEM)
SMEM = pl.BlockSpec(memory_space=pltpu.SMEM)
HBM = pl.BlockSpec(memory_space=pltpu.HBM)
ALL = 60 * 1024 * 1024
NEAR = 55_800_000


class Loaded:
    def __init__(self, source, held, sems, first, parts):
        size = held.shape[0] // parts
        self.held, self.size = held, size
        self.copies = []
        for k in range(parts):
            rows = pl.ds(k * size, size)
            copy = pltpu.make_async_copy(source.at[rows], held.at[rows], sems.at[first + k])
            copy.start()
            self.copies.append(copy)

    def part(self, k):
        if self.copies[k] is not None:
            self.copies[k].wait()
            self.copies[k] = None
        return self.held[pl.ds(k * self.size, self.size)]

    def wait(self):
        for k, copy in enumerate(self.copies):
            if copy is not None:
                copy.wait()
                self.copies[k] = None

    def __getitem__(self, at):
        self.wait()
        return self.held[at]


class Stored:
    def __init__(self, held, target, sem):
        self.held, self.target, self.sem = held, target, sem
        self.copy = pltpu.make_async_copy(held, target, sem)
        self.waited = False

    def __setitem__(self, at, value):
        self.held[at] = value

    def __getitem__(self, at):
        return self.held[at]

    def wait(self):
        self.copy.wait()
        self.waited = True

    def send(self, rows=None):
        if rows is None:
            self.copy.start()
        else:
            pltpu.make_async_copy(self.held.at[rows], self.target.at[rows], self.sem).start()


def call(kernel, ins, outs, name, near=(), scalars=(), scratch=(), parts=None, idle=(), flops=0, moved=0):
    parts = parts or {}
    far = [k for k in range(len(ins)) if k not in (*near, *scalars, *idle)]
    specs = [VMEM if k in near else SMEM if k in scalars else HBM for k in range(len(ins))]
    held = [pltpu.VMEM(ins[k].shape, ins[k].dtype) for k in far]
    held += [pltpu.VMEM(s, t) for s, t in outs]
    counts = [parts.get(k, 1) for k in far]
    dma = pltpu.SemaphoreType.DMA

    def body(*refs):
        operands, refs = list(refs[: len(ins)]), refs[len(ins) :]
        targets, refs = refs[: len(outs)], refs[len(outs) :]
        copies, refs = refs[: len(far)], refs[len(far) :]
        results, refs = refs[: len(outs)], refs[len(outs) :]
        load_sems, store_sems = refs[0], refs[1]
        first = 0
        for k, copy, count in zip(far, copies, counts, strict=True):
            operands[k] = Loaded(operands[k], copy, load_sems, first, count)
            first += count
        stores = [
            Stored(results[k], targets[k], store_sems.at[k]) for k in range(len(outs))
        ]
        kernel(*operands, *stores, *refs[2:])
        for k in far:
            operands[k].wait()
        for store in stores:
            if not store.waited:
                store.wait()

    return pl.pallas_call(
        body,
        out_shape=[jax.ShapeDtypeStruct(s, t) for s, t in outs],
        in_specs=specs,
        out_specs=[HBM] * len(outs),
        scratch_shapes=held + [dma((max(sum(counts), 1),)), dma((len(outs),))] + list(scratch),
        compiler_params=pltpu.CompilerParams(vmem_limit_bytes=NEAR if near else ALL),
        cost_estimate=pl.CostEstimate(flops=flops, bytes_accessed=moved, transcendentals=0),
        name=name,
    )(*ins)


def exchange(x):
    return lax.all_to_all(x, AXES, split_axis=0, concat_axis=0, tiled=True)


def local(features, cotangent, w_self, w_neigh, bias, src_slot, dst_slot, edge_live, mirror_list):
    line = mirror_list.reshape(1, MIRRORS)
    lists = mirror_list[0].T
    square = ((1024, 1024), BF16)
    payload = ((PEERS, 16, F), BF16)

    (out1,) = call(pull_kernel, (lists, features), [((PEERS, 8, F), BF16)], "pull")
    got1 = exchange(out1)

    edges = (EDGES // LANES, LANES)
    rows_f32, rows_bf16 = ((1024, F), F32), ((1024, F), BF16)
    mm, mg, gm, gg, sums, tally = call(
        build_kernel,
        (edge_live, src_slot.reshape(edges), dst_slot.reshape(edges), features),
        [square] * 4 + [rows_f32, rows_bf16],
        "build",
        scalars=(0,),
        scratch=[
            pltpu.VMEM(edges, jnp.int32),
            pltpu.SMEM(edges, jnp.int32),
            pltpu.SemaphoreType.DMA,
        ]
        + [pltpu.VMEM((WORDS, 1, LANES), jnp.int32) for _ in range(COPIES)],
        flops=20_000_000_000,
        moved=20_000_000,
    )
    (out2,) = call(push_kernel, (got1, sums, gg, tally), [payload], "push", parts={2: PARTS})
    got2 = exchange(out2)
    gather, turned, sums_m, tally_m = call(
        local_kernel,
        (features, lists, mm, got1, mg),
        [square, ((F, MASTERS), BF16), rows_f32, rows_bf16],
        "local",
        flops=2_000_000_000,
        moved=6_000_000,
    )
    act, grad, msg, out3, total = call(
        dense_kernel,
        (
            line, got2, tally_m, sums_m, w_self, bias.reshape(1, H), features, w_neigh,
            cotangent, gather, turned,
        ),
        [((MASTERS, H), BF16), ((MASTERS, H), BF16), rows_bf16, payload, ((8, F), F32)],
        "dense",
    )
    got3 = exchange(out3)
    turned_gg, mirror, base = call(
        back_local_kernel,
        (gg, msg, mg, mm, grad, w_self, got2),
        [square, rows_f32, rows_f32],
        "back_local",
        idle=(6,),
        flops=2_000_000_000,
        moved=6_000_000,
    )
    (out4,) = call(
        back_push_kernel,
        (got3, mirror, total, turned_gg),
        [payload],
        "back_push",
        parts={3: PARTS},
    )
    got4 = exchange(out4)
    (base2,) = call(
        back_mirror_kernel,
        (got3, gm, base),
        [rows_f32],
        "back_mirror",
        flops=2_000_000_000,
        moved=6_000_000,
    )
    grad_features, grad_self, grad_neigh, bias_out = call(
        last_kernel,
        (line, got4, base2),
        [rows_bf16, ((F, H), F32), ((F, H), F32), ((2, F), F32)],
        "last",
        near=(1,),
    )
    return act, grad_features, grad_self, grad_neigh, bias_out.reshape(H)


def solution(mesh):
    placed = (
        P(AXES, None),
        P(AXES, None),
        P(),
        P(),
        P(),
        P(AXES),
        P(AXES),
        P(AXES),
        P(AXES, None, None),
    )
    return jax.shard_map(
        local,
        mesh=mesh,
        in_specs=placed,
        out_specs=(P(AXES, None), P(AXES, None), P(), P(), P()),
        check_vma=False,
    )
```

time: 122 us -> 112 us (0.918)
  local copies, waits for them, and re-layouts: 30 us -> 3.1 us
  Pallas kernels: 29.7 us -> 47.5 us
  waiting for transfers between devices: 27.5 us -> 29 us
    unnamed x37 -> x11, local copies, waits for them, and re-layouts: 29.2 us -> 2.41 us
    pallas_call x9, Pallas kernels: 29.7 us -> 47.5 us  [call(): pl.pallas_call(body, out_shape=[jax.ShapeDtypeStruct(s, t) for s, t in ou...]
    all_to_all x4, waiting for transfers between devices: 27.5 us -> 29 us  [exchange(): return lax.all_to_all(x, AXES, split_axis=0, concat_axis=0, tiled=True)]
  transfers between devices with their start and end apart: 4 -> 4, of which waited for: 3 -> 3; matrix products, arithmetic and copies ran while one was open for 1% -> 1% of each run, Pallas kernels for 16% -> 26%
where the time goes in v2:
time: 112 us
  Pallas kernels  47.5 us (42%)
  starting transfers between devices  30.7 us (27%)
  waiting for transfers between devices  29 us (26%)
  local copies, waits for them, and re-layouts  3.1 us (3%)
  between operations  1.57 us (1%)
    pallas_call x9, Pallas kernels, call(): pl.pallas_call(body, out_shape=[jax.ShapeDtypeStruct(s, t) for s, t in ou...  47.5 us
    all_to_all x4, starting transfers between devices, exchange(): return lax.all_to_all(x, AXES, split_axis=0, concat_axis=0, tiled=True)  30.7 us
    all_to_all x4, waiting for transfers between devices, exchange(): return lax.all_to_all(x, AXES, split_axis=0, concat_axis=0, tiled=True)  29 us
    unnamed x11, local copies, waits for them, and re-layouts  2.41 us
  transfers between devices with their start and end apart: 4, of which 3 were waited for; matrix products, arithmetic and copies ran while one was open for 1% of the time, Pallas kernels for 26%

profile of v2, /device:TPU:1, one launch (start us, length us, event | category | flops | bytes accessed | tf_op | source)
XLA Modules:
  0.0 111.9 jit_solution(2566491199249178967)
XLA Ops:
  0.6 2.8 %pull.1 = bf16[128,8,128]{2,1,0:T(8,128)(2,1)} custom-call(s32[8,128]{1,0:T(8,128)} %bitcast.7, bf16[1024,128]{1,0:T(8,128)(2,1)} %refs_6_.1), custom_call_target="tpu_custom_call" | custom-call | tf_op jit(solution)/shard_map/pull/pallas_call | solution.py:424
  3.4 11.5 %all-to-all-start = ((bf16[128,8,128]{2,1,0:T(8,128)(2,1)}), bf16[128,8,128]{2,1,0:T(8,128)(2,1)S(1)}, u32[]{:S(2)}, u32[]{:S(2)}) async-start(bf16[128,8,128]{2,1,0:T(8,128)(2,1)} %pull.1), calls=%async_computation | async-start | bytes 524288 | tf_op jit(solution)/shard_map/all_to_all | solution.py:437
  15.6 16.3 %build.1 = (bf16[1024,1024]{1,0:T(8,128)(2,1)}, bf16[1024,1024]{1,0:T(8,128)(2,1)}, bf16[1024,1024]{1,0:T(8,128)(2,1)}, bf16[1024,1024]{1,0:T(8,128)(2,1)}, f32[...) custom-call(s32[1]{0:T(128)S(6)} %copy.16.refs_0_, s32[64,128]{1,0:T(8,128)} %bitcast.10, s32[64,128]{1,0:T(8,128)} %bitcast.11, ...), custom_call_target="tpu_custom_call" | custom-call | flops 20000000000 | bytes 20000000 | tf_op jit(solution)/shard_map/build/pallas_call | solution.py:424
  31.9 0.0 all-to-all-done.refs_0_.refs_3_
  31.9 0.0 copy-start.3
  31.9 0.7 copy-done.3
  32.6 0.0 copy-start.4
  32.6 3.4 %push.1 = bf16[128,16,128]{2,1,0:T(8,128)(2,1)} custom-call(bf16[128,8,128]{2,1,0:T(8,128)(2,1)} %copy-done.3, f32[1024,128]{1,0:T(8,128)} %get-tuple-element.27.refs_1_, bf16[1024,1024]{1,0:T(8,128)(2,1)} %get-tuple-element.28.refs_2_.refs_0_, bf16[1024,128]{1,0:T(8,128)(2,1)} %get-tuple-element.29.refs_3_), custom_call_target="tpu_custom_call" | custom-call | tf_op jit(solution)/shard_map/push/pallas_call | solution.py:424
  36.0 11.2 %all-to-all-start.1 = ((bf16[128,16,128]{2,1,0:T(8,128)(2,1)}), bf16[128,16,128]{2,1,0:T(8,128)(2,1)S(1)}, u32[]{:S(2)}, u32[]{:S(2)}) async-start(bf16[128,16,128]{2,1,0:T(8,128)(2,1)} %push.1), calls=%async_computation.1 | async-start | bytes 1048576 | tf_op jit(solution)/shard_map/all_to_all | solution.py:437
  47.2 0.0 copy-done.4
  47.2 0.1 copy.15
  47.3 0.7 reshape.25.refs_0_
  48.0 4.7 %local.1 = (bf16[1024,1024]{1,0:T(8,128)(2,1)}, bf16[128,1024]{1,0:T(8,128)(2,1)}, f32[1024,128]{1,0:T(8,128)}, bf16[1024,128]{1,0:T(8,128)(2,1)}) custom-call(bf16[1024,128]{1,0:T(8,128)(2,1)} %refs_6_.1, s32[8,128]{1,0:T(8,128)} %bitcast.8, bf16[1024,1024]{1,0:T(8,128)(2,1)} %get-tuple-element.30.refs_2_.refs_3_, bf16[128,8,128]{2,1,0:T(8,128)(2,1)} %copy-done.3, ...), custom_call_target="tpu_custom_call" | custom-call | flops 2000000000 | bytes 6000000 | tf_op jit(solution)/shard_map/local/pallas_call | solution.py:424
  52.8 8.5 %all-to-all-done.1.refs_1_.refs_6_ = bf16[128,16,128]{2,1,0:T(8,128)(2,1)S(1)} async-done(((bf16[128,16,128]{2,1,0:T(8,128)(2,1)}), bf16[128,16,128]{2,1,0:T(8,128)(2,1)S(1)}, u32[]{:S(2)}, u32[]{:S(2)}) %all-to-all-start.1) | async-done | bytes 524320 | tf_op jit(solution)/shard_map/all_to_all | solution.py:437
  61.3 0.0 copy-start.1
  61.3 0.8 copy-done.1
  62.1 6.6 %dense.1 = (bf16[1024,256]{1,0:T(8,128)(2,1)}, bf16[1024,256]{1,0:T(8,128)(2,1)}, bf16[1024,128]{1,0:T(8,128)(2,1)}, bf16[128,16,128]{2,1,0:T(8,128)(2,1)}, f32[8,128]{1,0:T(8,128)}) custom-call(s32[1,1024]{1,0:T(1,128)} %reshape.25.refs_0_, bf16[128,16,128]{2,1,0:T(8,128)(2,1)} %copy-done.1, bf16[1024,128]{1,0:T(8,128)(2,1)} %get-tuple-element.32.refs_2_, ...), custom_call_target="tpu_custom_call" | custom-call | tf_op jit(solution)/shard_map/dense/pallas_call | solution.py:424
  68.7 4.0 %all-to-all-start.2 = ((bf16[128,16,128]{2,1,0:T(8,128)(2,1)}), bf16[128,16,128]{2,1,0:T(8,128)(2,1)S(1)}, u32[]{:S(2)}, u32[]{:S(2)}) async-start(bf16[128,16,128]{2,1,0:T(8,128)(2,1)} %get-tuple-element.37), calls=%async_computation.2 | async-start | bytes 1048576 | tf_op jit(solution)/shard_map/all_to_all | solution.py:437
  72.7 4.7 %back_local.1 = (bf16[1024,1024]{1,0:T(8,128)(2,1)}, f32[1024,128]{1,0:T(8,128)}, f32[1024,128]{1,0:T(8,128)}) custom-call(bf16[1024,1024]{1,0:T(8,128)(2,1)} %get-tuple-element.28.refs_2_.refs_0_, bf16[1024,128]{1,0:T(8,128)(2,1)} %get-tuple-element.38.refs_1_, bf16[1024,1024]{1,0:T(8,128)(2,1)} %get-tuple-element.31.refs_4_.refs_2_, ...), custom_call_target="tpu_custom_call" | custom-call | flops 2000000000 | bytes 6000000 | tf_op jit(solution)/shard_map/back_local/pallas_call | solution.py:424
  77.4 9.5 %all-to-all-done.2.refs_0_ = bf16[128,16,128]{2,1,0:T(8,128)(2,1)S(1)} async-done(((bf16[128,16,128]{2,1,0:T(8,128)(2,1)}), bf16[128,16,128]{2,1,0:T(8,128)(2,1)S(1)}, u32[]{:S(2)}, u32[]{:S(2)}) %all-to-all-start.2) | async-done | bytes 524320 | tf_op jit(solution)/shard_map/all_to_all | solution.py:437
  86.9 0.0 copy-start.2
  86.9 0.8 copy-done.2
  87.7 3.3 %back_push.1 = bf16[128,16,128]{2,1,0:T(8,128)(2,1)} custom-call(bf16[128,16,128]{2,1,0:T(8,128)(2,1)} %copy-done.2, f32[1024,128]{1,0:T(8,128)} %get-tuple-element.40.refs_1_, f32[8,128]{1,0:T(8,128)} %get-tuple-element.41.refs_2_, bf16[1024,1024]{1,0:T(8,128)(2,1)} %get-tuple-element.42.refs_3_), custom_call_target="tpu_custom_call" | custom-call | tf_op jit(solution)/shard_map/back_push/pallas_call | solution.py:424
  91.0 4.0 %all-to-all-start.3 = ((bf16[128,16,128]{2,1,0:T(8,128)(2,1)}), bf16[128,16,128]{2,1,0:T(8,128)(2,1)S(1)}, u32[]{:S(2)}, u32[]{:S(2)}) async-start(bf16[128,16,128]{2,1,0:T(8,128)(2,1)} %back_push.1), calls=%async_computation.3 | async-start | bytes 1048576 | tf_op jit(solution)/shard_map/all_to_all | solution.py:437
  95.0 0.0 copy-start
  95.0 3.2 %back_mirror.1.refs_2_ = f32[1024,128]{1,0:T(8,128)} custom-call(bf16[128,16,128]{2,1,0:T(8,128)(2,1)} %copy-done.2, bf16[1024,1024]{1,0:T(8,128)(2,1)} %get-tuple-element.43.refs_1_, f32[1024,128]{1,0:T(8,128)} %get-tuple-element.44.refs_2_), custom_call_target="tpu_custom_call" | custom-call | flops 2000000000 | bytes 6000000 | tf_op jit(solution)/shard_map/back_mirror/pallas_call | solution.py:424
  98.2 11.0 %all-to-all-done.3.refs_1_ = bf16[128,16,128]{2,1,0:T(8,128)(2,1)S(1)} async-done(((bf16[128,16,128]{2,1,0:T(8,128)(2,1)}), bf16[128,16,128]{2,1,0:T(8,128)(2,1)S(1)}, u32[]{:S(2)}, u32[]{:S(2)}) %all-to-all-start.3) | async-done | bytes 524320 | tf_op jit(solution)/shard_map/all_to_all | solution.py:437
  109.2 0.0 copy-done
  109.2 2.6 %last.1 = (bf16[1024,128]{1,0:T(8,128)(2,1)}, f32[128,256]{1,0:T(8,128)}, f32[128,256]{1,0:T(8,128)}, f32[2,128]{1,0:T(2,128)}) custom-call(s32[1,1024]{1,0:T(1,128)S(1)} %copy-done, bf16[128,16,128]{2,1,0:T(8,128)(2,1)S(1)} %all-to-all-done.3.refs_1_, f32[1024,128]{1,0:T(8,128)} %back_mirror.1.refs_2_), custom_call_target="tpu_custom_call" | custom-call | tf_op jit(solution)/shard_map/last/pallas_call | solution.py:424
Async XLA Ops:
  3.4 28.5 %all-to-all-start = ((bf16[128,8,128]{2,1,0:T(8,128)(2,1)}), bf16[128,8,128]{2,1,0:T(8,128)(2,1)S(1)}, u32[]{:S(2)}, u32[]{:S(2)}) async-start(bf16[128,8,128]{2,1,0:T(8,128)(2,1)} %pull.1), calls=%async_computation | async-start | bytes 524288 | tf_op jit(solution)/shard_map/all_to_all | solution.py:437
  31.9 0.7 copy-start.3
  32.6 14.6 %copy-start.4 = (s32[1,128,8]{1,2,0:T(8,128)S(1)}, s32[1,128,8]{1,2,0:T(8,128)}, u32[]{:S(2)}) copy-start(s32[1,128,8]{1,2,0:T(8,128)} %param.17) | copy-start | bytes 12292
  36.0 25.3 %all-to-all-start.1 = ((bf16[128,16,128]{2,1,0:T(8,128)(2,1)}), bf16[128,16,128]{2,1,0:T(8,128)(2,1)S(1)}, u32[]{:S(2)}, u32[]{:S(2)}) async-start(bf16[128,16,128]{2,1,0:T(8,128)(2,1)} %push.1), calls=%async_computation.1 | async-start | bytes 1048576 | tf_op jit(solution)/shard_map/all_to_all | solution.py:437
  61.3 0.8 copy-start.1
  68.7 18.2 %all-to-all-start.2 = ((bf16[128,16,128]{2,1,0:T(8,128)(2,1)}), bf16[128,16,128]{2,1,0:T(8,128)(2,1)S(1)}, u32[]{:S(2)}, u32[]{:S(2)}) async-start(bf16[128,16,128]{2,1,0:T(8,128)(2,1)} %get-tuple-element.37), calls=%async_computation.2 | async-start | bytes 1048576 | tf_op jit(solution)/shard_map/all_to_all | solution.py:437
  86.9 0.8 copy-start.2
  91.0 18.2 %all-to-all-start.3 = ((bf16[128,16,128]{2,1,0:T(8,128)(2,1)}), bf16[128,16,128]{2,1,0:T(8,128)(2,1)S(1)}, u32[]{:S(2)}, u32[]{:S(2)}) async-start(bf16[128,16,128]{2,1,0:T(8,128)(2,1)} %back_push.1), calls=%async_computation.3 | async-start | bytes 1048576 | tf_op jit(solution)/shard_map/all_to_all | solution.py:437
  95.0 14.2 %copy-start = (s32[1,1024]{1,0:T(1,128)S(1)}, s32[1,1024]{1,0:T(1,128)}, u32[]{:S(2)}) copy-start(s32[1,1024]{1,0:T(1,128)} %reshape.25.refs_0_) | copy-start | bytes 12292

commit v3 on v2

--- a/solution.py
+++ b/solution.py
@@ -18,7 +18,7 @@
 H = 256
 LANES = 128
 COPIES = 6
-TURN = 128
+TURN = 256
 PARTS = 4
 WORDS = SLOTS * (SLOTS // 512)
 
@@ -45,29 +45,60 @@
     return jnp.where(places == line, 1.0, 0.0).astype(BF16)
 
 
+def diagonal(slots):
+    shape = (PEERS, 8, 8)
+    spread = jnp.broadcast_to(slots[:, None, :], shape)
+    here = lax.broadcasted_iota(jnp.int32, shape, 1) == lax.broadcasted_iota(jnp.int32, shape, 2)
+    return jnp.sum(jnp.where(here, spread, 0.0), axis=2, keepdims=True)
+
+
 def as_column(lists):
-    turned = jnp.transpose(lists.astype(F32))
-    shape = (PEERS, 8, 8)
-    spread = jnp.broadcast_to(turned[:, None, :], shape)
-    here = lax.broadcasted_iota(jnp.int32, shape, 1) == lax.broadcasted_iota(jnp.int32, shape, 2)
-    column = jnp.sum(jnp.where(here, spread, 0.0), axis=2, keepdims=True)
-    return column.reshape(MIRRORS, 1).astype(jnp.int32)
-
-
-def pull_kernel(lists_ref, rows_ref, out_ref):
-    matrix = gather_matrix(as_column(lists_ref[...]))
+    return diagonal(jnp.transpose(lists.astype(F32))).reshape(MIRRORS, 1).astype(jnp.int32)
+
+
+def numbers():
+    shape = (EDGES // LANES, LANES)
+    row = lax.broadcasted_iota(jnp.int32, shape, 0) * LANES
+    return row + lax.broadcasted_iota(jnp.int32, shape, 1)
+
+
+def pull_kernel(
+    live_ref, lists_ref, src_ref, dst_ref, rows_ref, out_ref, gather_ref, code_ref, hot_ref, low_ref
+):
+    gather_ref[...] = gather_matrix(as_column(lists_ref[...]))
+    gather_ref.send()
+    src, dst = src_ref[...], dst_ref[...]
+    live = numbers() < live_ref[0]
+    place = ((src >> 7) & 3) * SLOTS + dst
+    code = place | ((src & 127) << 13) | ((src >> 9) << 24)
+    code_ref[...] = jnp.where(live, code, 128 << 13)
+    code_ref.send()
+    slot = jnp.where(live, dst - MASTERS, -1)
+    peer, low = slot >> 3, slot & 7
+    peers = lax.broadcasted_iota(jnp.int32, (PEERS, LANES), 0)
+    lows = lax.broadcasted_iota(jnp.int32, (16, LANES), 0)
+    for k in range(EDGES // LANES):
+        at = pl.ds(k * LANES, LANES)
+        hot_ref[:, at] = jnp.where(peers == peer[k : k + 1], 1.0, 0.0).astype(BF16)
+        low_ref[:, at] = jnp.where(lows == low[k : k + 1], 1.0, 0.0).astype(BF16)
+    tally = jnp.broadcast_to(diagonal(dot_nt(hot_ref[...], low_ref[...])[:, :8]), (PEERS, 8, LANES))
+    high, rest = split(tally)
+    left = lax.broadcasted_iota(jnp.int32, tally.shape, 2) < LANES // 2
+    tally = jnp.where(left, high, rest)
     rows = rows_ref[...]
     for c in range(2):
-        picked = dot(matrix[c * 512 : (c + 1) * 512], rows).reshape(PEERS // 2, 8, F)
+        picked = dot(gather_ref[c * 512 : (c + 1) * 512], rows).reshape(PEERS // 2, 8, F)
         half = pl.ds(c * (PEERS // 2), PEERS // 2)
-        out_ref[half] = picked.astype(BF16)
+        both = [picked, tally[c * (PEERS // 2) : (c + 1) * (PEERS // 2)]]
+        out_ref[half] = jnp.concatenate(both, axis=1).astype(BF16)
         out_ref.send(half)
 
 
 def build_kernel(
-    live_ref, src_ref, dst_ref, rows_ref, mm_ref, mg_ref, gm_ref, gg_ref, sums_ref, tally_ref,
-    code_ref, codes, sem, *tables3
+    live_ref, code_ref, rows_ref, mm_ref, mg_ref, gm_ref, gg_ref, sums_ref, codes, sem, *tables3
 ):
+    load = pltpu.make_async_copy(code_ref, codes, sem)
+    load.start()
     tables = [t.reshape(WORDS, LANES) for t in tables3]
     n = live_ref[0]
 
@@ -76,26 +107,21 @@
             t[pl.ds(pl.multiple_of(i * 256, 256), 256), :] = jnp.zeros((256, LANES), jnp.int32)
         return carry
 
-    lax.fori_loop(0, WORDS // 512, clear, 0)
-    src, dst = src_ref[...], dst_ref[...]
-    shape = (EDGES // LANES, LANES)
-    number = lax.broadcasted_iota(jnp.int32, shape, 0) * LANES
-    number = number + lax.broadcasted_iota(jnp.int32, shape, 1)
-    place = ((src >> 7) & 3) * SLOTS + dst
-    code = place | ((src & 127) << 13) | ((src >> 9) << 24)
-    code_ref[...] = jnp.where(number < n, code, 128 << 13)
-    move = pltpu.make_async_copy(code_ref, codes, sem)
-    move.start()
-    lax.fori_loop(WORDS // 512, WORDS // 256, clear, 0)
-    move.wait()
+    lax.fori_loop(0, WORDS // 256, clear, 0)
+    load.wait()
 
     lanes = lax.broadcasted_iota(jnp.int32, (1, LANES), 1) << 13
     one = jnp.ones((1, LANES), jnp.int32)
+
+    def code_at(k, i):
+        row, lane = divmod(k, LANES)
+        part = codes.at[pl.ds(row, EDGES // LANES - TURN // LANES + 1), pl.ds(lane, 1)]
+        return part[i * (TURN // LANES), 0]
 
     def turn(i, carry):
         for start in range(0, TURN, COPIES):
             count = min(COPIES, TURN - start)
-            words = [codes[i, start + k] for k in range(count)]
+            words = [code_at(start + k, i) for k in range(count)]
             where = [w & (WORDS - 1) for w in words]
             adds = []
             for w in words:
@@ -120,8 +146,7 @@
                 seen = seen + jnp.sum(counts.reshape(16, 8, LANES), axis=0)
         return seen
 
-    ones = jnp.ones((MASTERS, LANES), BF16)
-    wide = jnp.concatenate([rows_ref[...], ones], axis=1)
+    rows = rows_ref[...]
 
     def widen(read):
         def mirrors(i, seen):
@@ -130,10 +155,7 @@
 
         def masters(i, seen):
             e = pl.multiple_of(i * 256, 256)
-            own = dot(gm_ref[pl.ds(e, 256), :], wide)
-            far = dot(gg_ref[pl.ds(e, 256), :], ones)
-            sums_ref[pl.ds(e, 256), :] = own[:, :F]
-            tally_ref[pl.ds(e, 256), :] = two_parts(own[:, F:] + far)
+            sums_ref[pl.ds(e, 256), :] = dot(gm_ref[pl.ds(e, 256), :], rows)
             for h in range(2):
                 d = pl.multiple_of(i * 256 + h * 128, 128)
                 seen = put(mm_ref, mg_ref, d, d, read, seen)
@@ -146,11 +168,10 @@
         gm_ref.send()
         seen = lax.fori_loop(0, MASTERS // 256, masters, seen)
         sums_ref.send()
-        tally_ref.send()
         return seen
 
     def finish():
-        for ref in (mm_ref, mg_ref, gm_ref, gg_ref, sums_ref, tally_ref):
+        for ref in (mm_ref, mg_ref, gm_ref, gg_ref, sums_ref):
             ref.wait()
 
     def read_bytes(at):
@@ -197,81 +218,82 @@
     return high, (x - high).astype(BF16).astype(F32)
 
 
-def two_parts(x):
-    high, low = split(x)
-    left = lax.broadcasted_iota(jnp.int32, x.shape, 1) < LANES // 2
-    return jnp.where(left, high, low).astype(BF16)
-
-
-def push_kernel(got_ref, sums_ref, gg_ref, tally_ref, out_ref):
-    got = got_ref[...].reshape(MIRRORS, F)
+def parts_of(got):
+    got = got.astype(F32)
+    return got[:, :8].reshape(MIRRORS, F).astype(BF16), got[:, 8:]
+
+
+def push_kernel(got_ref, sums_ref, gg_ref, out_ref):
+    got, _ = parts_of(got_ref[...])
     for c in range(PARTS):
         rows, peers = part_of(MIRRORS, c), part_of(PEERS, c)
         sums = dot(gg_ref.part(c), got) + sums_ref[rows]
-        tally = tally_ref[rows].astype(F32)
-        shape = (PEERS // PARTS, 8, F)
-        both = jnp.concatenate([sums.reshape(shape), tally.reshape(shape)], axis=1)
-        out_ref[peers] = both.astype(BF16)
+        out_ref[peers] = sums.reshape(PEERS // PARTS, 8, F).astype(BF16)
         out_ref.send(peers)
 
 
 def local_kernel(
-    rows_ref, lists_ref, mm_ref, got_ref, mg_ref, gather_ref, turned_ref, sums_ref, tally_ref
+    got_ref, line_ref, rows_ref, mm_ref, mg_ref, turned_ref, sums_ref, inverse_ref
 ):
-    gather_ref[...] = gather_matrix(as_column(lists_ref[...]))
-    gather_ref.send()
+    both = got_ref[...].astype(F32)
+    both = [both[:, :8].reshape(MIRRORS, F), both[:, 8:].reshape(MIRRORS, LANES)]
+    both = jnp.concatenate(both, axis=1).astype(BF16)
+    got, tally = both[:, :F], both[:, F:]
+    degree = dot(scatter_matrix(line_ref[...]), tally)
+    degree = degree + pltpu.roll(degree, LANES // 2, 1)
     rows = rows_ref[...]
     turned_ref[...] = rows.astype(F32).T.astype(BF16)
     turned_ref.send()
     ones = jnp.ones((MASTERS, LANES), BF16)
-    got = got_ref[...].reshape(MIRRORS, F)
     both = dot(mm_ref[...], jnp.concatenate([rows, ones], axis=1)) + dot(
         mg_ref[...], jnp.concatenate([got, ones], axis=1)
     )
     sums_ref[...] = both[:, :F]
     sums_ref.send()
-    tally_ref[...] = two_parts(both[:, F:])
-    tally_ref.send()
+    inverse_ref[...] = 1.0 / jnp.maximum(both[:, F:] + degree, 1.0)
+    inverse_ref.send()
 
 
 def dense_kernel(
-    line_ref, got_ref, tally_ref, sums_ref, self_ref, bias_ref, rows_ref, neigh_ref, cot_ref,
+    got_ref, line_ref, sums_ref, inverse_ref, self_ref, bias_ref, rows_ref, neigh_ref, cot_ref,
     gather_ref, turned_ref,
     act_ref, grad_ref, msg_ref, out_ref, total_ref,
 ):
-    scatter = scatter_matrix(line_ref[...])
-    got = got_ref[...].astype(F32)
-    wide = jnp.concatenate(
-        [got[:, :8].reshape(MIRRORS, F), got[:, 8:].reshape(MIRRORS, LANES)], axis=1
-    ).astype(BF16)
-    folded = dot(scatter, wide)
-    tally = folded[:, F:] + tally_ref[...].astype(F32)
-    degree = tally + pltpu.roll(tally, LANES // 2, 1)
-    inverse = 1.0 / jnp.maximum(degree, 1.0)
-    mean = (sums_ref[...] + folded[:, :F]) * inverse
-    w = neigh_ref[...]
-    pre = dot(rows_ref[...], self_ref[...]) + dot(mean.astype(BF16), w) + bias_ref[...]
-    sig = jax.nn.sigmoid(pre)
-    act_ref[...] = (pre * sig).astype(BF16)
-    act_ref.send()
-    grad = (cot_ref[...].astype(F32) * sig * (1.0 + pre * (1.0 - sig))).astype(BF16)
-    grad_ref[...] = grad
-    grad_ref.send()
-    msg = (dot_nt(grad, w) * inverse).astype(BF16)
-    msg_ref[...] = msg
-    msg_ref.send()
-    picked = dot(gather_ref[...], msg).reshape(PEERS, 8, F)
-    turned = jnp.concatenate([turned_ref[...], mean.T.astype(BF16)], axis=0)
-    terms = dot(turned, grad)
+    got = got_ref[...].reshape(MIRRORS, F)
+    w_self, w_neigh, bias, line = self_ref[...], neigh_ref[...], bias_ref[...], line_ref[...]
+    size = MASTERS // PARTS
+    terms, total = 0.0, 0.0
+    for c in range(PARTS):
+        rows = part_of(MASTERS, c)
+        places = lax.broadcasted_iota(jnp.int32, (size, MIRRORS), 0) + c * size
+        scatter = jnp.where(places == line, 1.0, 0.0).astype(BF16)
+        inverse = inverse_ref[rows]
+        mean = (sums_ref[rows] + dot(scatter, got)) * inverse
+        pre = dot(rows_ref[rows], w_self) + dot(mean.astype(BF16), w_neigh) + bias
+        sig = jax.nn.sigmoid(pre)
+        act_ref[rows] = (pre * sig).astype(BF16)
+        act_ref.send(rows)
+        grad = (cot_ref[rows].astype(F32) * sig * (1.0 + pre * (1.0 - sig))).astype(BF16)
+        grad_ref[rows] = grad
+        grad_ref.send(rows)
+        msg_ref[rows] = (dot_nt(grad, w_neigh) * inverse).astype(BF16)
+        msg_ref.send(rows)
+        turned = [turned_ref[:, c * size : (c + 1) * size], mean.T.astype(BF16)]
+        terms = terms + dot(jnp.concatenate(turned, axis=0), grad)
+        total = total + dot(jnp.ones((8, size), BF16), grad)
     flat = jnp.concatenate([terms[:, :F], terms[:, F:]], axis=0).reshape(PEERS // 2, 8, F)
     high, low = split(flat)
     first = lax.broadcasted_iota(jnp.int32, (PEERS // 2, 8, F), 1) < 4
     even = jnp.where(first, high, pltpu.roll(low, 4, 1))
     odd = jnp.where(first, pltpu.roll(high, 4, 1), low)
     mixed = jnp.stack([even, odd], axis=1).reshape(PEERS, 8, F)
-    out_ref[...] = jnp.concatenate([picked, mixed], axis=1).astype(BF16)
-    out_ref.send()
-    total = dot(jnp.ones((8, MASTERS), BF16), grad)
+    msg = msg_ref[...]
+    for c in range(PARTS):
+        peers, count = part_of(PEERS, c), PEERS // PARTS
+        picked = dot(gather_ref.part(c), msg).reshape(count, 8, F)
+        both = [picked, mixed[c * count : (c + 1) * count]]
+        out_ref[peers] = jnp.concatenate(both, axis=1).astype(BF16)
+        out_ref.send(peers)
     high, low = split(total)
     sub = lax.broadcasted_iota(jnp.int32, (8, F), 0)
     tile = jnp.where(sub == 4, high[:, :F], 0.0)
@@ -282,7 +304,7 @@
 
 
 def back_local_kernel(
-    gg_ref, msg_ref, mg_ref, mm_ref, grad_ref, w_ref, _, turned_ref, mirror_ref, base_ref
+    gg_ref, msg_ref, mg_ref, mm_ref, grad_ref, w_ref, turned_ref, mirror_ref, base_ref
 ):
     turned_ref[...] = gg_ref[...].T
     turned_ref.send()
@@ -294,9 +316,8 @@
 
 
 def back_push_kernel(got_ref, mirror_ref, total_ref, turned_ref, out_ref):
-    got = got_ref[...].astype(F32)
-    rows = got[:, :8].reshape(MIRRORS, F).astype(BF16)
-    total = jnp.sum(got[:, 8:], axis=0)
+    rows, terms = parts_of(got_ref[...])
+    total = jnp.sum(terms, axis=0)
     total = total + pltpu.roll(total, 4, 0)
     sub = lax.broadcasted_iota(jnp.int32, (8, F), 0)
     tile = jnp.where(sub < 4, total, total_ref[...])
@@ -316,11 +337,9 @@
 
 
 def last_kernel(line_ref, got_ref, base_ref, grad_ref, self_ref, neigh_ref, bias_ref):
-    got = got_ref[...].astype(F32)
-    rows = got[:, :8].reshape(MIRRORS, F).astype(BF16)
+    rows, tiles = parts_of(got_ref[...])
     grad_ref[...] = (dot(scatter_matrix(line_ref[...]), rows) + base_ref[...]).astype(BF16)
     grad_ref.send()
-    tiles = got[:, 8:]
     pairs = tiles.reshape(PEERS // 2, 2, 8, F)
     first = lax.broadcasted_iota(jnp.int32, (PEERS // 2, 8, F), 1) < 4
     flat = jnp.where(first, pairs[:, 0], pltpu.roll(pairs[:, 1], 4, 1)).reshape(2 * H, F)
@@ -338,7 +357,6 @@
 SMEM = pl.BlockSpec(memory_space=pltpu.SMEM)
 HBM = pl.BlockSpec(memory_space=pltpu.HBM)
 ALL = 60 * 1024 * 1024
-NEAR = 55_800_000
 
 
 class Loaded:
@@ -392,9 +410,12 @@
             pltpu.make_async_copy(self.held.at[rows], self.target.at[rows], self.sem).start()
 
 
-def call(kernel, ins, outs, name, near=(), scalars=(), scratch=(), parts=None, idle=(), flops=0, moved=0):
+def call(
+    kernel, ins, outs, name, near=(), scalars=(), bare=(), scratch=(), parts=None,
+    room=ALL, flops=0, moved=0,
+):
     parts = parts or {}
-    far = [k for k in range(len(ins)) if k not in (*near, *scalars, *idle)]
+    far = [k for k in range(len(ins)) if k not in (*near, *scalars, *bare)]
     specs = [VMEM if k in near else SMEM if k in scalars else HBM for k in range(len(ins))]
     held = [pltpu.VMEM(ins[k].shape, ins[k].dtype) for k in far]
     held += [pltpu.VMEM(s, t) for s, t in outs]
@@ -403,23 +424,22 @@
 
     def body(*refs):
         operands, refs = list(refs[: len(ins)]), refs[len(ins) :]
-        targets, refs = refs[: len(outs)], refs[len(outs) :]
+        results, refs = list(refs[: len(outs)]), refs[len(outs) :]
         copies, refs = refs[: len(far)], refs[len(far) :]
-        results, refs = refs[: len(outs)], refs[len(outs) :]
+        holds, refs = refs[: len(outs)], refs[len(outs) :]
         load_sems, store_sems = refs[0], refs[1]
         first = 0
         for k, copy, count in zip(far, copies, counts, strict=True):
             operands[k] = Loaded(operands[k], copy, load_sems, first, count)
             first += count
-        stores = [
-            Stored(results[k], targets[k], store_sems.at[k]) for k in range(len(outs))
-        ]
-        kernel(*operands, *stores, *refs[2:])
+        for k, hold in enumerate(holds):
+            results[k] = Stored(hold, results[k], store_sems.at[k])
+        kernel(*operands, *results, *refs[2:])
         for k in far:
             operands[k].wait()
-        for store in stores:
-            if not store.waited:
-                store.wait()
+        for result in results:
+            if not result.waited:
+                result.wait()
 
     return pl.pallas_call(
         body,
@@ -427,7 +447,7 @@
         in_specs=specs,
         out_specs=[HBM] * len(outs),
         scratch_shapes=held + [dma((max(sum(counts), 1),)), dma((len(outs),))] + list(scratch),
-        compiler_params=pltpu.CompilerParams(vmem_limit_bytes=NEAR if near else ALL),
+        compiler_params=pltpu.CompilerParams(vmem_limit_bytes=room),
         cost_estimate=pl.CostEstimate(flops=flops, bytes_accessed=moved, transcendentals=0),
         name=name,
     )(*ins)
@@ -443,32 +463,44 @@
     square = ((1024, 1024), BF16)
     payload = ((PEERS, 16, F), BF16)
 
-    (out1,) = call(pull_kernel, (lists, features), [((PEERS, 8, F), BF16)], "pull")
+    edges = (EDGES // LANES, LANES)
+    src, dst = src_slot.reshape(edges), dst_slot.reshape(edges)
+    rows_f32, rows_bf16 = ((1024, F), F32), ((1024, F), BF16)
+    out1, gather, code = call(
+        pull_kernel,
+        (edge_live, lists, src, dst, features),
+        [payload, square, (edges, jnp.int32)],
+        "pull",
+        scalars=(0,),
+        scratch=[pltpu.VMEM((PEERS, EDGES), BF16), pltpu.VMEM((16, EDGES), BF16)],
+    )
     got1 = exchange(out1)
-
-    edges = (EDGES // LANES, LANES)
-    rows_f32, rows_bf16 = ((1024, F), F32), ((1024, F), BF16)
-    mm, mg, gm, gg, sums, tally = call(
+    mm, mg, gm, gg, sums = call(
         build_kernel,
-        (edge_live, src_slot.reshape(edges), dst_slot.reshape(edges), features),
-        [square] * 4 + [rows_f32, rows_bf16],
+        (edge_live, code, features),
+        [square] * 4 + [rows_f32],
         "build",
         scalars=(0,),
-        scratch=[
-            pltpu.VMEM(edges, jnp.int32),
-            pltpu.SMEM(edges, jnp.int32),
-            pltpu.SemaphoreType.DMA,
-        ]
+        bare=(1,),
+        scratch=[pltpu.SMEM(edges, jnp.int32), pltpu.SemaphoreType.DMA]
         + [pltpu.VMEM((WORDS, 1, LANES), jnp.int32) for _ in range(COPIES)],
         flops=20_000_000_000,
         moved=20_000_000,
     )
-    (out2,) = call(push_kernel, (got1, sums, gg, tally), [payload], "push", parts={2: PARTS})
+    (out2,) = call(
+        push_kernel,
+        (got1, sums, gg),
+        [((PEERS, 8, F), BF16)],
+        "push",
+        near=(0,),
+        room=55_400_000,
+        parts={2: PARTS},
+    )
     got2 = exchange(out2)
-    gather, turned, sums_m, tally_m = call(
+    turned, sums_m, inverse = call(
         local_kernel,
-        (features, lists, mm, got1, mg),
-        [square, ((F, MASTERS), BF16), rows_f32, rows_bf16],
+        (got1, line, features, mm, mg),
+        [((F, MASTERS), BF16), rows_f32, rows_f32],
         "local",
         flops=2_000_000_000,
         moved=6_000_000,
@@ -476,19 +508,21 @@
     act, grad, msg, out3, total = call(
         dense_kernel,
         (
-            line, got2, tally_m, sums_m, w_self, bias.reshape(1, H), features, w_neigh,
-            cotangent, gather, turned,
+            got2, line, sums_m, inverse, w_self, bias.reshape(1, H), features, w_neigh, cotangent,
+            gather, turned,
         ),
         [((MASTERS, H), BF16), ((MASTERS, H), BF16), rows_bf16, payload, ((8, F), F32)],
         "dense",
+        near=(0,),
+        room=55_800_000,
+        parts={9: PARTS},
     )
     got3 = exchange(out3)
     turned_gg, mirror, base = call(
         back_local_kernel,
-        (gg, msg, mg, mm, grad, w_self, got2),
+        (gg, msg, mg, mm, grad, w_self),
         [square, rows_f32, rows_f32],
         "back_local",
-        idle=(6,),
         flops=2_000_000_000,
         moved=6_000_000,
     )
@@ -497,6 +531,8 @@
         (got3, mirror, total, turned_gg),
         [payload],
         "back_push",
+        near=(0,),
+        room=55_200_000,
         parts={3: PARTS},
     )
     got4 = exchange(out4)
@@ -514,6 +550,7 @@
         [rows_bf16, ((F, H), F32), ((F, H), F32), ((2, F), F32)],
         "last",
         near=(1,),
+        room=55_700_000,
     )
     return act, grad_features, grad_self, grad_neigh, bias_out.reshape(H)
 

time: 112 us -> 107 us (0.955)
  local copies, waits for them, and re-layouts: 3.1 us -> 0.83 us
  waiting for transfers between devices: 29 us -> 27 us
    unnamed x11 -> x17, local copies, waits for them, and re-layouts: 2.41 us -> 0.14 us
    all_to_all x4, waiting for transfers between devices: 29 us -> 27 us  [exchange(): return lax.all_to_all(x, AXES, split_axis=0, concat_axis=0, tiled=True)]
  transfers between devices with their start and end apart: 4 -> 4, of which waited for: 3 -> 4; matrix products, arithmetic and copies ran while one was open for 1% -> 1% of each run, Pallas kernels for 26% -> 24%
where the time goes in v3:
time: 107 us
  Pallas kernels  46.5 us (43%)
  starting transfers between devices  31.2 us (29%)
  waiting for transfers between devices  27 us (25%)
  between operations  1.6 us (1%)
    pallas_call x9, Pallas kernels, call(): pl.pallas_call(body, out_shape=[jax.ShapeDtypeStruct(s, t) for s, t in ou...  46.5 us
    all_to_all x4, starting transfers between devices, exchange(): return lax.all_to_all(x, AXES, split_axis=0, concat_axis=0, tiled=True)  31.2 us
    all_to_all x4, waiting for transfers between devices, exchange(): return lax.all_to_all(x, AXES, split_axis=0, concat_axis=0, tiled=True)  27 us
  transfers between devices with their start and end apart: 4, of which 4 were waited for; matrix products, arithmetic and copies ran while one was open for 1% of the time, Pallas kernels for 24%

profile of v3, /device:TPU:1, one launch (start us, length us, event | category | flops | bytes accessed | tf_op | source)
XLA Modules:
  0.0 107.1 jit_solution(15287746180383727400)
XLA Ops:
  1.3 4.7 %pull.1 = (bf16[128,16,128]{2,1,0:T(8,128)(2,1)}, bf16[1024,1024]{1,0:T(8,128)(2,1)}, s32[64,128]{1,0:T(8,128)}) custom-call(s32[1]{0:T(128)S(6)} %copy.16.refs_0_, s32[8,128]{1,0:T(8,128)} %bitcast.10, s32[64,128]{1,0:T(8,128)} %bitcast.8, s32[64,128]{1,0:T(8,128)} %bitcast.9, bf16[1024,128]{1,0:T(8,128)(2,1)} %refs_6_.1), custom_call_target="tpu_custom_call" | custom-call | tf_op jit(solution)/shard_map/pull/pallas_call | solution.py:444
  6.0 11.5 %all-to-all-start = ((bf16[128,16,128]{2,1,0:T(8,128)(2,1)}), bf16[128,16,128]{2,1,0:T(8,128)(2,1)S(1)}, u32[]{:S(2)}, u32[]{:S(2)}) async-start(bf16[128,16,128]{2,1,0:T(8,128)(2,1)} %get-tuple-element.28), calls=%async_computation | async-start | bytes 1048576 | tf_op jit(solution)/shard_map/all_to_all | solution.py:457
  17.5 12.5 %build.1 = (bf16[1024,1024]{1,0:T(8,128)(2,1)}, bf16[1024,1024]{1,0:T(8,128)(2,1)}, bf16[1024,1024]{1,0:T(8,128)(2,1)}, bf16[1024,1024]{1,0:T(8,128)(2,1)}, f32[1024,128]{1,0:T(8,128)}) custom-call(s32[1]{0:T(128)S(6)} %copy.16.refs_0_, s32[64,128]{1,0:T(8,128)} %get-tuple-element.29.refs_1_, bf16[1024,128]{1,0:T(8,128)(2,1)} %refs_6_.1), custom_call_target="tpu_custom_call" | custom-call | flops 20000000000 | bytes 20000000 | tf_op jit(solution)/shard_map/build/pallas_call | solution.py:444
  30.1 0.0 copy-start.7
  30.1 1.5 %all-to-all-done.refs_0_ = bf16[128,16,128]{2,1,0:T(8,128)(2,1)S(1)} async-done(((bf16[128,16,128]{2,1,0:T(8,128)(2,1)}), bf16[128,16,128]{2,1,0:T(8,128)(2,1)S(1)}, u32[]{:S(2)}, u32[]{:S(2)}) %all-to-all-start) | async-done | bytes 524320 | tf_op jit(solution)/shard_map/all_to_all | solution.py:457
  31.6 0.0 copy-start
  31.6 3.2 %push.1 = bf16[128,8,128]{2,1,0:T(8,128)(2,1)} custom-call(bf16[128,16,128]{2,1,0:T(8,128)(2,1)S(1)} %all-to-all-done.refs_0_, f32[1024,128]{1,0:T(8,128)} %get-tuple-element.30.refs_1_, bf16[1024,1024]{1,0:T(8,128)(2,1)} %get-tuple-element.31.refs_2_.refs_0_), custom_call_target="tpu_custom_call" | custom-call | tf_op jit(solution)/shard_map/push/pallas_call | solution.py:444
  34.9 10.9 %all-to-all-start.1 = ((bf16[128,8,128]{2,1,0:T(8,128)(2,1)}), bf16[128,8,128]{2,1,0:T(8,128)(2,1)S(1)}, u32[]{:S(2)}, u32[]{:S(2)}) async-start(bf16[128,8,128]{2,1,0:T(8,128)(2,1)} %push.1), calls=%async_computation.1 | async-start | bytes 524288 | tf_op jit(solution)/shard_map/all_to_all | solution.py:457
  45.8 0.0 copy-done.7
  45.8 0.1 copy.15
  45.9 0.7 reshape.27.refs_1_.refs_0_
  46.6 0.0 copy-done
  46.6 0.0 copy-start.2
  46.6 0.0 copy-start.3
  46.6 0.0 copy-start.4
  46.6 0.0 copy-start.5
  46.6 5.5 %local.1 = (bf16[128,1024]{1,0:T(8,128)(2,1)}, f32[1024,128]{1,0:T(8,128)}, f32[1024,128]{1,0:T(8,128)}) custom-call(bf16[128,16,128]{2,1,0:T(8,128)(2,1)} %copy-done, s32[1,1024]{1,0:T(1,128)} %reshape.27.refs_1_.refs_0_, bf16[1024,128]{1,0:T(8,128)(2,1)} %refs_6_.1, bf16[1024,1024]{1,0:T(8,128)(2,1)} %get-tuple-element.32.refs_3_, ...), custom_call_target="tpu_custom_call" | custom-call | flops 2000000000 | bytes 6000000 | tf_op jit(solution)/shard_map/local/pallas_call | solution.py:444
  52.2 5.1 %all-to-all-done.1.refs_0_ = bf16[128,8,128]{2,1,0:T(8,128)(2,1)S(1)} async-done(((bf16[128,8,128]{2,1,0:T(8,128)(2,1)}), bf16[128,8,128]{2,1,0:T(8,128)(2,1)S(1)}, u32[]{:S(2)}, u32[]{:S(2)}) %all-to-all-start.1) | async-done | bytes 262176 | tf_op jit(solution)/shard_map/all_to_all | solution.py:457
  57.3 0.0 copy-done.2
  57.3 0.0 copy-done.3
  57.3 0.0 copy-done.4
  57.3 0.0 copy-done.5
  57.3 6.7 %dense.1 = (bf16[1024,256]{1,0:T(8,128)(2,1)}, bf16[1024,256]{1,0:T(8,128)(2,1)}, bf16[1024,128]{1,0:T(8,128)(2,1)S(1)}, bf16[128,16,128]{2,1,0:T(8,128)(2,1)}, f32[8,128]{1,0:T(8,128)S(1)}) custom-call(bf16[128,8,128]{2,1,0:T(8,128)(2,1)S(1)} %all-to-all-done.1.refs_0_, s32[1,1024]{1,0:T(1,128)S(1)} %copy-done.4, f32[1024,128]{1,0:T(8,128)} %get-tuple-element.34.refs_2_, ...), custom_call_target="tpu_custom_call" | custom-call | tf_op jit(solution)/shard_map/dense/pallas_call | solution.py:444
  64.0 0.0 copy-start.6
  64.0 4.7 %all-to-all-start.2 = ((bf16[128,16,128]{2,1,0:T(8,128)(2,1)}), bf16[128,16,128]{2,1,0:T(8,128)(2,1)S(1)}, u32[]{:S(2)}, u32[]{:S(2)}) async-start(bf16[128,16,128]{2,1,0:T(8,128)(2,1)} %get-tuple-element.39), calls=%async_computation.2 | async-start | bytes 1048576 | tf_op jit(solution)/shard_map/all_to_all | solution.py:457
  68.7 0.0 copy-done.6
  68.7 4.7 %back_local.1 = (bf16[1024,1024]{1,0:T(8,128)(2,1)}, f32[1024,128]{1,0:T(8,128)}, f32[1024,128]{1,0:T(8,128)}) custom-call(bf16[1024,1024]{1,0:T(8,128)(2,1)} %get-tuple-element.31.refs_2_.refs_0_, bf16[1024,128]{1,0:T(8,128)(2,1)} %copy-done.6, bf16[1024,1024]{1,0:T(8,128)(2,1)} %get-tuple-element.33.refs_4_.refs_2_, ...), custom_call_target="tpu_custom_call" | custom-call | flops 2000000000 | bytes 6000000 | tf_op jit(solution)/shard_map/back_local/pallas_call | solution.py:444
  73.4 9.4 %all-to-all-done.2.refs_0_ = bf16[128,16,128]{2,1,0:T(8,128)(2,1)S(1)} async-done(((bf16[128,16,128]{2,1,0:T(8,128)(2,1)}), bf16[128,16,128]{2,1,0:T(8,128)(2,1)S(1)}, u32[]{:S(2)}, u32[]{:S(2)}) %all-to-all-start.2) | async-done | bytes 524320 | tf_op jit(solution)/shard_map/all_to_all | solution.py:457
  82.8 0.0 copy-start.1
  82.8 3.3 %back_push.1 = bf16[128,16,128]{2,1,0:T(8,128)(2,1)} custom-call(bf16[128,16,128]{2,1,0:T(8,128)(2,1)S(1)} %all-to-all-done.2.refs_0_, f32[1024,128]{1,0:T(8,128)} %get-tuple-element.42.refs_1_, f32[8,128]{1,0:T(8,128)S(1)} %get-tuple-element.43.refs_2_, bf16[1024,1024]{1,0:T(8,128)(2,1)} %get-tuple-element.44.refs_3_), custom_call_target="tpu_custom_call" | custom-call | tf_op jit(solution)/shard_map/back_push/pallas_call | solution.py:444
  86.1 0.0 copy-done.1
  86.1 4.0 %all-to-all-start.3 = ((bf16[128,16,128]{2,1,0:T(8,128)(2,1)}), bf16[128,16,128]{2,1,0:T(8,128)(2,1)S(1)}, u32[]{:S(2)}, u32[]{:S(2)}) async-start(bf16[128,16,128]{2,1,0:T(8,128)(2,1)} %back_push.1), calls=%async_computation.3 | async-start | bytes 1048576 | tf_op jit(solution)/shard_map/all_to_all | solution.py:457
  90.1 3.2 %back_mirror.1.refs_2_ = f32[1024,128]{1,0:T(8,128)} custom-call(bf16[128,16,128]{2,1,0:T(8,128)(2,1)} %copy-done.1, bf16[1024,1024]{1,0:T(8,128)(2,1)} %get-tuple-element.45.refs_1_, f32[1024,128]{1,0:T(8,128)} %get-tuple-element.46.refs_2_), custom_call_target="tpu_custom_call" | custom-call | flops 2000000000 | bytes 6000000 | tf_op jit(solution)/shard_map/back_mirror/pallas_call | solution.py:444
  93.3 11.0 %all-to-all-done.3.refs_1_ = bf16[128,16,128]{2,1,0:T(8,128)(2,1)S(1)} async-done(((bf16[128,16,128]{2,1,0:T(8,128)(2,1)}), bf16[128,16,128]{2,1,0:T(8,128)(2,1)S(1)}, u32[]{:S(2)}, u32[]{:S(2)}) %all-to-all-start.3) | async-done | bytes 524320 | tf_op jit(solution)/shard_map/all_to_all | solution.py:457
  104.3 2.6 %last.1 = (bf16[1024,128]{1,0:T(8,128)(2,1)}, f32[128,256]{1,0:T(8,128)}, f32[128,256]{1,0:T(8,128)}, f32[2,128]{1,0:T(2,128)}) custom-call(s32[1,1024]{1,0:T(1,128)S(1)} %copy-done.4, bf16[128,16,128]{2,1,0:T(8,128)(2,1)S(1)} %all-to-all-done.3.refs_1_, f32[1024,128]{1,0:T(8,128)} %back_mirror.1.refs_2_), custom_call_target="tpu_custom_call" | custom-call | tf_op jit(solution)/shard_map/last/pallas_call | solution.py:444
Async XLA Ops:
  6.0 25.6 %all-to-all-start = ((bf16[128,16,128]{2,1,0:T(8,128)(2,1)}), bf16[128,16,128]{2,1,0:T(8,128)(2,1)S(1)}, u32[]{:S(2)}, u32[]{:S(2)}) async-start(bf16[128,16,128]{2,1,0:T(8,128)(2,1)} %get-tuple-element.28), calls=%async_computation | async-start | bytes 1048576 | tf_op jit(solution)/shard_map/all_to_all | solution.py:457
  30.1 15.7 %copy-start.7 = (s32[1,128,8]{1,2,0:T(8,128)S(1)}, s32[1,128,8]{1,2,0:T(8,128)}, u32[]{:S(2)}) copy-start(s32[1,128,8]{1,2,0:T(8,128)} %param.17) | copy-start | bytes 12292
  31.6 15.0 %copy-start = (bf16[128,16,128]{2,1,0:T(8,128)(2,1)}, bf16[128,16,128]{2,1,0:T(8,128)(2,1)S(1)}, u32[]{:S(2)}) copy-start(bf16[128,16,128]{2,1,0:T(8,128)(2,1)S(1)} %all-to-all-done.refs_0_) | copy-start | bytes 1572868
  34.9 22.4 %all-to-all-start.1 = ((bf16[128,8,128]{2,1,0:T(8,128)(2,1)}), bf16[128,8,128]{2,1,0:T(8,128)(2,1)S(1)}, u32[]{:S(2)}, u32[]{:S(2)}) async-start(bf16[128,8,128]{2,1,0:T(8,128)(2,1)} %push.1), calls=%async_computation.1 | async-start | bytes 524288 | tf_op jit(solution)/shard_map/all_to_all | solution.py:457
  46.6 10.6 %copy-start.2 = (bf16[128,256]{1,0:T(8,128)(2,1)S(1)}, bf16[128,256]{1,0:T(8,128)(2,1)}, u32[]{:S(2)}) copy-start(bf16[128,256]{1,0:T(8,128)(2,1)} %refs_7_.1) | copy-start | bytes 196612
  46.6 10.6 %copy-start.3 = (bf16[128,256]{1,0:T(8,128)(2,1)S(1)}, bf16[128,256]{1,0:T(8,128)(2,1)}, u32[]{:S(2)}) copy-start(bf16[128,256]{1,0:T(8,128)(2,1)} %refs_5_.1) | copy-start | bytes 196612
  46.6 10.6 %copy-start.4 = (s32[1,1024]{1,0:T(1,128)S(1)}, s32[1,1024]{1,0:T(1,128)}, u32[]{:S(2)}) copy-start(s32[1,1024]{1,0:T(1,128)} %reshape.27.refs_1_.refs_0_) | copy-start | bytes 12292
  46.6 10.6 %copy-start.5 = (f32[256]{0:T(256)S(1)}, f32[256]{0:T(256)}, u32[]{:S(2)}) copy-start(f32[256]{0:T(256)} %param.13) | copy-start | bytes 3076
  64.0 4.7 %copy-start.6 = (bf16[1024,128]{1,0:T(8,128)(2,1)}, bf16[1024,128]{1,0:T(8,128)(2,1)S(1)}, u32[]{:S(2)}) copy-start(bf16[1024,128]{1,0:T(8,128)(2,1)S(1)} %get-tuple-element.40.refs_1_) | copy-start | bytes 786436
  64.0 18.8 %all-to-all-start.2 = ((bf16[128,16,128]{2,1,0:T(8,128)(2,1)}), bf16[128,16,128]{2,1,0:T(8,128)(2,1)S(1)}, u32[]{:S(2)}, u32[]{:S(2)}) async-start(bf16[128,16,128]{2,1,0:T(8,128)(2,1)} %get-tuple-element.39), calls=%async_computation.2 | async-start | bytes 1048576 | tf_op jit(solution)/shard_map/all_to_all | solution.py:457
  82.8 3.3 %copy-start.1 = (bf16[128,16,128]{2,1,0:T(8,128)(2,1)}, bf16[128,16,128]{2,1,0:T(8,128)(2,1)S(1)}, u32[]{:S(2)}) copy-start(bf16[128,16,128]{2,1,0:T(8,128)(2,1)S(1)} %all-to-all-done.2.refs_0_) | copy-start | bytes 1572868
  86.1 18.2 %all-to-all-start.3 = ((bf16[128,16,128]{2,1,0:T(8,128)(2,1)}), bf16[128,16,128]{2,1,0:T(8,128)(2,1)S(1)}, u32[]{:S(2)}, u32[]{:S(2)}) async-start(bf16[128,16,128]{2,1,0:T(8,128)(2,1)} %back_push.1), calls=%async_computation.3 | async-start | bytes 1048576 | tf_op jit(solution)/shard_map/all_to_all | solution.py:457

commit v4 on v3

--- a/solution.py
+++ b/solution.py
@@ -20,7 +20,7 @@
 COPIES = 6
 TURN = 256
 PARTS = 4
-WORDS = SLOTS * (SLOTS // 512)
+WORDS = SLOTS * (SLOTS // 1024)
 
 
 def part_of(size, k):
@@ -40,20 +40,22 @@
     return jnp.where(places == column, 1.0, 0.0).astype(BF16)
 
 
-def scatter_matrix(line):
-    places = lax.broadcasted_iota(jnp.int32, (MASTERS, MIRRORS), 0)
+def scatter_part(line, c):
+    size = MASTERS // PARTS
+    places = lax.broadcasted_iota(jnp.int32, (size, MIRRORS), 0) + c * size
     return jnp.where(places == line, 1.0, 0.0).astype(BF16)
 
 
-def diagonal(slots):
-    shape = (PEERS, 8, 8)
+def pick(slots, first):
+    shape = (PEERS, 8, slots.shape[1])
     spread = jnp.broadcast_to(slots[:, None, :], shape)
-    here = lax.broadcasted_iota(jnp.int32, shape, 1) == lax.broadcasted_iota(jnp.int32, shape, 2)
+    wanted = first + lax.broadcasted_iota(jnp.int32, shape, 1)
+    here = lax.broadcasted_iota(jnp.int32, shape, 2) == wanted
     return jnp.sum(jnp.where(here, spread, 0.0), axis=2, keepdims=True)
 
 
 def as_column(lists):
-    return diagonal(jnp.transpose(lists.astype(F32))).reshape(MIRRORS, 1).astype(jnp.int32)
+    return pick(jnp.transpose(lists.astype(F32)), 0).reshape(MIRRORS, 1).astype(jnp.int32)
 
 
 def numbers():
@@ -63,31 +65,34 @@
 
 
 def pull_kernel(
-    live_ref, lists_ref, src_ref, dst_ref, rows_ref, out_ref, gather_ref, code_ref, hot_ref, low_ref
+    live_ref, lists_ref, src_ref, dst_ref, rows_ref, out_ref, code_ref, high_ref, low_ref
 ):
-    gather_ref[...] = gather_matrix(as_column(lists_ref[...]))
-    gather_ref.send()
+    gather = gather_matrix(as_column(lists_ref[...]))
     src, dst = src_ref[...], dst_ref[...]
     live = numbers() < live_ref[0]
-    place = ((src >> 7) & 3) * SLOTS + dst
-    code = place | ((src & 127) << 13) | ((src >> 9) << 24)
-    code_ref[...] = jnp.where(live, code, 128 << 13)
+    place = ((src >> 7) & 1) * SLOTS + dst
+    code = place | ((src & 127) << 12) | ((src >> 8) << 22)
+    code_ref[...] = jnp.where(live, code, 128 << 12)
     code_ref.send()
     slot = jnp.where(live, dst - MASTERS, -1)
-    peer, low = slot >> 3, slot & 7
-    peers = lax.broadcasted_iota(jnp.int32, (PEERS, LANES), 0)
-    lows = lax.broadcasted_iota(jnp.int32, (16, LANES), 0)
+    high, low = slot >> 5, slot & 31
+    places = lax.broadcasted_iota(jnp.int32, (32, LANES), 0)
     for k in range(EDGES // LANES):
         at = pl.ds(k * LANES, LANES)
-        hot_ref[:, at] = jnp.where(peers == peer[k : k + 1], 1.0, 0.0).astype(BF16)
-        low_ref[:, at] = jnp.where(lows == low[k : k + 1], 1.0, 0.0).astype(BF16)
-    tally = jnp.broadcast_to(diagonal(dot_nt(hot_ref[...], low_ref[...])[:, :8]), (PEERS, 8, LANES))
+        high_ref[:, at] = jnp.where(places == high[k : k + 1], 1.0, 0.0).astype(BF16)
+        low_ref[:, at] = jnp.where(places == low[k : k + 1], 1.0, 0.0).astype(BF16)
+    counts = dot_nt(high_ref[...], low_ref[...])
+    peer = lax.broadcasted_iota(jnp.int32, (PEERS, 32), 0)
+    of_peer = jnp.where(peer >> 2 == lax.broadcasted_iota(jnp.int32, (PEERS, 32), 1), 1.0, 0.0)
+    counts = sum(dot(of_peer.astype(BF16), part.astype(BF16)) for part in split(counts))
+    peer = lax.broadcasted_iota(jnp.int32, (PEERS, 8, 32), 0)
+    tally = jnp.broadcast_to(pick(counts, (peer & 3) << 3), (PEERS, 8, LANES))
     high, rest = split(tally)
     left = lax.broadcasted_iota(jnp.int32, tally.shape, 2) < LANES // 2
     tally = jnp.where(left, high, rest)
     rows = rows_ref[...]
     for c in range(2):
-        picked = dot(gather_ref[c * 512 : (c + 1) * 512], rows).reshape(PEERS // 2, 8, F)
+        picked = dot(gather[c * 512 : (c + 1) * 512], rows).reshape(PEERS // 2, 8, F)
         half = pl.ds(c * (PEERS // 2), PEERS // 2)
         both = [picked, tally[c * (PEERS // 2) : (c + 1) * (PEERS // 2)]]
         out_ref[half] = jnp.concatenate(both, axis=1).astype(BF16)
@@ -110,7 +115,7 @@
     lax.fori_loop(0, WORDS // 256, clear, 0)
     load.wait()
 
-    lanes = lax.broadcasted_iota(jnp.int32, (1, LANES), 1) << 13
+    lanes = lax.broadcasted_iota(jnp.int32, (1, LANES), 1) << 12
     one = jnp.ones((1, LANES), jnp.int32)
 
     def code_at(k, i):
@@ -126,8 +131,8 @@
             adds = []
             for w in words:
                 w = jnp.full((1, LANES), w, jnp.int32)
-                bit = lax.shift_left(one, lax.shift_right_logical(w, 21))
-                adds.append(jnp.where(lanes == (w & (255 << 13)), bit, 0))
+                bit = lax.shift_left(one, lax.shift_right_logical(w, 20))
+                adds.append(jnp.where(lanes == (w & (255 << 12)), bit, 0))
             olds = [tables3[k][where[k]] for k in range(count)]
             for k in range(count):
                 tables3[k][where[k]] = olds[k] + adds[k]
@@ -137,11 +142,11 @@
     lax.fori_loop(0, turns, turn, 0)
 
     def put(near_ref, far_ref, to, at, read, seen):
-        for j in range(4):
+        for j in range(2):
             words = read(pl.ds(pl.multiple_of(j * SLOTS + at, 128), 128))
             for q, counts in enumerate(words):
-                half = near_ref if q < 2 else far_ref
-                left = (q % 2) * 512 + j * LANES
+                half = near_ref if q < 4 else far_ref
+                left = (q % 4) * 256 + j * LANES
                 half[pl.ds(to, 128), pl.ds(left, LANES)] = counts.astype(F32).astype(BF16)
                 seen = seen + jnp.sum(counts.reshape(16, 8, LANES), axis=0)
         return seen
@@ -150,8 +155,13 @@
 
     def widen(read):
         def mirrors(i, seen):
-            d = pl.multiple_of(i * 128, 128)
-            return put(gm_ref, gg_ref, d, MASTERS + d, read, seen)
+            for h in range(2):
+                d = pl.multiple_of(i * 256 + h * 128, 128)
+                seen = put(gm_ref, gg_ref, d, MASTERS + d, read, seen)
+            e = pl.multiple_of(i * 256, 256)
+            gg_ref.send(pl.ds(e, 256))
+            gm_ref.send(pl.ds(e, 256))
+            return seen
 
         def masters(i, seen):
             e = pl.multiple_of(i * 256, 256)
@@ -163,9 +173,7 @@
             mg_ref.send(pl.ds(e, 256))
             return seen
 
-        seen = lax.fori_loop(0, MIRRORS // 128, mirrors, jnp.zeros((8, LANES), jnp.int32))
-        gg_ref.send()
-        gm_ref.send()
+        seen = lax.fori_loop(0, MIRRORS // 256, mirrors, jnp.zeros((8, LANES), jnp.int32))
         seen = lax.fori_loop(0, MASTERS // 256, masters, seen)
         sums_ref.send()
         return seen
@@ -174,16 +182,16 @@
         for ref in (mm_ref, mg_ref, gm_ref, gg_ref, sums_ref):
             ref.wait()
 
-    def read_bytes(at):
+    def read_fours(at):
         x = tables[0][at, :]
         for t in tables[1:]:
             x = x + t[at, :]
-        yield x & 255
-        yield lax.shift_right_logical(x, 8) & 255
-        yield lax.shift_right_logical(x, 16) & 255
-        yield lax.shift_right_logical(x, 24)
-
-    found = jnp.sum(widen(read_bytes).astype(F32))
+        yield x & 15
+        for q in range(1, 7):
+            yield lax.shift_right_logical(x, 4 * q) & 15
+        yield lax.shift_right_logical(x, 28)
+
+    found = jnp.sum(widen(read_fours).astype(F32))
     finish()
 
     @pl.when(found != n.astype(F32))
@@ -193,21 +201,19 @@
         def edge(e, carry):
             word = codes[e // LANES, e % LANES]
             at = word & (WORDS - 1)
-            q = word >> 24
-            one = jnp.where(
-                lanes == (word & (127 << 13)), jnp.where(q % 2 == 1, 65536, 1), 0
-            )
-            tables3[0][at] = tables3[0][at] + jnp.where(q < 2, one, 0)
-            tables3[1][at] = tables3[1][at] + jnp.where(q < 2, 0, one)
+            q = word >> 22
+            one = jnp.where(lanes == (word & (127 << 12)), jnp.where(q >= 4, 65536, 1), 0)
+            for k in range(4):
+                tables3[k][at] = tables3[k][at] + jnp.where(q % 4 == k, one, 0)
             return carry
 
         lax.fori_loop(0, n, edge, 0)
 
         def read_halves(at):
-            for t in tables[:2]:
-                x = t[at, :]
-                yield x & 65535
-                yield lax.shift_right_logical(x, 16)
+            for t in tables[:4]:
+                yield t[at, :] & 65535
+            for t in tables[:4]:
+                yield lax.shift_right_logical(t[at, :], 16)
 
         widen(read_halves)
         finish()
@@ -221,6 +227,12 @@
 def parts_of(got):
     got = got.astype(F32)
     return got[:, :8].reshape(MIRRORS, F).astype(BF16), got[:, 8:]
+
+
+def two_parts(x):
+    high, low = split(x)
+    left = lax.broadcasted_iota(jnp.int32, x.shape, 1) < LANES // 2
+    return jnp.where(left, high, low).astype(BF16)
 
 
 def push_kernel(got_ref, sums_ref, gg_ref, out_ref):
@@ -233,51 +245,59 @@
 
 
 def local_kernel(
-    got_ref, line_ref, rows_ref, mm_ref, mg_ref, turned_ref, sums_ref, inverse_ref
+    got_ref, rows_ref, mg_ref, mm_ref, turned_ref, told_ref, sums_ref, tally_ref
 ):
+    rows = rows_ref[...]
+    turned_ref[...] = rows.astype(F32).T.astype(BF16)
+    turned_ref.send()
     both = got_ref[...].astype(F32)
     both = [both[:, :8].reshape(MIRRORS, F), both[:, 8:].reshape(MIRRORS, LANES)]
     both = jnp.concatenate(both, axis=1).astype(BF16)
-    got, tally = both[:, :F], both[:, F:]
-    degree = dot(scatter_matrix(line_ref[...]), tally)
-    degree = degree + pltpu.roll(degree, LANES // 2, 1)
-    rows = rows_ref[...]
-    turned_ref[...] = rows.astype(F32).T.astype(BF16)
-    turned_ref.send()
+    told_ref[...] = both[:, F:]
+    told_ref.send()
     ones = jnp.ones((MASTERS, LANES), BF16)
-    both = dot(mm_ref[...], jnp.concatenate([rows, ones], axis=1)) + dot(
-        mg_ref[...], jnp.concatenate([got, ones], axis=1)
-    )
-    sums_ref[...] = both[:, :F]
-    sums_ref.send()
-    inverse_ref[...] = 1.0 / jnp.maximum(both[:, F:] + degree, 1.0)
-    inverse_ref.send()
+    near = jnp.concatenate([rows, ones], axis=1)
+    far = jnp.concatenate([both[:, :F], ones], axis=1)
+    for c in range(PARTS):
+        part = part_of(MASTERS, c)
+        both = dot(mg_ref.part(c), far) + dot(mm_ref.part(c), near)
+        sums_ref[part] = both[:, :F]
+        sums_ref.send(part)
+        tally_ref[part] = two_parts(both[:, F:])
+        tally_ref.send(part)
 
 
 def dense_kernel(
-    got_ref, line_ref, sums_ref, inverse_ref, self_ref, bias_ref, rows_ref, neigh_ref, cot_ref,
-    gather_ref, turned_ref,
-    act_ref, grad_ref, msg_ref, out_ref, total_ref,
+    got_ref, line_ref, told_ref, tally_ref, sums_ref, rows_ref, self_ref, neigh_ref, bias_ref,
+    cot_ref, turned_ref,
+    act_ref, own_ref, msg_ref, out_ref, total_ref,
 ):
-    got = got_ref[...].reshape(MIRRORS, F)
-    w_self, w_neigh, bias, line = self_ref[...], neigh_ref[...], bias_ref[...], line_ref[...]
+    line = line_ref[...]
+    wide = jnp.concatenate([got_ref[...].reshape(MIRRORS, F), told_ref[...]], axis=1)
+    w = jnp.concatenate([self_ref[...], neigh_ref[...]], axis=0)
+    bias = bias_ref[...]
     size = MASTERS // PARTS
-    terms, total = 0.0, 0.0
+    terms, total, picked = 0.0, 0.0, 0.0
     for c in range(PARTS):
         rows = part_of(MASTERS, c)
-        places = lax.broadcasted_iota(jnp.int32, (size, MIRRORS), 0) + c * size
-        scatter = jnp.where(places == line, 1.0, 0.0).astype(BF16)
-        inverse = inverse_ref[rows]
-        mean = (sums_ref[rows] + dot(scatter, got)) * inverse
-        pre = dot(rows_ref[rows], w_self) + dot(mean.astype(BF16), w_neigh) + bias
+        scatter = scatter_part(line, c)
+        folded = dot(scatter, wide)
+        degree = folded[:, F:] + tally_ref[rows].astype(F32)
+        degree = degree + pltpu.roll(degree, LANES // 2, 1)
+        inverse = 1.0 / jnp.maximum(degree, 1.0)
+        mean = (sums_ref[rows] + folded[:, :F]) * inverse
+        pre = dot(jnp.concatenate([rows_ref[rows], mean.astype(BF16)], axis=1), w) + bias
         sig = jax.nn.sigmoid(pre)
         act_ref[rows] = (pre * sig).astype(BF16)
         act_ref.send(rows)
         grad = (cot_ref[rows].astype(F32) * sig * (1.0 + pre * (1.0 - sig))).astype(BF16)
-        grad_ref[rows] = grad
-        grad_ref.send(rows)
-        msg_ref[rows] = (dot_nt(grad, w_neigh) * inverse).astype(BF16)
+        back = dot_nt(grad, w)
+        own_ref[rows] = back[:, :F]
+        own_ref.send(rows)
+        msg = back[:, F:] * inverse
+        msg_ref[rows] = msg.astype(BF16)
         msg_ref.send(rows)
+        picked = picked + dot(msg.T.astype(BF16), scatter)
         turned = [turned_ref[:, c * size : (c + 1) * size], mean.T.astype(BF16)]
         terms = terms + dot(jnp.concatenate(turned, axis=0), grad)
         total = total + dot(jnp.ones((8, size), BF16), grad)
@@ -287,11 +307,10 @@
     even = jnp.where(first, high, pltpu.roll(low, 4, 1))
     odd = jnp.where(first, pltpu.roll(high, 4, 1), low)
     mixed = jnp.stack([even, odd], axis=1).reshape(PEERS, 8, F)
-    msg = msg_ref[...]
     for c in range(PARTS):
         peers, count = part_of(PEERS, c), PEERS // PARTS
-        picked = dot(gather_ref.part(c), msg).reshape(count, 8, F)
-        both = [picked, mixed[c * count : (c + 1) * count]]
+        rows = picked[:, c * 8 * count : (c + 1) * 8 * count].T.reshape(count, 8, F)
+        both = [rows, mixed[c * count : (c + 1) * count]]
         out_ref[peers] = jnp.concatenate(both, axis=1).astype(BF16)
         out_ref.send(peers)
     high, low = split(total)
@@ -304,14 +323,14 @@
 
 
 def back_local_kernel(
-    gg_ref, msg_ref, mg_ref, mm_ref, grad_ref, w_ref, turned_ref, mirror_ref, base_ref
+    gg_ref, msg_ref, mg_ref, mm_ref, own_ref, turned_ref, mirror_ref, base_ref
 ):
     turned_ref[...] = gg_ref[...].T
     turned_ref.send()
     msg = msg_ref[...].astype(F32).T.astype(BF16)
     mirror_ref[...] = dot(msg, mg_ref[...]).T
     mirror_ref.send()
-    base_ref[...] = dot(msg, mm_ref[...]).T + dot_nt(grad_ref[...], w_ref[...])
+    base_ref[...] = dot(msg, mm_ref[...]).T + own_ref[...]
     base_ref.send()
 
 
@@ -338,8 +357,11 @@
 
 def last_kernel(line_ref, got_ref, base_ref, grad_ref, self_ref, neigh_ref, bias_ref):
     rows, tiles = parts_of(got_ref[...])
-    grad_ref[...] = (dot(scatter_matrix(line_ref[...]), rows) + base_ref[...]).astype(BF16)
-    grad_ref.send()
+    line = line_ref[...]
+    for c in range(PARTS):
+        part = part_of(MASTERS, c)
+        grad_ref[part] = (dot(scatter_part(line, c), rows) + base_ref[part]).astype(BF16)
+        grad_ref.send(part)
     pairs = tiles.reshape(PEERS // 2, 2, 8, F)
     first = lax.broadcasted_iota(jnp.int32, (PEERS // 2, 8, F), 1) < 4
     flat = jnp.where(first, pairs[:, 0], pltpu.roll(pairs[:, 1], 4, 1)).reshape(2 * H, F)
@@ -466,13 +488,13 @@
     edges = (EDGES // LANES, LANES)
     src, dst = src_slot.reshape(edges), dst_slot.reshape(edges)
     rows_f32, rows_bf16 = ((1024, F), F32), ((1024, F), BF16)
-    out1, gather, code = call(
+    out1, code = call(
         pull_kernel,
         (edge_live, lists, src, dst, features),
-        [payload, square, (edges, jnp.int32)],
+        [payload, (edges, jnp.int32)],
         "pull",
         scalars=(0,),
-        scratch=[pltpu.VMEM((PEERS, EDGES), BF16), pltpu.VMEM((16, EDGES), BF16)],
+        scratch=[pltpu.VMEM((32, EDGES), BF16), pltpu.VMEM((32, EDGES), BF16)],
     )
     got1 = exchange(out1)
     mm, mg, gm, gg, sums = call(
@@ -497,30 +519,30 @@
         parts={2: PARTS},
     )
     got2 = exchange(out2)
-    turned, sums_m, inverse = call(
+    turned, told, sums_m, tally = call(
         local_kernel,
-        (got1, line, features, mm, mg),
-        [((F, MASTERS), BF16), rows_f32, rows_f32],
+        (got1, features, mg, mm),
+        [((F, MASTERS), BF16), rows_bf16, rows_f32, rows_bf16],
         "local",
+        parts={2: PARTS, 3: PARTS},
         flops=2_000_000_000,
         moved=6_000_000,
     )
-    act, grad, msg, out3, total = call(
+    act, own, msg, out3, total = call(
         dense_kernel,
         (
-            got2, line, sums_m, inverse, w_self, bias.reshape(1, H), features, w_neigh, cotangent,
-            gather, turned,
+            got2, line, told, tally, sums_m, features, w_self, w_neigh, bias.reshape(1, H),
+            cotangent, turned,
         ),
-        [((MASTERS, H), BF16), ((MASTERS, H), BF16), rows_bf16, payload, ((8, F), F32)],
+        [((MASTERS, H), BF16), rows_f32, rows_bf16, payload, ((8, F), F32)],
         "dense",
         near=(0,),
         room=55_800_000,
-        parts={9: PARTS},
     )
     got3 = exchange(out3)
     turned_gg, mirror, base = call(
         back_local_kernel,
-        (gg, msg, mg, mm, grad, w_self),
+        (gg, msg, mg, mm, own),
         [square, rows_f32, rows_f32],
         "back_local",
         flops=2_000_000_000,

time: 107 us -> 105 us (0.981)
  Pallas kernels: 46.5 us -> 41.9 us
  waiting for transfers between devices: 27 us -> 30.8 us
  starting transfers between devices: 31.2 us -> 30.1 us
    pallas_call x9, Pallas kernels: 46.5 us -> 41.9 us  [call(): pl.pallas_call(body, out_shape=[jax.ShapeDtypeStruct(s, t) for s, t in ou...]
    all_to_all x4, waiting for transfers between devices: 27 us -> 30.8 us  [exchange(): return lax.all_to_all(x, AXES, split_axis=0, concat_axis=0, tiled=True)]
    all_to_all x4, starting transfers between devices: 31.2 us -> 30.1 us  [exchange(): return lax.all_to_all(x, AXES, split_axis=0, concat_axis=0, tiled=True)]
  transfers between devices with their start and end apart: 4 -> 4, of which waited for: 4 -> 4; matrix products, arithmetic and copies ran while one was open for 1% -> 0% of each run, Pallas kernels for 24% -> 22%
where the time goes in v4:
time: 105 us
  Pallas kernels  41.9 us (40%)
  waiting for transfers between devices  30.8 us (29%)
  starting transfers between devices  30.1 us (29%)
  between operations  1.61 us (2%)
    pallas_call x9, Pallas kernels, call(): pl.pallas_call(body, out_shape=[jax.ShapeDtypeStruct(s, t) for s, t in ou...  41.9 us
    all_to_all x4, waiting for transfers between devices, exchange(): return lax.all_to_all(x, AXES, split_axis=0, concat_axis=0, tiled=True)  30.8 us
    all_to_all x4, starting transfers between devices, exchange(): return lax.all_to_all(x, AXES, split_axis=0, concat_axis=0, tiled=True)  30.1 us
  transfers between devices with their start and end apart: 4, of which 4 were waited for; matrix products, arithmetic and copies ran while one was open for 0% of the time, Pallas kernels for 22%

profile of v4, /device:TPU:1, one launch (start us, length us, event | category | flops | bytes accessed | tf_op | source)
XLA Modules:
  0.0 104.6 jit_solution(1197569225611958737)
XLA Ops:
  1.3 3.8 %pull.1 = (bf16[128,16,128]{2,1,0:T(8,128)(2,1)}, s32[64,128]{1,0:T(8,128)}) custom-call(s32[1]{0:T(128)S(6)} %copy.16.refs_0_, s32[8,128]{1,0:T(8,128)} %bitcast.10, s32[64,128]{1,0:T(8,128)} %bitcast.8, s32[64,128]{1,0:T(8,128)} %bitcast.9, bf16[1024,128]{1,0:T(8,128)(2,1)} %refs_5_.1), custom_call_target="tpu_custom_call" | custom-call | tf_op jit(solution)/shard_map/pull/pallas_call | solution.py:466
  5.1 11.5 %all-to-all-start = ((bf16[128,16,128]{2,1,0:T(8,128)(2,1)}), bf16[128,16,128]{2,1,0:T(8,128)(2,1)S(1)}, u32[]{:S(2)}, u32[]{:S(2)}) async-start(bf16[128,16,128]{2,1,0:T(8,128)(2,1)} %get-tuple-element.28), calls=%async_computation | async-start | bytes 1048576 | tf_op jit(solution)/shard_map/all_to_all | solution.py:479
  16.6 9.4 %build.1 = (bf16[1024,1024]{1,0:T(8,128)(2,1)}, bf16[1024,1024]{1,0:T(8,128)(2,1)}, bf16[1024,1024]{1,0:T(8,128)(2,1)}, bf16[1024,1024]{1,0:T(8,128)(2,1)}, f32[1024,128]{1,0:T(8,128)}) custom-call(s32[1]{0:T(128)S(6)} %copy.16.refs_0_, s32[64,128]{1,0:T(8,128)} %get-tuple-element.29.refs_1_, bf16[1024,128]{1,0:T(8,128)(2,1)} %refs_5_.1), custom_call_target="tpu_custom_call" | custom-call | flops 20000000000 | bytes 20000000 | tf_op jit(solution)/shard_map/build/pallas_call | solution.py:466
  26.1 0.0 copy-start.6
  26.1 4.6 %all-to-all-done.refs_0_ = bf16[128,16,128]{2,1,0:T(8,128)(2,1)S(1)} async-done(((bf16[128,16,128]{2,1,0:T(8,128)(2,1)}), bf16[128,16,128]{2,1,0:T(8,128)(2,1)S(1)}, u32[]{:S(2)}, u32[]{:S(2)}) %all-to-all-start) | async-done | bytes 524320 | tf_op jit(solution)/shard_map/all_to_all | solution.py:479
  30.7 0.0 copy-start
  30.7 3.2 %push.1 = bf16[128,8,128]{2,1,0:T(8,128)(2,1)} custom-call(bf16[128,16,128]{2,1,0:T(8,128)(2,1)S(1)} %all-to-all-done.refs_0_, f32[1024,128]{1,0:T(8,128)} %get-tuple-element.30.refs_1_, bf16[1024,1024]{1,0:T(8,128)(2,1)} %get-tuple-element.31.refs_2_.refs_0_), custom_call_target="tpu_custom_call" | custom-call | tf_op jit(solution)/shard_map/push/pallas_call | solution.py:466
  33.9 10.3 %all-to-all-start.1 = ((bf16[128,8,128]{2,1,0:T(8,128)(2,1)}), bf16[128,8,128]{2,1,0:T(8,128)(2,1)S(1)}, u32[]{:S(2)}, u32[]{:S(2)}) async-start(bf16[128,8,128]{2,1,0:T(8,128)(2,1)} %push.1), calls=%async_computation.1 | async-start | bytes 524288 | tf_op jit(solution)/shard_map/all_to_all | solution.py:479
  44.2 0.0 copy-done.6
  44.3 0.1 copy.15
  44.4 0.1 reshape.27.refs_1_.refs_0_
  44.5 0.0 copy-done
  44.5 0.0 copy-start.2
  44.5 0.0 copy-start.3
  44.5 0.0 copy-start.4
  44.5 5.7 %local.1 = (bf16[128,1024]{1,0:T(8,128)(2,1)}, bf16[1024,128]{1,0:T(8,128)(2,1)}, f32[1024,128]{1,0:T(8,128)}, bf16[1024,128]{1,0:T(8,128)(2,1)}) custom-call(bf16[128,16,128]{2,1,0:T(8,128)(2,1)} %copy-done, bf16[1024,128]{1,0:T(8,128)(2,1)} %refs_5_.1, bf16[1024,1024]{1,0:T(8,128)(2,1)} %get-tuple-element.32.refs_2_, ...), custom_call_target="tpu_custom_call" | custom-call | flops 2000000000 | bytes 6000000 | tf_op jit(solution)/shard_map/local/pallas_call | solution.py:466
  50.2 5.5 %all-to-all-done.1.refs_0_ = bf16[128,8,128]{2,1,0:T(8,128)(2,1)S(1)} async-done(((bf16[128,8,128]{2,1,0:T(8,128)(2,1)}), bf16[128,8,128]{2,1,0:T(8,128)(2,1)S(1)}, u32[]{:S(2)}, u32[]{:S(2)}) %all-to-all-start.1) | async-done | bytes 262176 | tf_op jit(solution)/shard_map/all_to_all | solution.py:479
  55.7 0.0 copy-done.2
  55.7 0.0 copy-done.3
  55.7 0.0 copy-done.4
  55.7 6.4 %dense.1 = (bf16[1024,256]{1,0:T(8,128)(2,1)}, f32[1024,128]{1,0:T(8,128)}, bf16[1024,128]{1,0:T(8,128)(2,1)S(1)}, bf16[128,16,128]{2,1,0:T(8,128)(2,1)}, f32[8,128]{1,0:T(8,128)S(1)}) custom-call(bf16[128,8,128]{2,1,0:T(8,128)(2,1)S(1)} %all-to-all-done.1.refs_0_, s32[1,1024]{1,0:T(1,128)S(1)} %reshape.27.refs_1_.refs_0_, ...), custom_call_target="tpu_custom_call" | custom-call | tf_op jit(solution)/shard_map/dense/pallas_call | solution.py:466
  62.1 0.0 copy-start.5
  62.1 4.3 %all-to-all-start.2 = ((bf16[128,16,128]{2,1,0:T(8,128)(2,1)}), bf16[128,16,128]{2,1,0:T(8,128)(2,1)S(1)}, u32[]{:S(2)}, u32[]{:S(2)}) async-start(bf16[128,16,128]{2,1,0:T(8,128)(2,1)} %get-tuple-element.39), calls=%async_computation.2 | async-start | bytes 1048576 | tf_op jit(solution)/shard_map/all_to_all | solution.py:479
  66.4 0.0 copy-done.5
  66.4 4.4 %back_local.1 = (bf16[1024,1024]{1,0:T(8,128)(2,1)}, f32[1024,128]{1,0:T(8,128)}, f32[1024,128]{1,0:T(8,128)}) custom-call(bf16[1024,1024]{1,0:T(8,128)(2,1)} %get-tuple-element.31.refs_2_.refs_0_, bf16[1024,128]{1,0:T(8,128)(2,1)} %copy-done.5, bf16[1024,1024]{1,0:T(8,128)(2,1)} %get-tuple-element.32.refs_2_, bf16[1024,1024]{1,0:T(8,128)(2,1)} %get-tuple-element.33.refs_3_, ...), custom_call_target="tpu_custom_call" | custom-call | flops 2000000000 | bytes 6000000 | tf_op jit(solution)/shard_map/back_local/pallas_call | solution.py:466
  70.8 9.7 %all-to-all-done.2.refs_0_ = bf16[128,16,128]{2,1,0:T(8,128)(2,1)S(1)} async-done(((bf16[128,16,128]{2,1,0:T(8,128)(2,1)}), bf16[128,16,128]{2,1,0:T(8,128)(2,1)S(1)}, u32[]{:S(2)}, u32[]{:S(2)}) %all-to-all-start.2) | async-done | bytes 524320 | tf_op jit(solution)/shard_map/all_to_all | solution.py:479
  80.5 0.0 copy-start.1
  80.5 3.3 %back_push.1 = bf16[128,16,128]{2,1,0:T(8,128)(2,1)} custom-call(bf16[128,16,128]{2,1,0:T(8,128)(2,1)S(1)} %all-to-all-done.2.refs_0_, f32[1024,128]{1,0:T(8,128)} %get-tuple-element.42.refs_1_, f32[8,128]{1,0:T(8,128)S(1)} %get-tuple-element.43.refs_2_, bf16[1024,1024]{1,0:T(8,128)(2,1)} %get-tuple-element.44.refs_3_), custom_call_target="tpu_custom_call" | custom-call | tf_op jit(solution)/shard_map/back_push/pallas_call | solution.py:466
  83.8 0.0 copy-done.1
  83.8 4.0 %all-to-all-start.3 = ((bf16[128,16,128]{2,1,0:T(8,128)(2,1)}), bf16[128,16,128]{2,1,0:T(8,128)(2,1)S(1)}, u32[]{:S(2)}, u32[]{:S(2)}) async-start(bf16[128,16,128]{2,1,0:T(8,128)(2,1)} %back_push.1), calls=%async_computation.3 | async-start | bytes 1048576 | tf_op jit(solution)/shard_map/all_to_all | solution.py:479
  87.8 3.2 %back_mirror.1.refs_2_ = f32[1024,128]{1,0:T(8,128)} custom-call(bf16[128,16,128]{2,1,0:T(8,128)(2,1)} %copy-done.1, bf16[1024,1024]{1,0:T(8,128)(2,1)} %get-tuple-element.45.refs_1_, f32[1024,128]{1,0:T(8,128)} %get-tuple-element.46.refs_2_), custom_call_target="tpu_custom_call" | custom-call | flops 2000000000 | bytes 6000000 | tf_op jit(solution)/shard_map/back_mirror/pallas_call | solution.py:466
  91.0 11.0 %all-to-all-done.3.refs_1_ = bf16[128,16,128]{2,1,0:T(8,128)(2,1)S(1)} async-done(((bf16[128,16,128]{2,1,0:T(8,128)(2,1)}), bf16[128,16,128]{2,1,0:T(8,128)(2,1)S(1)}, u32[]{:S(2)}, u32[]{:S(2)}) %all-to-all-start.3) | async-done | bytes 524320 | tf_op jit(solution)/shard_map/all_to_all | solution.py:479
  102.0 2.5 %last.1 = (bf16[1024,128]{1,0:T(8,128)(2,1)}, f32[128,256]{1,0:T(8,128)}, f32[128,256]{1,0:T(8,128)}, f32[2,128]{1,0:T(2,128)}) custom-call(s32[1,1024]{1,0:T(1,128)S(1)} %reshape.27.refs_1_.refs_0_, bf16[128,16,128]{2,1,0:T(8,128)(2,1)S(1)} %all-to-all-done.3.refs_1_, f32[1024,128]{1,0:T(8,128)} %back_mirror.1.refs_2_), custom_call_target="tpu_custom_call" | custom-call | tf_op jit(solution)/shard_map/last/pallas_call | solution.py:466
Async XLA Ops:
  5.1 25.6 %all-to-all-start = ((bf16[128,16,128]{2,1,0:T(8,128)(2,1)}), bf16[128,16,128]{2,1,0:T(8,128)(2,1)S(1)}, u32[]{:S(2)}, u32[]{:S(2)}) async-start(bf16[128,16,128]{2,1,0:T(8,128)(2,1)} %get-tuple-element.28), calls=%async_computation | async-start | bytes 1048576 | tf_op jit(solution)/shard_map/all_to_all | solution.py:479
  26.1 18.2 %copy-start.6 = (s32[1,128,8]{1,2,0:T(8,128)S(1)}, s32[1,128,8]{1,2,0:T(8,128)}, u32[]{:S(2)}) copy-start(s32[1,128,8]{1,2,0:T(8,128)} %param.17) | copy-start | bytes 12292
  30.7 13.8 %copy-start = (bf16[128,16,128]{2,1,0:T(8,128)(2,1)}, bf16[128,16,128]{2,1,0:T(8,128)(2,1)S(1)}, u32[]{:S(2)}) copy-start(bf16[128,16,128]{2,1,0:T(8,128)(2,1)S(1)} %all-to-all-done.refs_0_) | copy-start | bytes 1572868
  33.9 21.8 %all-to-all-start.1 = ((bf16[128,8,128]{2,1,0:T(8,128)(2,1)}), bf16[128,8,128]{2,1,0:T(8,128)(2,1)S(1)}, u32[]{:S(2)}, u32[]{:S(2)}) async-start(bf16[128,8,128]{2,1,0:T(8,128)(2,1)} %push.1), calls=%async_computation.1 | async-start | bytes 524288 | tf_op jit(solution)/shard_map/all_to_all | solution.py:479
  44.5 11.2 %copy-start.2 = (bf16[128,256]{1,0:T(8,128)(2,1)S(1)}, bf16[128,256]{1,0:T(8,128)(2,1)}, u32[]{:S(2)}) copy-start(bf16[128,256]{1,0:T(8,128)(2,1)} %refs_6_.1) | copy-start | bytes 196612
  44.5 11.2 %copy-start.3 = (bf16[128,256]{1,0:T(8,128)(2,1)S(1)}, bf16[128,256]{1,0:T(8,128)(2,1)}, u32[]{:S(2)}) copy-start(bf16[128,256]{1,0:T(8,128)(2,1)} %refs_7_.1) | copy-start | bytes 196612
  44.5 11.2 %copy-start.4 = (f32[256]{0:T(256)S(1)}, f32[256]{0:T(256)}, u32[]{:S(2)}) copy-start(f32[256]{0:T(256)} %param.13) | copy-start | bytes 3076
  62.1 4.3 %copy-start.5 = (bf16[1024,128]{1,0:T(8,128)(2,1)}, bf16[1024,128]{1,0:T(8,128)(2,1)S(1)}, u32[]{:S(2)}) copy-start(bf16[1024,128]{1,0:T(8,128)(2,1)S(1)} %get-tuple-element.40.refs_1_) | copy-start | bytes 786436
  62.1 18.4 %all-to-all-start.2 = ((bf16[128,16,128]{2,1,0:T(8,128)(2,1)}), bf16[128,16,128]{2,1,0:T(8,128)(2,1)S(1)}, u32[]{:S(2)}, u32[]{:S(2)}) async-start(bf16[128,16,128]{2,1,0:T(8,128)(2,1)} %get-tuple-element.39), calls=%async_computation.2 | async-start | bytes 1048576 | tf_op jit(solution)/shard_map/all_to_all | solution.py:479
  80.5 3.3 %copy-start.1 = (bf16[128,16,128]{2,1,0:T(8,128)(2,1)}, bf16[128,16,128]{2,1,0:T(8,128)(2,1)S(1)}, u32[]{:S(2)}) copy-start(bf16[128,16,128]{2,1,0:T(8,128)(2,1)S(1)} %all-to-all-done.2.refs_0_) | copy-start | bytes 1572868
  83.8 18.2 %all-to-all-start.3 = ((bf16[128,16,128]{2,1,0:T(8,128)(2,1)}), bf16[128,16,128]{2,1,0:T(8,128)(2,1)S(1)}, u32[]{:S(2)}, u32[]{:S(2)}) async-start(bf16[128,16,128]{2,1,0:T(8,128)(2,1)} %back_push.1), calls=%async_computation.3 | async-start | bytes 1048576 | tf_op jit(solution)/shard_map/all_to_all | solution.py:479

commit v5 on v4

--- a/solution.py
+++ b/solution.py
@@ -23,8 +23,8 @@
 WORDS = SLOTS * (SLOTS // 1024)
 
 
-def part_of(size, k):
-    return pl.ds(k * (size // PARTS), size // PARTS)
+def part_of(size, k, parts=PARTS):
+    return pl.ds(k * (size // parts), size // parts)
 
 
 def dot(a, b):
@@ -40,8 +40,8 @@
     return jnp.where(places == column, 1.0, 0.0).astype(BF16)
 
 
-def scatter_part(line, c):
-    size = MASTERS // PARTS
+def scatter_part(line, c, parts=PARTS):
+    size = MASTERS // parts
     places = lax.broadcasted_iota(jnp.int32, (size, MIRRORS), 0) + c * size
     return jnp.where(places == line, 1.0, 0.0).astype(BF16)
 
@@ -258,13 +258,11 @@
     ones = jnp.ones((MASTERS, LANES), BF16)
     near = jnp.concatenate([rows, ones], axis=1)
     far = jnp.concatenate([both[:, :F], ones], axis=1)
-    for c in range(PARTS):
-        part = part_of(MASTERS, c)
-        both = dot(mg_ref.part(c), far) + dot(mm_ref.part(c), near)
-        sums_ref[part] = both[:, :F]
-        sums_ref.send(part)
-        tally_ref[part] = two_parts(both[:, F:])
-        tally_ref.send(part)
+    both = dot(mg_ref[...], far) + dot(mm_ref[...], near)
+    sums_ref[...] = both[:, :F]
+    sums_ref.send()
+    tally_ref[...] = two_parts(both[:, F:])
+    tally_ref.send()
 
 
 def dense_kernel(
@@ -276,12 +274,12 @@
     wide = jnp.concatenate([got_ref[...].reshape(MIRRORS, F), told_ref[...]], axis=1)
     w = jnp.concatenate([self_ref[...], neigh_ref[...]], axis=0)
     bias = bias_ref[...]
-    size = MASTERS // PARTS
+    size = MASTERS // 2
+    scatters = [scatter_part(line, c, 2) for c in range(2)]
+    folds = [dot(scatter, wide) for scatter in scatters]
     terms, total, picked = 0.0, 0.0, 0.0
-    for c in range(PARTS):
-        rows = part_of(MASTERS, c)
-        scatter = scatter_part(line, c)
-        folded = dot(scatter, wide)
+    for c in range(2):
+        rows, scatter, folded = part_of(MASTERS, c, 2), scatters[c], folds[c]
         degree = folded[:, F:] + tally_ref[rows].astype(F32)
         degree = degree + pltpu.roll(degree, LANES // 2, 1)
         inverse = 1.0 / jnp.maximum(degree, 1.0)
@@ -289,14 +287,13 @@
         pre = dot(jnp.concatenate([rows_ref[rows], mean.astype(BF16)], axis=1), w) + bias
         sig = jax.nn.sigmoid(pre)
         act_ref[rows] = (pre * sig).astype(BF16)
-        act_ref.send(rows)
         grad = (cot_ref[rows].astype(F32) * sig * (1.0 + pre * (1.0 - sig))).astype(BF16)
         back = dot_nt(grad, w)
         own_ref[rows] = back[:, :F]
-        own_ref.send(rows)
         msg = back[:, F:] * inverse
         msg_ref[rows] = msg.astype(BF16)
-        msg_ref.send(rows)
+        for ref in (act_ref, own_ref, msg_ref):
+            ref.send(rows)
         picked = picked + dot(msg.T.astype(BF16), scatter)
         turned = [turned_ref[:, c * size : (c + 1) * size], mean.T.astype(BF16)]
         terms = terms + dot(jnp.concatenate(turned, axis=0), grad)
@@ -307,8 +304,8 @@
     even = jnp.where(first, high, pltpu.roll(low, 4, 1))
     odd = jnp.where(first, pltpu.roll(high, 4, 1), low)
     mixed = jnp.stack([even, odd], axis=1).reshape(PEERS, 8, F)
-    for c in range(PARTS):
-        peers, count = part_of(PEERS, c), PEERS // PARTS
+    for c in range(2):
+        peers, count = part_of(PEERS, c, 2), PEERS // 2
         rows = picked[:, c * 8 * count : (c + 1) * 8 * count].T.reshape(count, 8, F)
         both = [rows, mixed[c * count : (c + 1) * count]]
         out_ref[peers] = jnp.concatenate(both, axis=1).astype(BF16)
@@ -524,7 +521,6 @@
         (got1, features, mg, mm),
         [((F, MASTERS), BF16), rows_bf16, rows_f32, rows_bf16],
         "local",
-        parts={2: PARTS, 3: PARTS},
         flops=2_000_000_000,
         moved=6_000_000,
     )

time: 105 us -> 104 us (level)
  no operation moved by 1% of the time
where the time goes in v5:
time: 104 us
  Pallas kernels  41 us (39%)
  waiting for transfers between devices  30.7 us (30%)
  starting transfers between devices  30.1 us (29%)
  between operations  1.61 us (2%)
    pallas_call x9, Pallas kernels, call(): pl.pallas_call(body, out_shape=[jax.ShapeDtypeStruct(s, t) for s, t in ou...  41 us
    all_to_all x4, waiting for transfers between devices, exchange(): return lax.all_to_all(x, AXES, split_axis=0, concat_axis=0, tiled=True)  30.7 us
    all_to_all x4, starting transfers between devices, exchange(): return lax.all_to_all(x, AXES, split_axis=0, concat_axis=0, tiled=True)  30.1 us
  transfers between devices with their start and end apart: 4, of which 4 were waited for; matrix products, arithmetic and copies ran while one was open for 0% of the time, Pallas kernels for 22%

profile of v5, /device:TPU:1, one launch (start us, length us, event | category | flops | bytes accessed | tf_op | source)
XLA Modules:
  0.0 103.6 jit_solution(5298319425289485647)
XLA Ops:
  1.3 3.8 %pull.1 = (bf16[128,16,128]{2,1,0:T(8,128)(2,1)}, s32[64,128]{1,0:T(8,128)}) custom-call(s32[1]{0:T(128)S(6)} %copy.16.refs_0_, s32[8,128]{1,0:T(8,128)} %bitcast.10, s32[64,128]{1,0:T(8,128)} %bitcast.8, s32[64,128]{1,0:T(8,128)} %bitcast.9, bf16[1024,128]{1,0:T(8,128)(2,1)} %refs_5_.1), custom_call_target="tpu_custom_call" | custom-call | tf_op jit(solution)/shard_map/pull/pallas_call | solution.py:463
  5.1 11.5 %all-to-all-start = ((bf16[128,16,128]{2,1,0:T(8,128)(2,1)}), bf16[128,16,128]{2,1,0:T(8,128)(2,1)S(1)}, u32[]{:S(2)}, u32[]{:S(2)}) async-start(bf16[128,16,128]{2,1,0:T(8,128)(2,1)} %get-tuple-element.28), calls=%async_computation | async-start | bytes 1048576 | tf_op jit(solution)/shard_map/all_to_all | solution.py:476
  16.6 10.4 %build.1 = (bf16[1024,1024]{1,0:T(8,128)(2,1)}, bf16[1024,1024]{1,0:T(8,128)(2,1)}, bf16[1024,1024]{1,0:T(8,128)(2,1)}, bf16[1024,1024]{1,0:T(8,128)(2,1)}, f32[1024,128]{1,0:T(8,128)}) custom-call(s32[1]{0:T(128)S(6)} %copy.16.refs_0_, s32[64,128]{1,0:T(8,128)} %get-tuple-element.29.refs_1_, bf16[1024,128]{1,0:T(8,128)(2,1)} %refs_5_.1), custom_call_target="tpu_custom_call" | custom-call | flops 20000000000 | bytes 20000000 | tf_op jit(solution)/shard_map/build/pallas_call | solution.py:463
  27.0 0.0 copy-start.6
  27.0 3.7 %all-to-all-done.refs_0_ = bf16[128,16,128]{2,1,0:T(8,128)(2,1)S(1)} async-done(((bf16[128,16,128]{2,1,0:T(8,128)(2,1)}), bf16[128,16,128]{2,1,0:T(8,128)(2,1)S(1)}, u32[]{:S(2)}, u32[]{:S(2)}) %all-to-all-start) | async-done | bytes 524320 | tf_op jit(solution)/shard_map/all_to_all | solution.py:476
  30.7 0.0 copy-start
  30.7 3.2 %push.1 = bf16[128,8,128]{2,1,0:T(8,128)(2,1)} custom-call(bf16[128,16,128]{2,1,0:T(8,128)(2,1)S(1)} %all-to-all-done.refs_0_, f32[1024,128]{1,0:T(8,128)} %get-tuple-element.30.refs_1_, bf16[1024,1024]{1,0:T(8,128)(2,1)} %get-tuple-element.31.refs_2_.refs_0_), custom_call_target="tpu_custom_call" | custom-call | tf_op jit(solution)/shard_map/push/pallas_call | solution.py:463
  33.9 10.5 %all-to-all-start.1 = ((bf16[128,8,128]{2,1,0:T(8,128)(2,1)}), bf16[128,8,128]{2,1,0:T(8,128)(2,1)S(1)}, u32[]{:S(2)}, u32[]{:S(2)}) async-start(bf16[128,8,128]{2,1,0:T(8,128)(2,1)} %push.1), calls=%async_computation.1 | async-start | bytes 524288 | tf_op jit(solution)/shard_map/all_to_all | solution.py:476
  44.5 0.0 copy-done.6
  44.5 0.1 copy.15
  44.6 0.1 reshape.27.refs_1_.refs_0_
  44.7 0.0 copy-done
  44.7 0.0 copy-start.2
  44.7 0.0 copy-start.3
  44.7 0.0 copy-start.4
  44.7 4.9 %local.1 = (bf16[128,1024]{1,0:T(8,128)(2,1)}, bf16[1024,128]{1,0:T(8,128)(2,1)}, f32[1024,128]{1,0:T(8,128)}, bf16[1024,128]{1,0:T(8,128)(2,1)}) custom-call(bf16[128,16,128]{2,1,0:T(8,128)(2,1)} %copy-done, bf16[1024,128]{1,0:T(8,128)(2,1)} %refs_5_.1, bf16[1024,1024]{1,0:T(8,128)(2,1)} %get-tuple-element.32.refs_2_, ...), custom_call_target="tpu_custom_call" | custom-call | flops 2000000000 | bytes 6000000 | tf_op jit(solution)/shard_map/local/pallas_call | solution.py:463
  49.7 6.2 %all-to-all-done.1.refs_0_ = bf16[128,8,128]{2,1,0:T(8,128)(2,1)S(1)} async-done(((bf16[128,8,128]{2,1,0:T(8,128)(2,1)}), bf16[128,8,128]{2,1,0:T(8,128)(2,1)S(1)}, u32[]{:S(2)}, u32[]{:S(2)}) %all-to-all-start.1) | async-done | bytes 262176 | tf_op jit(solution)/shard_map/all_to_all | solution.py:476
  55.9 0.0 copy-done.2
  55.9 0.0 copy-done.3
  55.9 0.0 copy-done.4
  56.0 5.3 %dense.1 = (bf16[1024,256]{1,0:T(8,128)(2,1)}, f32[1024,128]{1,0:T(8,128)}, bf16[1024,128]{1,0:T(8,128)(2,1)S(1)}, bf16[128,16,128]{2,1,0:T(8,128)(2,1)}, f32[8,128]{1,0:T(8,128)S(1)}) custom-call(bf16[128,8,128]{2,1,0:T(8,128)(2,1)S(1)} %all-to-all-done.1.refs_0_, s32[1,1024]{1,0:T(1,128)S(1)} %reshape.27.refs_1_.refs_0_, ...), custom_call_target="tpu_custom_call" | custom-call | tf_op jit(solution)/shard_map/dense/pallas_call | solution.py:463
  61.2 0.0 copy-start.5
  61.3 4.0 %all-to-all-start.2 = ((bf16[128,16,128]{2,1,0:T(8,128)(2,1)}), bf16[128,16,128]{2,1,0:T(8,128)(2,1)S(1)}, u32[]{:S(2)}, u32[]{:S(2)}) async-start(bf16[128,16,128]{2,1,0:T(8,128)(2,1)} %get-tuple-element.39), calls=%async_computation.2 | async-start | bytes 1048576 | tf_op jit(solution)/shard_map/all_to_all | solution.py:476
  65.3 0.0 copy-done.5
  65.3 4.4 %back_local.1 = (bf16[1024,1024]{1,0:T(8,128)(2,1)}, f32[1024,128]{1,0:T(8,128)}, f32[1024,128]{1,0:T(8,128)}) custom-call(bf16[1024,1024]{1,0:T(8,128)(2,1)} %get-tuple-element.31.refs_2_.refs_0_, bf16[1024,128]{1,0:T(8,128)(2,1)} %copy-done.5, bf16[1024,1024]{1,0:T(8,128)(2,1)} %get-tuple-element.32.refs_2_, bf16[1024,1024]{1,0:T(8,128)(2,1)} %get-tuple-element.33.refs_3_, ...), custom_call_target="tpu_custom_call" | custom-call | flops 2000000000 | bytes 6000000 | tf_op jit(solution)/shard_map/back_local/pallas_call | solution.py:463
  69.7 9.7 %all-to-all-done.2.refs_0_ = bf16[128,16,128]{2,1,0:T(8,128)(2,1)S(1)} async-done(((bf16[128,16,128]{2,1,0:T(8,128)(2,1)}), bf16[128,16,128]{2,1,0:T(8,128)(2,1)S(1)}, u32[]{:S(2)}, u32[]{:S(2)}) %all-to-all-start.2) | async-done | bytes 524320 | tf_op jit(solution)/shard_map/all_to_all | solution.py:476
  79.4 0.0 copy-start.1
  79.4 3.3 %back_push.1 = bf16[128,16,128]{2,1,0:T(8,128)(2,1)} custom-call(bf16[128,16,128]{2,1,0:T(8,128)(2,1)S(1)} %all-to-all-done.2.refs_0_, f32[1024,128]{1,0:T(8,128)} %get-tuple-element.42.refs_1_, f32[8,128]{1,0:T(8,128)S(1)} %get-tuple-element.43.refs_2_, bf16[1024,1024]{1,0:T(8,128)(2,1)} %get-tuple-element.44.refs_3_), custom_call_target="tpu_custom_call" | custom-call | tf_op jit(solution)/shard_map/back_push/pallas_call | solution.py:463
  82.7 0.0 copy-done.1
  82.7 4.0 %all-to-all-start.3 = ((bf16[128,16,128]{2,1,0:T(8,128)(2,1)}), bf16[128,16,128]{2,1,0:T(8,128)(2,1)S(1)}, u32[]{:S(2)}, u32[]{:S(2)}) async-start(bf16[128,16,128]{2,1,0:T(8,128)(2,1)} %back_push.1), calls=%async_computation.3 | async-start | bytes 1048576 | tf_op jit(solution)/shard_map/all_to_all | solution.py:476
  86.7 3.2 %back_mirror.1.refs_2_ = f32[1024,128]{1,0:T(8,128)} custom-call(bf16[128,16,128]{2,1,0:T(8,128)(2,1)} %copy-done.1, bf16[1024,1024]{1,0:T(8,128)(2,1)} %get-tuple-element.45.refs_1_, f32[1024,128]{1,0:T(8,128)} %get-tuple-element.46.refs_2_), custom_call_target="tpu_custom_call" | custom-call | flops 2000000000 | bytes 6000000 | tf_op jit(solution)/shard_map/back_mirror/pallas_call | solution.py:463
  89.9 11.0 %all-to-all-done.3.refs_1_ = bf16[128,16,128]{2,1,0:T(8,128)(2,1)S(1)} async-done(((bf16[128,16,128]{2,1,0:T(8,128)(2,1)}), bf16[128,16,128]{2,1,0:T(8,128)(2,1)S(1)}, u32[]{:S(2)}, u32[]{:S(2)}) %all-to-all-start.3) | async-done | bytes 524320 | tf_op jit(solution)/shard_map/all_to_all | solution.py:476
  100.9 2.5 %last.1 = (bf16[1024,128]{1,0:T(8,128)(2,1)}, f32[128,256]{1,0:T(8,128)}, f32[128,256]{1,0:T(8,128)}, f32[2,128]{1,0:T(2,128)}) custom-call(s32[1,1024]{1,0:T(1,128)S(1)} %reshape.27.refs_1_.refs_0_, bf16[128,16,128]{2,1,0:T(8,128)(2,1)S(1)} %all-to-all-done.3.refs_1_, f32[1024,128]{1,0:T(8,128)} %back_mirror.1.refs_2_), custom_call_target="tpu_custom_call" | custom-call | tf_op jit(solution)/shard_map/last/pallas_call | solution.py:463
Async XLA Ops:
  5.1 25.6 %all-to-all-start = ((bf16[128,16,128]{2,1,0:T(8,128)(2,1)}), bf16[128,16,128]{2,1,0:T(8,128)(2,1)S(1)}, u32[]{:S(2)}, u32[]{:S(2)}) async-start(bf16[128,16,128]{2,1,0:T(8,128)(2,1)} %get-tuple-element.28), calls=%async_computation | async-start | bytes 1048576 | tf_op jit(solution)/shard_map/all_to_all | solution.py:476
  27.0 17.5 %copy-start.6 = (s32[1,128,8]{1,2,0:T(8,128)S(1)}, s32[1,128,8]{1,2,0:T(8,128)}, u32[]{:S(2)}) copy-start(s32[1,128,8]{1,2,0:T(8,128)} %param.17) | copy-start | bytes 12292
  30.7 14.0 %copy-start = (bf16[128,16,128]{2,1,0:T(8,128)(2,1)}, bf16[128,16,128]{2,1,0:T(8,128)(2,1)S(1)}, u32[]{:S(2)}) copy-start(bf16[128,16,128]{2,1,0:T(8,128)(2,1)S(1)} %all-to-all-done.refs_0_) | copy-start | bytes 1572868
  33.9 22.0 %all-to-all-start.1 = ((bf16[128,8,128]{2,1,0:T(8,128)(2,1)}), bf16[128,8,128]{2,1,0:T(8,128)(2,1)S(1)}, u32[]{:S(2)}, u32[]{:S(2)}) async-start(bf16[128,8,128]{2,1,0:T(8,128)(2,1)} %push.1), calls=%async_computation.1 | async-start | bytes 524288 | tf_op jit(solution)/shard_map/all_to_all | solution.py:476
  44.7 11.2 %copy-start.2 = (bf16[128,256]{1,0:T(8,128)(2,1)S(1)}, bf16[128,256]{1,0:T(8,128)(2,1)}, u32[]{:S(2)}) copy-start(bf16[128,256]{1,0:T(8,128)(2,1)} %refs_6_.1) | copy-start | bytes 196612
  44.7 11.2 %copy-start.3 = (bf16[128,256]{1,0:T(8,128)(2,1)S(1)}, bf16[128,256]{1,0:T(8,128)(2,1)}, u32[]{:S(2)}) copy-start(bf16[128,256]{1,0:T(8,128)(2,1)} %refs_7_.1) | copy-start | bytes 196612
  44.7 11.2 %copy-start.4 = (f32[256]{0:T(256)S(1)}, f32[256]{0:T(256)}, u32[]{:S(2)}) copy-start(f32[256]{0:T(256)} %param.13) | copy-start | bytes 3076
  61.2 4.0 %copy-start.5 = (bf16[1024,128]{1,0:T(8,128)(2,1)}, bf16[1024,128]{1,0:T(8,128)(2,1)S(1)}, u32[]{:S(2)}) copy-start(bf16[1024,128]{1,0:T(8,128)(2,1)S(1)} %get-tuple-element.40.refs_1_) | copy-start | bytes 786436
  61.3 18.2 %all-to-all-start.2 = ((bf16[128,16,128]{2,1,0:T(8,128)(2,1)}), bf16[128,16,128]{2,1,0:T(8,128)(2,1)S(1)}, u32[]{:S(2)}, u32[]{:S(2)}) async-start(bf16[128,16,128]{2,1,0:T(8,128)(2,1)} %get-tuple-element.39), calls=%async_computation.2 | async-start | bytes 1048576 | tf_op jit(solution)/shard_map/all_to_all | solution.py:476
  79.4 3.3 %copy-start.1 = (bf16[128,16,128]{2,1,0:T(8,128)(2,1)}, bf16[128,16,128]{2,1,0:T(8,128)(2,1)S(1)}, u32[]{:S(2)}) copy-start(bf16[128,16,128]{2,1,0:T(8,128)(2,1)S(1)} %all-to-all-done.2.refs_0_) | copy-start | bytes 1572868
  82.7 18.2 %all-to-all-start.3 = ((bf16[128,16,128]{2,1,0:T(8,128)(2,1)}), bf16[128,16,128]{2,1,0:T(8,128)(2,1)S(1)}, u32[]{:S(2)}, u32[]{:S(2)}) async-start(bf16[128,16,128]{2,1,0:T(8,128)(2,1)} %back_push.1), calls=%async_computation.3 | async-start | bytes 1048576 | tf_op jit(solution)/shard_map/all_to_all | solution.py:476

commit v6 on v5

--- a/solution.py
+++ b/solution.py
@@ -99,8 +99,45 @@
         out_ref.send(half)
 
 
+def fours(x):
+    yield x & 15
+    for q in range(1, 7):
+        yield lax.shift_right_logical(x, 4 * q) & 15
+    yield lax.shift_right_logical(x, 28)
+
+
+def put(near_ref, far_ref, row, j, counts):
+    for q, count in enumerate(counts):
+        half = near_ref if q < 4 else far_ref
+        left = (q % 4) * 256 + j * LANES
+        half[pl.ds(row, 128), pl.ds(left, LANES)] = count.astype(F32).astype(BF16)
+
+
+def load_masters(flag_ref, words_ref, mm_hbm, mg_hbm, mm, mg, sem):
+    words_ref.wait()
+
+    @pl.when(flag_ref[0] == 0)
+    def _():
+        def block(i, carry):
+            d = pl.multiple_of(i * 128, 128)
+            for j in range(2):
+                at = pl.ds(pl.multiple_of(j * MASTERS + d, 128), 128)
+                put(mm, mg, d, j, fours(words_ref[at, :]))
+            return carry
+
+        lax.fori_loop(0, MASTERS // 128, block, 0)
+
+    @pl.when(flag_ref[0] != 0)
+    def _():
+        for source, target in ((mm_hbm, mm), (mg_hbm, mg)):
+            copy = pltpu.make_async_copy(source, target, sem)
+            copy.start()
+            copy.wait()
+
+
 def build_kernel(
-    live_ref, code_ref, rows_ref, mm_ref, mg_ref, gm_ref, gg_ref, sums_ref, codes, sem, *tables3
+    live_ref, code_ref, rows_ref, words_ref, gm_ref, gg_ref, sums_ref, flag_ref, mm_hbm, mg_hbm,
+    codes, sem, mm, mg, *tables3
 ):
     load = pltpu.make_async_copy(code_ref, codes, sem)
     load.start()
@@ -141,58 +178,56 @@
     turns = (n + TURN - 1) // TURN
     lax.fori_loop(0, turns, turn, 0)
 
-    def put(near_ref, far_ref, to, at, read, seen):
-        for j in range(2):
-            words = read(pl.ds(pl.multiple_of(j * SLOTS + at, 128), 128))
-            for q, counts in enumerate(words):
-                half = near_ref if q < 4 else far_ref
-                left = (q % 4) * 256 + j * LANES
-                half[pl.ds(to, 128), pl.ds(left, LANES)] = counts.astype(F32).astype(BF16)
-                seen = seen + jnp.sum(counts.reshape(16, 8, LANES), axis=0)
-        return seen
-
     rows = rows_ref[...]
-
-    def widen(read):
-        def mirrors(i, seen):
-            for h in range(2):
-                d = pl.multiple_of(i * 256 + h * 128, 128)
-                seen = put(gm_ref, gg_ref, d, MASTERS + d, read, seen)
-            e = pl.multiple_of(i * 256, 256)
-            gg_ref.send(pl.ds(e, 256))
-            gm_ref.send(pl.ds(e, 256))
-            return seen
-
-        def masters(i, seen):
-            e = pl.multiple_of(i * 256, 256)
-            sums_ref[pl.ds(e, 256), :] = dot(gm_ref[pl.ds(e, 256), :], rows)
-            for h in range(2):
-                d = pl.multiple_of(i * 256 + h * 128, 128)
-                seen = put(mm_ref, mg_ref, d, d, read, seen)
-            mm_ref.send(pl.ds(e, 256))
-            mg_ref.send(pl.ds(e, 256))
-            return seen
-
-        seen = lax.fori_loop(0, MIRRORS // 256, mirrors, jnp.zeros((8, LANES), jnp.int32))
-        seen = lax.fori_loop(0, MASTERS // 256, masters, seen)
-        sums_ref.send()
-        return seen
-
-    def finish():
-        for ref in (mm_ref, mg_ref, gm_ref, gg_ref, sums_ref):
-            ref.wait()
-
-    def read_fours(at):
+    none = jnp.zeros((8, LANES), jnp.int32)
+
+    def add_up(x):
+        return jnp.sum(x.reshape(16, 8, LANES), axis=0)
+
+    def table_sum(j, row):
+        at = pl.ds(pl.multiple_of(j * SLOTS + row, 128), 128)
         x = tables[0][at, :]
         for t in tables[1:]:
             x = x + t[at, :]
-        yield x & 15
-        for q in range(1, 7):
-            yield lax.shift_right_logical(x, 4 * q) & 15
-        yield lax.shift_right_logical(x, 28)
-
-    found = jnp.sum(widen(read_fours).astype(F32))
+        return x
+
+    def mirrors(i, seen):
+        e = pl.multiple_of(i * 256, 256)
+        for h in range(2):
+            d = pl.multiple_of(i * 256 + h * 128, 128)
+            for j in range(2):
+                counts = list(fours(table_sum(j, MASTERS + d)))
+                put(gm_ref, gg_ref, d, j, counts)
+                for count in counts:
+                    seen = seen + add_up(count)
+        gg_ref.send(pl.ds(e, 256))
+        gm_ref.send(pl.ds(e, 256))
+        return seen
+
+    def masters(i, seen):
+        e = pl.multiple_of(i * 256, 256)
+        sums_ref[pl.ds(e, 256), :] = dot(gm_ref[pl.ds(e, 256), :], rows)
+        for j in range(2):
+            for h in range(2):
+                x = table_sum(j, pl.multiple_of(i * 256 + h * 128, 128))
+                words_ref[pl.ds(pl.multiple_of(j * MASTERS + e + h * 128, 128), 128), :] = x
+                pairs = (x & 0x0F0F0F0F) + (lax.shift_right_logical(x, 4) & 0x0F0F0F0F)
+                fourth = (pairs & 0x00FF00FF) + (lax.shift_right_logical(pairs, 8) & 0x00FF00FF)
+                seen = seen + add_up(fourth)
+            words_ref.send(pl.ds(pl.multiple_of(j * MASTERS + e, 256), 256))
+        return seen
+
+    def finish():
+        sums_ref.send()
+        for ref in (words_ref, gm_ref, gg_ref, sums_ref):
+            ref.wait()
+
+    seen = lax.fori_loop(0, MIRRORS // 256, mirrors, none)
+    halves = lax.fori_loop(0, MASTERS // 256, masters, none)
+    seen = seen + (halves & 0xFFFF) + lax.shift_right_logical(halves, 16)
+    found = jnp.sum(seen.astype(F32))
     finish()
+    flag_ref[0] = jnp.where(found != n.astype(F32), 1, 0)
 
     @pl.when(found != n.astype(F32))
     def _():
@@ -209,14 +244,28 @@
 
         lax.fori_loop(0, n, edge, 0)
 
-        def read_halves(at):
-            for t in tables[:4]:
-                yield t[at, :] & 65535
-            for t in tables[:4]:
-                yield lax.shift_right_logical(t[at, :], 16)
-
-        widen(read_halves)
+        def wide(j, row):
+            at = pl.ds(pl.multiple_of(j * SLOTS + row, 128), 128)
+            found = [t[at, :] for t in tables[:4]]
+            return [x & 65535 for x in found] + [lax.shift_right_logical(x, 16) for x in found]
+
+        def block(i, carry):
+            d = pl.multiple_of(i * 128, 128)
+            for j in range(2):
+                put(gm_ref, gg_ref, d, j, wide(j, MASTERS + d))
+                put(mm, mg, d, j, wide(j, d))
+            sums_ref[pl.ds(d, 128), :] = dot(gm_ref[pl.ds(d, 128), :], rows)
+            return carry
+
+        lax.fori_loop(0, MASTERS // 128, block, 0)
+        words_ref.send()
+        gm_ref.send()
+        gg_ref.send()
         finish()
+        for source, target in ((mm, mm_hbm), (mg, mg_hbm)):
+            copy = pltpu.make_async_copy(source, target, sem)
+            copy.start()
+            copy.wait()
 
 
 def split(x):
@@ -245,7 +294,8 @@
 
 
 def local_kernel(
-    got_ref, rows_ref, mg_ref, mm_ref, turned_ref, told_ref, sums_ref, tally_ref
+    flag_ref, got_ref, rows_ref, words_ref, mm_hbm, mg_hbm,
+    turned_ref, told_ref, sums_ref, tally_ref, mm, mg, sem,
 ):
     rows = rows_ref[...]
     turned_ref[...] = rows.astype(F32).T.astype(BF16)
@@ -258,7 +308,8 @@
     ones = jnp.ones((MASTERS, LANES), BF16)
     near = jnp.concatenate([rows, ones], axis=1)
     far = jnp.concatenate([both[:, :F], ones], axis=1)
-    both = dot(mg_ref[...], far) + dot(mm_ref[...], near)
+    load_masters(flag_ref, words_ref, mm_hbm, mg_hbm, mm, mg, sem)
+    both = dot(mg[...], far) + dot(mm[...], near)
     sums_ref[...] = both[:, :F]
     sums_ref.send()
     tally_ref[...] = two_parts(both[:, F:])
@@ -291,7 +342,7 @@
         back = dot_nt(grad, w)
         own_ref[rows] = back[:, :F]
         msg = back[:, F:] * inverse
-        msg_ref[rows] = msg.astype(BF16)
+        msg_ref[rows] = msg
         for ref in (act_ref, own_ref, msg_ref):
             ref.send(rows)
         picked = picked + dot(msg.T.astype(BF16), scatter)
@@ -320,14 +371,16 @@
 
 
 def back_local_kernel(
-    gg_ref, msg_ref, mg_ref, mm_ref, own_ref, turned_ref, mirror_ref, base_ref
+    flag_ref, gg_ref, msg_ref, words_ref, own_ref, mm_hbm, mg_hbm,
+    turned_ref, mirror_ref, base_ref, mm, mg, sem,
 ):
     turned_ref[...] = gg_ref[...].T
     turned_ref.send()
-    msg = msg_ref[...].astype(F32).T.astype(BF16)
-    mirror_ref[...] = dot(msg, mg_ref[...]).T
+    msg = msg_ref[...].T.astype(BF16)
+    load_masters(flag_ref, words_ref, mm_hbm, mg_hbm, mm, mg, sem)
+    mirror_ref[...] = dot(msg, mg[...]).T
     mirror_ref.send()
-    base_ref[...] = dot(msg, mm_ref[...]).T + own_ref[...]
+    base_ref[...] = dot(msg, mm[...]).T + own_ref[...]
     base_ref.send()
 
 
@@ -430,14 +483,15 @@
 
 
 def call(
-    kernel, ins, outs, name, near=(), scalars=(), bare=(), scratch=(), parts=None,
+    kernel, ins, outs, name, near=(), scalars=(), bare=(), plain=None, scratch=(), parts=None,
     room=ALL, flops=0, moved=0,
 ):
-    parts = parts or {}
+    parts, plain = parts or {}, plain or {}
+    away = [k for k in range(len(outs)) if k not in plain]
     far = [k for k in range(len(ins)) if k not in (*near, *scalars, *bare)]
     specs = [VMEM if k in near else SMEM if k in scalars else HBM for k in range(len(ins))]
     held = [pltpu.VMEM(ins[k].shape, ins[k].dtype) for k in far]
-    held += [pltpu.VMEM(s, t) for s, t in outs]
+    held += [pltpu.VMEM(*outs[k]) for k in away]
     counts = [parts.get(k, 1) for k in far]
     dma = pltpu.SemaphoreType.DMA
 
@@ -445,27 +499,27 @@
         operands, refs = list(refs[: len(ins)]), refs[len(ins) :]
         results, refs = list(refs[: len(outs)]), refs[len(outs) :]
         copies, refs = refs[: len(far)], refs[len(far) :]
-        holds, refs = refs[: len(outs)], refs[len(outs) :]
+        holds, refs = refs[: len(away)], refs[len(away) :]
         load_sems, store_sems = refs[0], refs[1]
         first = 0
         for k, copy, count in zip(far, copies, counts, strict=True):
             operands[k] = Loaded(operands[k], copy, load_sems, first, count)
             first += count
-        for k, hold in enumerate(holds):
-            results[k] = Stored(hold, results[k], store_sems.at[k])
+        for n, (k, hold) in enumerate(zip(away, holds, strict=True)):
+            results[k] = Stored(hold, results[k], store_sems.at[n])
         kernel(*operands, *results, *refs[2:])
         for k in far:
             operands[k].wait()
-        for result in results:
-            if not result.waited:
-                result.wait()
+        for k in away:
+            if not results[k].waited:
+                results[k].wait()
 
     return pl.pallas_call(
         body,
         out_shape=[jax.ShapeDtypeStruct(s, t) for s, t in outs],
         in_specs=specs,
-        out_specs=[HBM] * len(outs),
-        scratch_shapes=held + [dma((max(sum(counts), 1),)), dma((len(outs),))] + list(scratch),
+        out_specs=[plain.get(k, HBM) for k in range(len(outs))],
+        scratch_shapes=held + [dma((max(sum(counts), 1),)), dma((len(away),))] + list(scratch),
         compiler_params=pltpu.CompilerParams(vmem_limit_bytes=room),
         cost_estimate=pl.CostEstimate(flops=flops, bytes_accessed=moved, transcendentals=0),
         name=name,
@@ -494,14 +548,25 @@
         scratch=[pltpu.VMEM((32, EDGES), BF16), pltpu.VMEM((32, EDGES), BF16)],
     )
     got1 = exchange(out1)
-    mm, mg, gm, gg, sums = call(
+    quarters = [pltpu.VMEM(*square), pltpu.VMEM(*square)]
+    words, gm, gg, sums, flag, mm, mg = call(
         build_kernel,
         (edge_live, code, features),
-        [square] * 4 + [rows_f32],
+        [
+            ((2 * MASTERS, LANES), jnp.int32),
+            square,
+            square,
+            rows_f32,
+            ((1,), jnp.int32),
+            square,
+            square,
+        ],
         "build",
         scalars=(0,),
         bare=(1,),
+        plain={4: SMEM, 5: HBM, 6: HBM},
         scratch=[pltpu.SMEM(edges, jnp.int32), pltpu.SemaphoreType.DMA]
+        + quarters
         + [pltpu.VMEM((WORDS, 1, LANES), jnp.int32) for _ in range(COPIES)],
         flops=20_000_000_000,
         moved=20_000_000,
@@ -518,9 +583,12 @@
     got2 = exchange(out2)
     turned, told, sums_m, tally = call(
         local_kernel,
-        (got1, features, mg, mm),
+        (flag, got1, features, words, mm, mg),
         [((F, MASTERS), BF16), rows_bf16, rows_f32, rows_bf16],
         "local",
+        scalars=(0,),
+        bare=(4, 5),
+        scratch=quarters + [pltpu.SemaphoreType.DMA],
         flops=2_000_000_000,
         moved=6_000_000,
     )
@@ -530,7 +598,7 @@
             got2, line, told, tally, sums_m, features, w_self, w_neigh, bias.reshape(1, H),
             cotangent, turned,
         ),
-        [((MASTERS, H), BF16), rows_f32, rows_bf16, payload, ((8, F), F32)],
+        [((MASTERS, H), BF16), rows_f32, rows_f32, payload, ((8, F), F32)],
         "dense",
         near=(0,),
         room=55_800_000,
@@ -538,9 +606,12 @@
     got3 = exchange(out3)
     turned_gg, mirror, base = call(
         back_local_kernel,
-        (gg, msg, mg, mm, own),
+        (flag, gg, msg, words, own, mm, mg),
         [square, rows_f32, rows_f32],
         "back_local",
+        scalars=(0,),
+        bare=(5, 6),
+        scratch=quarters + [pltpu.SemaphoreType.DMA],
         flops=2_000_000_000,
         moved=6_000_000,
     )

time: 104 us -> 103 us (level)
  starting transfers between devices: 30.1 us -> 28.8 us
  waiting for transfers between devices: 30.7 us -> 29.4 us
    all_to_all x4, starting transfers between devices: 30.1 us -> 28.8 us  [exchange(): return lax.all_to_all(x, AXES, split_axis=0, concat_axis=0, tiled=True)]
    all_to_all x4, waiting for transfers between devices: 30.7 us -> 29.4 us  [exchange(): return lax.all_to_all(x, AXES, split_axis=0, concat_axis=0, tiled=True)]
  transfers between devices with their start and end apart: 4 -> 4, of which waited for: 4 -> 4; matrix products, arithmetic and copies ran while one was open for 0% -> 0% of each run, Pallas kernels for 22% -> 24%
where the time goes in v6:
time: 103 us; the launch traced here: 102 us
  Pallas kernels  41 us (40%)
  waiting for transfers between devices  29.4 us (29%)
  starting transfers between devices  28.8 us (28%)
  between operations  1.6 us (2%)
  local copies, waits for them, and re-layouts  1.18 us (1%)
    pallas_call x9, Pallas kernels, call(): pl.pallas_call(body, out_shape=[jax.ShapeDtypeStruct(s, t) for s, t in ou...  41 us
    all_to_all x4, waiting for transfers between devices, exchange(): return lax.all_to_all(x, AXES, split_axis=0, concat_axis=0, tiled=True)  29.4 us
    all_to_all x4, starting transfers between devices, exchange(): return lax.all_to_all(x, AXES, split_axis=0, concat_axis=0, tiled=True)  28.8 us
  transfers between devices with their start and end apart: 4, of which 4 were waited for; matrix products, arithmetic and copies ran while one was open for 0% of the time, Pallas kernels for 24%

profile of v6, /device:TPU:1, one launch (start us, length us, event | category | flops | bytes accessed | tf_op | source)
XLA Modules:
  0.0 102.0 jit_solution(17036125794637428313)
XLA Ops:
  1.3 3.8 %pull.1 = (bf16[128,16,128]{2,1,0:T(8,128)(2,1)}, s32[64,128]{1,0:T(8,128)}) custom-call(s32[1]{0:T(128)S(6)} %copy.16.refs_0_, s32[8,128]{1,0:T(8,128)} %bitcast.10, s32[64,128]{1,0:T(8,128)} %bitcast.8, s32[64,128]{1,0:T(8,128)} %bitcast.9, bf16[1024,128]{1,0:T(8,128)(2,1)} %refs_5_.1), custom_call_target="tpu_custom_call" | custom-call | tf_op jit(solution)/shard_map/pull/pallas_call | solution.py:517
  5.1 11.5 %all-to-all-start = ((bf16[128,16,128]{2,1,0:T(8,128)(2,1)}), bf16[128,16,128]{2,1,0:T(8,128)(2,1)S(1)}, u32[]{:S(2)}, u32[]{:S(2)}) async-start(bf16[128,16,128]{2,1,0:T(8,128)(2,1)} %get-tuple-element.30), calls=%async_computation | async-start | bytes 1048576 | tf_op jit(solution)/shard_map/all_to_all | solution.py:530
  16.6 9.1 %build.1 = (s32[2048,128]{1,0:T(8,128)}, bf16[1024,1024]{1,0:T(8,128)(2,1)}, bf16[1024,1024]{1,0:T(8,128)(2,1)}, f32[1024,128]{1,0:T(8,128)}, s32[1]{0:T(128)}, ...) custom-call(s32[1]{0:T(128)S(6)} %copy.16.refs_0_, s32[64,128]{1,0:T(8,128)} %get-tuple-element.31.refs_1_, ...), custom_call_target="tpu_custom_call" | custom-call | flops 20000000000 | bytes 20000000 | tf_op jit(solution)/shard_map/build/pallas_call | solution.py:517
  25.7 0.0 copy-start.6
  25.7 5.0 %all-to-all-done.refs_0_.refs_1_ = bf16[128,16,128]{2,1,0:T(8,128)(2,1)S(1)} async-done(((bf16[128,16,128]{2,1,0:T(8,128)(2,1)}), bf16[128,16,128]{2,1,0:T(8,128)(2,1)S(1)}, u32[]{:S(2)}, u32[]{:S(2)}) %all-to-all-start) | async-done | bytes 524320 | tf_op jit(solution)/shard_map/all_to_all | solution.py:530
  30.7 0.0 copy-start
  30.7 3.2 %push.1 = bf16[128,8,128]{2,1,0:T(8,128)(2,1)} custom-call(bf16[128,16,128]{2,1,0:T(8,128)(2,1)S(1)} %all-to-all-done.refs_0_.refs_1_, f32[1024,128]{1,0:T(8,128)} %get-tuple-element.32.refs_1_, bf16[1024,1024]{1,0:T(8,128)(2,1)} %get-tuple-element.33.refs_2_.refs_1_), custom_call_target="tpu_custom_call" | custom-call | tf_op jit(solution)/shard_map/push/pallas_call | solution.py:517
  33.9 9.1 %all-to-all-start.1 = ((bf16[128,8,128]{2,1,0:T(8,128)(2,1)}), bf16[128,8,128]{2,1,0:T(8,128)(2,1)S(1)}, u32[]{:S(2)}, u32[]{:S(2)}) async-start(bf16[128,8,128]{2,1,0:T(8,128)(2,1)} %push.1), calls=%async_computation.1 | async-start | bytes 524288 | tf_op jit(solution)/shard_map/all_to_all | solution.py:530
  43.0 0.0 copy-done.6
  43.0 0.1 copy.15
  43.1 0.1 reshape.27.refs_1_.refs_0_
  43.2 0.0 copy-done
  43.2 0.0 copy-start.3
  43.2 0.0 copy-start.4
  43.3 0.0 copy-start.5
  43.3 5.6 %local.1 = (bf16[128,1024]{1,0:T(8,128)(2,1)}, bf16[1024,128]{1,0:T(8,128)(2,1)}, f32[1024,128]{1,0:T(8,128)}, bf16[1024,128]{1,0:T(8,128)(2,1)}) custom-call(s32[1]{0:T(128)} %get-tuple-element.34.refs_0_, bf16[128,16,128]{2,1,0:T(8,128)(2,1)} %copy-done, bf16[1024,128]{1,0:T(8,128)(2,1)} %refs_5_.1, s32[2048,128]{1,0:T(8,128)} %get-tuple-element.35.refs_3_, ...), custom_call_target="tpu_custom_call" | custom-call | flops 2000000000 | bytes 6000000 | tf_op jit(solution)/shard_map/local/pallas_call | solution.py:517
  48.9 5.6 %all-to-all-done.1.refs_0_ = bf16[128,8,128]{2,1,0:T(8,128)(2,1)S(1)} async-done(((bf16[128,8,128]{2,1,0:T(8,128)(2,1)}), bf16[128,8,128]{2,1,0:T(8,128)(2,1)S(1)}, u32[]{:S(2)}, u32[]{:S(2)}) %all-to-all-start.1) | async-done | bytes 262176 | tf_op jit(solution)/shard_map/all_to_all | solution.py:530
  54.5 0.0 copy-done.3
  54.5 0.0 copy-done.4
  54.5 0.0 copy-done.5
  54.5 0.0 copy-start.2
  54.5 0.9 copy-done.2
  55.4 4.2 %dense.1 = (bf16[1024,256]{1,0:T(8,128)(2,1)}, f32[1024,128]{1,0:T(8,128)}, f32[1024,128]{1,0:T(8,128)}, bf16[128,16,128]{2,1,0:T(8,128)(2,1)}, f32[8,128]{1,0:T(8,128)S(1)}) custom-call(bf16[128,8,128]{2,1,0:T(8,128)(2,1)S(1)} %all-to-all-done.1.refs_0_, s32[1,1024]{1,0:T(1,128)S(1)} %reshape.27.refs_1_.refs_0_, bf16[1024,128]{1,0:T(8,128)(2,1)S(1)} %copy-done.2, ...), custom_call_target="tpu_custom_call" | custom-call | tf_op jit(solution)/shard_map/dense/pallas_call | solution.py:517
  59.6 4.2 %all-to-all-start.2 = ((bf16[128,16,128]{2,1,0:T(8,128)(2,1)}), bf16[128,16,128]{2,1,0:T(8,128)(2,1)S(1)}, u32[]{:S(2)}, u32[]{:S(2)}) async-start(bf16[128,16,128]{2,1,0:T(8,128)(2,1)} %get-tuple-element.43), calls=%async_computation.2 | async-start | bytes 1048576 | tf_op jit(solution)/shard_map/all_to_all | solution.py:530
  63.8 6.2 %back_local.1 = (bf16[1024,1024]{1,0:T(8,128)(2,1)}, f32[1024,128]{1,0:T(8,128)}, f32[1024,128]{1,0:T(8,128)}) custom-call(s32[1]{0:T(128)} %get-tuple-element.34.refs_0_, bf16[1024,1024]{1,0:T(8,128)(2,1)} %get-tuple-element.33.refs_2_.refs_1_, f32[1024,128]{1,0:T(8,128)} %get-tuple-element.44.refs_2_, s32[2048,128]{1,0:T(8,128)} %get-tuple-element.35.refs_3_, ...), custom_call_target="tpu_custom_call" | custom-call | flops 2000000000 | bytes 6000000 | tf_op jit(solution)/shard_map/back_local/pallas_call | solution.py:517
  70.0 7.9 %all-to-all-done.2.refs_0_ = bf16[128,16,128]{2,1,0:T(8,128)(2,1)S(1)} async-done(((bf16[128,16,128]{2,1,0:T(8,128)(2,1)}), bf16[128,16,128]{2,1,0:T(8,128)(2,1)S(1)}, u32[]{:S(2)}, u32[]{:S(2)}) %all-to-all-start.2) | async-done | bytes 524320 | tf_op jit(solution)/shard_map/all_to_all | solution.py:530
  77.9 0.0 copy-start.1
  77.9 3.3 %back_push.1 = bf16[128,16,128]{2,1,0:T(8,128)(2,1)} custom-call(bf16[128,16,128]{2,1,0:T(8,128)(2,1)S(1)} %all-to-all-done.2.refs_0_, f32[1024,128]{1,0:T(8,128)} %get-tuple-element.46.refs_1_, f32[8,128]{1,0:T(8,128)S(1)} %get-tuple-element.47.refs_2_, bf16[1024,1024]{1,0:T(8,128)(2,1)} %get-tuple-element.48.refs_3_), custom_call_target="tpu_custom_call" | custom-call | tf_op jit(solution)/shard_map/back_push/pallas_call | solution.py:517
  81.2 0.0 copy-done.1
  81.2 4.0 %all-to-all-start.3 = ((bf16[128,16,128]{2,1,0:T(8,128)(2,1)}), bf16[128,16,128]{2,1,0:T(8,128)(2,1)S(1)}, u32[]{:S(2)}, u32[]{:S(2)}) async-start(bf16[128,16,128]{2,1,0:T(8,128)(2,1)} %back_push.1), calls=%async_computation.3 | async-start | bytes 1048576 | tf_op jit(solution)/shard_map/all_to_all | solution.py:530
  85.2 3.2 %back_mirror.1.refs_2_ = f32[1024,128]{1,0:T(8,128)} custom-call(bf16[128,16,128]{2,1,0:T(8,128)(2,1)} %copy-done.1, bf16[1024,1024]{1,0:T(8,128)(2,1)} %get-tuple-element.49.refs_1_, f32[1024,128]{1,0:T(8,128)} %get-tuple-element.50.refs_2_), custom_call_target="tpu_custom_call" | custom-call | flops 2000000000 | bytes 6000000 | tf_op jit(solution)/shard_map/back_mirror/pallas_call | solution.py:517
  88.4 11.0 %all-to-all-done.3.refs_1_ = bf16[128,16,128]{2,1,0:T(8,128)(2,1)S(1)} async-done(((bf16[128,16,128]{2,1,0:T(8,128)(2,1)}), bf16[128,16,128]{2,1,0:T(8,128)(2,1)S(1)}, u32[]{:S(2)}, u32[]{:S(2)}) %all-to-all-start.3) | async-done | bytes 524320 | tf_op jit(solution)/shard_map/all_to_all | solution.py:530
  99.4 2.5 %last.1 = (bf16[1024,128]{1,0:T(8,128)(2,1)}, f32[128,256]{1,0:T(8,128)}, f32[128,256]{1,0:T(8,128)}, f32[2,128]{1,0:T(2,128)}) custom-call(s32[1,1024]{1,0:T(1,128)S(1)} %reshape.27.refs_1_.refs_0_, bf16[128,16,128]{2,1,0:T(8,128)(2,1)S(1)} %all-to-all-done.3.refs_1_, f32[1024,128]{1,0:T(8,128)} %back_mirror.1.refs_2_), custom_call_target="tpu_custom_call" | custom-call | tf_op jit(solution)/shard_map/last/pallas_call | solution.py:517
Async XLA Ops:
  5.1 25.6 %all-to-all-start = ((bf16[128,16,128]{2,1,0:T(8,128)(2,1)}), bf16[128,16,128]{2,1,0:T(8,128)(2,1)S(1)}, u32[]{:S(2)}, u32[]{:S(2)}) async-start(bf16[128,16,128]{2,1,0:T(8,128)(2,1)} %get-tuple-element.30), calls=%async_computation | async-start | bytes 1048576 | tf_op jit(solution)/shard_map/all_to_all | solution.py:530
  25.7 17.3 %copy-start.6 = (s32[1,128,8]{1,2,0:T(8,128)S(1)}, s32[1,128,8]{1,2,0:T(8,128)}, u32[]{:S(2)}) copy-start(s32[1,128,8]{1,2,0:T(8,128)} %param.17) | copy-start | bytes 12292
  30.7 12.5 %copy-start = (bf16[128,16,128]{2,1,0:T(8,128)(2,1)}, bf16[128,16,128]{2,1,0:T(8,128)(2,1)S(1)}, u32[]{:S(2)}) copy-start(bf16[128,16,128]{2,1,0:T(8,128)(2,1)S(1)} %all-to-all-done.refs_0_.refs_1_) | copy-start | bytes 1572868
  33.9 20.5 %all-to-all-start.1 = ((bf16[128,8,128]{2,1,0:T(8,128)(2,1)}), bf16[128,8,128]{2,1,0:T(8,128)(2,1)S(1)}, u32[]{:S(2)}, u32[]{:S(2)}) async-start(bf16[128,8,128]{2,1,0:T(8,128)(2,1)} %push.1), calls=%async_computation.1 | async-start | bytes 524288 | tf_op jit(solution)/shard_map/all_to_all | solution.py:530
  43.2 11.2 %copy-start.3 = (bf16[128,256]{1,0:T(8,128)(2,1)S(1)}, bf16[128,256]{1,0:T(8,128)(2,1)}, u32[]{:S(2)}) copy-start(bf16[128,256]{1,0:T(8,128)(2,1)} %refs_6_.1) | copy-start | bytes 196612
  43.2 11.2 %copy-start.4 = (bf16[128,256]{1,0:T(8,128)(2,1)S(1)}, bf16[128,256]{1,0:T(8,128)(2,1)}, u32[]{:S(2)}) copy-start(bf16[128,256]{1,0:T(8,128)(2,1)} %refs_7_.1) | copy-start | bytes 196612
  43.3 11.2 %copy-start.5 = (f32[256]{0:T(256)S(1)}, f32[256]{0:T(256)}, u32[]{:S(2)}) copy-start(f32[256]{0:T(256)} %param.13) | copy-start | bytes 3076
  54.5 1.0 copy-start.2
  59.6 18.3 %all-to-all-start.2 = ((bf16[128,16,128]{2,1,0:T(8,128)(2,1)}), bf16[128,16,128]{2,1,0:T(8,128)(2,1)S(1)}, u32[]{:S(2)}, u32[]{:S(2)}) async-start(bf16[128,16,128]{2,1,0:T(8,128)(2,1)} %get-tuple-element.43), calls=%async_computation.2 | async-start | bytes 1048576 | tf_op jit(solution)/shard_map/all_to_all | solution.py:530
  77.9 3.3 %copy-start.1 = (bf16[128,16,128]{2,1,0:T(8,128)(2,1)}, bf16[128,16,128]{2,1,0:T(8,128)(2,1)S(1)}, u32[]{:S(2)}) copy-start(bf16[128,16,128]{2,1,0:T(8,128)(2,1)S(1)} %all-to-all-done.2.refs_0_) | copy-start | bytes 1572868
  81.2 18.2 %all-to-all-start.3 = ((bf16[128,16,128]{2,1,0:T(8,128)(2,1)}), bf16[128,16,128]{2,1,0:T(8,128)(2,1)S(1)}, u32[]{:S(2)}, u32[]{:S(2)}) async-start(bf16[128,16,128]{2,1,0:T(8,128)(2,1)} %back_push.1), calls=%async_computation.3 | async-start | bytes 1048576 | tf_op jit(solution)/shard_map/all_to_all | solution.py:530

commit v7 on v6

--- a/solution.py
+++ b/solution.py
@@ -586,6 +586,7 @@
         (flag, got1, features, words, mm, mg),
         [((F, MASTERS), BF16), rows_bf16, rows_f32, rows_bf16],
         "local",
+        room=55_000_000,
         scalars=(0,),
         bare=(4, 5),
         scratch=quarters + [pltpu.SemaphoreType.DMA],
@@ -601,7 +602,7 @@
         [((MASTERS, H), BF16), rows_f32, rows_f32, payload, ((8, F), F32)],
         "dense",
         near=(0,),
-        room=55_800_000,
+        room=55_000_000,
     )
     got3 = exchange(out3)
     turned_gg, mirror, base = call(

time: 103 us -> 102 us (level)
  Pallas kernels: 41 us -> 44.1 us
  waiting for transfers between devices: 29.4 us -> 26.4 us
    pallas_call x9, Pallas kernels: 41 us -> 44.1 us  [call(): pl.pallas_call(body, out_shape=[jax.ShapeDtypeStruct(s, t) for s, t in ou...]
    all_to_all x4, waiting for transfers between devices: 29.4 us -> 26.4 us  [exchange(): return lax.all_to_all(x, AXES, split_axis=0, concat_axis=0, tiled=True)]
  transfers between devices with their start and end apart: 4 -> 4, of which waited for: 4 -> 4; matrix products, arithmetic and copies ran while one was open for 0% -> 0% of each run, Pallas kernels for 24% -> 27%
where the time goes in v7:
time: 102 us; the launch traced here: 101 us
  Pallas kernels  44.1 us (43%)
  starting transfers between devices  29.1 us (29%)
  waiting for transfers between devices  26.4 us (26%)
  between operations  1.61 us (2%)
    pallas_call x9, Pallas kernels, call(): pl.pallas_call(body, out_shape=[jax.ShapeDtypeStruct(s, t) for s, t in ou...  44.1 us
    all_to_all x4, starting transfers between devices, exchange(): return lax.all_to_all(x, AXES, split_axis=0, concat_axis=0, tiled=True)  29.1 us
    all_to_all x4, waiting for transfers between devices, exchange(): return lax.all_to_all(x, AXES, split_axis=0, concat_axis=0, tiled=True)  26.4 us
  transfers between devices with their start and end apart: 4, of which 4 were waited for; matrix products, arithmetic and copies ran while one was open for 0% of the time, Pallas kernels for 27%

profile of v7, /device:TPU:1, one launch (start us, length us, event | category | flops | bytes accessed | tf_op | source)
XLA Modules:
  0.0 101.5 jit_solution(10386462843062429770)
XLA Ops:
  1.3 3.8 %pull.1 = (bf16[128,16,128]{2,1,0:T(8,128)(2,1)}, s32[64,128]{1,0:T(8,128)}) custom-call(s32[1]{0:T(128)S(6)} %copy.16.refs_0_, s32[8,128]{1,0:T(8,128)} %bitcast.10, s32[64,128]{1,0:T(8,128)} %bitcast.8, s32[64,128]{1,0:T(8,128)} %bitcast.9, bf16[1024,128]{1,0:T(8,128)(2,1)} %refs_5_.1), custom_call_target="tpu_custom_call" | custom-call | tf_op jit(solution)/shard_map/pull/pallas_call | solution.py:517
  5.1 11.5 %all-to-all-start = ((bf16[128,16,128]{2,1,0:T(8,128)(2,1)}), bf16[128,16,128]{2,1,0:T(8,128)(2,1)S(1)}, u32[]{:S(2)}, u32[]{:S(2)}) async-start(bf16[128,16,128]{2,1,0:T(8,128)(2,1)} %get-tuple-element.30), calls=%async_computation | async-start | bytes 1048576 | tf_op jit(solution)/shard_map/all_to_all | solution.py:530
  16.6 12.2 %build.1 = (s32[2048,128]{1,0:T(8,128)}, bf16[1024,1024]{1,0:T(8,128)(2,1)}, bf16[1024,1024]{1,0:T(8,128)(2,1)}, f32[1024,128]{1,0:T(8,128)}, s32[1]{0:T(128)}, ...) custom-call(s32[1]{0:T(128)S(6)} %copy.16.refs_0_, s32[64,128]{1,0:T(8,128)} %get-tuple-element.31.refs_1_, ...), custom_call_target="tpu_custom_call" | custom-call | flops 20000000000 | bytes 20000000 | tf_op jit(solution)/shard_map/build/pallas_call | solution.py:517
  28.8 0.0 copy-start.6
  28.9 0.0 copy-start.2
  28.9 1.8 %all-to-all-done.refs_0_.refs_1_ = bf16[128,16,128]{2,1,0:T(8,128)(2,1)S(1)} async-done(((bf16[128,16,128]{2,1,0:T(8,128)(2,1)}), bf16[128,16,128]{2,1,0:T(8,128)(2,1)S(1)}, u32[]{:S(2)}, u32[]{:S(2)}) %all-to-all-start) | async-done | bytes 524320 | tf_op jit(solution)/shard_map/all_to_all | solution.py:530
  30.7 0.0 copy-start
  30.7 3.2 %push.1 = bf16[128,8,128]{2,1,0:T(8,128)(2,1)} custom-call(bf16[128,16,128]{2,1,0:T(8,128)(2,1)S(1)} %all-to-all-done.refs_0_.refs_1_, f32[1024,128]{1,0:T(8,128)} %get-tuple-element.32.refs_1_, bf16[1024,1024]{1,0:T(8,128)(2,1)} %get-tuple-element.33.refs_2_.refs_1_), custom_call_target="tpu_custom_call" | custom-call | tf_op jit(solution)/shard_map/push/pallas_call | solution.py:517
  33.9 9.5 %all-to-all-start.1 = ((bf16[128,8,128]{2,1,0:T(8,128)(2,1)}), bf16[128,8,128]{2,1,0:T(8,128)(2,1)S(1)}, u32[]{:S(2)}, u32[]{:S(2)}) async-start(bf16[128,8,128]{2,1,0:T(8,128)(2,1)} %push.1), calls=%async_computation.1 | async-start | bytes 524288 | tf_op jit(solution)/shard_map/all_to_all | solution.py:530
  43.5 0.0 copy-done.6
  43.5 0.1 copy.15
  43.6 0.1 reshape.27.refs_1_.refs_0_
  43.7 0.0 copy-done
  43.7 0.0 copy-done.2
  43.7 0.0 copy-start.3
  43.7 0.0 copy-start.4
  43.7 0.0 copy-start.5
  43.7 5.5 %local.1 = (bf16[128,1024]{1,0:T(8,128)(2,1)S(1)}, bf16[1024,128]{1,0:T(8,128)(2,1)S(1)}, f32[1024,128]{1,0:T(8,128)}, bf16[1024,128]{1,0:T(8,128)(2,1)S(1)}) custom-call(s32[1]{0:T(128)} %get-tuple-element.34.refs_0_, bf16[128,16,128]{2,1,0:T(8,128)(2,1)} %copy-done, bf16[1024,128]{1,0:T(8,128)(2,1)S(1)} %copy-done.2, ...), custom_call_target="tpu_custom_call" | custom-call | flops 2000000000 | bytes 6000000 | tf_op jit(solution)/shard_map/local/pallas_call | solution.py:517
  49.2 5.7 %all-to-all-done.1.refs_0_ = bf16[128,8,128]{2,1,0:T(8,128)(2,1)S(1)} async-done(((bf16[128,8,128]{2,1,0:T(8,128)(2,1)}), bf16[128,8,128]{2,1,0:T(8,128)(2,1)S(1)}, u32[]{:S(2)}, u32[]{:S(2)}) %all-to-all-start.1) | async-done | bytes 262176 | tf_op jit(solution)/shard_map/all_to_all | solution.py:530
  54.9 0.0 copy-done.3
  54.9 0.0 copy-done.4
  54.9 0.0 copy-done.5
  54.9 4.2 %dense.1 = (bf16[1024,256]{1,0:T(8,128)(2,1)}, f32[1024,128]{1,0:T(8,128)}, f32[1024,128]{1,0:T(8,128)}, bf16[128,16,128]{2,1,0:T(8,128)(2,1)}, f32[8,128]{1,0:T(8,128)S(1)}) custom-call(bf16[128,8,128]{2,1,0:T(8,128)(2,1)S(1)} %all-to-all-done.1.refs_0_, s32[1,1024]{1,0:T(1,128)S(1)} %reshape.27.refs_1_.refs_0_, ...), custom_call_target="tpu_custom_call" | custom-call | tf_op jit(solution)/shard_map/dense/pallas_call | solution.py:517
  59.1 4.1 %all-to-all-start.2 = ((bf16[128,16,128]{2,1,0:T(8,128)(2,1)}), bf16[128,16,128]{2,1,0:T(8,128)(2,1)S(1)}, u32[]{:S(2)}, u32[]{:S(2)}) async-start(bf16[128,16,128]{2,1,0:T(8,128)(2,1)} %get-tuple-element.43), calls=%async_computation.2 | async-start | bytes 1048576 | tf_op jit(solution)/shard_map/all_to_all | solution.py:530
  63.2 6.2 %back_local.1 = (bf16[1024,1024]{1,0:T(8,128)(2,1)}, f32[1024,128]{1,0:T(8,128)}, f32[1024,128]{1,0:T(8,128)}) custom-call(s32[1]{0:T(128)} %get-tuple-element.34.refs_0_, bf16[1024,1024]{1,0:T(8,128)(2,1)} %get-tuple-element.33.refs_2_.refs_1_, f32[1024,128]{1,0:T(8,128)} %get-tuple-element.44.refs_2_, s32[2048,128]{1,0:T(8,128)} %get-tuple-element.35.refs_3_, ...), custom_call_target="tpu_custom_call" | custom-call | flops 2000000000 | bytes 6000000 | tf_op jit(solution)/shard_map/back_local/pallas_call | solution.py:517
  69.5 7.9 %all-to-all-done.2.refs_0_ = bf16[128,16,128]{2,1,0:T(8,128)(2,1)S(1)} async-done(((bf16[128,16,128]{2,1,0:T(8,128)(2,1)}), bf16[128,16,128]{2,1,0:T(8,128)(2,1)S(1)}, u32[]{:S(2)}, u32[]{:S(2)}) %all-to-all-start.2) | async-done | bytes 524320 | tf_op jit(solution)/shard_map/all_to_all | solution.py:530
  77.3 0.0 copy-start.1
  77.3 3.3 %back_push.1 = bf16[128,16,128]{2,1,0:T(8,128)(2,1)} custom-call(bf16[128,16,128]{2,1,0:T(8,128)(2,1)S(1)} %all-to-all-done.2.refs_0_, f32[1024,128]{1,0:T(8,128)} %get-tuple-element.46.refs_1_, f32[8,128]{1,0:T(8,128)S(1)} %get-tuple-element.47.refs_2_, bf16[1024,1024]{1,0:T(8,128)(2,1)} %get-tuple-element.48.refs_3_), custom_call_target="tpu_custom_call" | custom-call | tf_op jit(solution)/shard_map/back_push/pallas_call | solution.py:517
  80.6 0.0 copy-done.1
  80.6 4.0 %all-to-all-start.3 = ((bf16[128,16,128]{2,1,0:T(8,128)(2,1)}), bf16[128,16,128]{2,1,0:T(8,128)(2,1)S(1)}, u32[]{:S(2)}, u32[]{:S(2)}) async-start(bf16[128,16,128]{2,1,0:T(8,128)(2,1)} %back_push.1), calls=%async_computation.3 | async-start | bytes 1048576 | tf_op jit(solution)/shard_map/all_to_all | solution.py:530
  84.6 3.2 %back_mirror.1.refs_2_ = f32[1024,128]{1,0:T(8,128)} custom-call(bf16[128,16,128]{2,1,0:T(8,128)(2,1)} %copy-done.1, bf16[1024,1024]{1,0:T(8,128)(2,1)} %get-tuple-element.49.refs_1_, f32[1024,128]{1,0:T(8,128)} %get-tuple-element.50.refs_2_), custom_call_target="tpu_custom_call" | custom-call | flops 2000000000 | bytes 6000000 | tf_op jit(solution)/shard_map/back_mirror/pallas_call | solution.py:517
  87.8 11.0 %all-to-all-done.3.refs_1_ = bf16[128,16,128]{2,1,0:T(8,128)(2,1)S(1)} async-done(((bf16[128,16,128]{2,1,0:T(8,128)(2,1)}), bf16[128,16,128]{2,1,0:T(8,128)(2,1)S(1)}, u32[]{:S(2)}, u32[]{:S(2)}) %all-to-all-start.3) | async-done | bytes 524320 | tf_op jit(solution)/shard_map/all_to_all | solution.py:530
  98.8 2.5 %last.1 = (bf16[1024,128]{1,0:T(8,128)(2,1)}, f32[128,256]{1,0:T(8,128)}, f32[128,256]{1,0:T(8,128)}, f32[2,128]{1,0:T(2,128)}) custom-call(s32[1,1024]{1,0:T(1,128)S(1)} %reshape.27.refs_1_.refs_0_, bf16[128,16,128]{2,1,0:T(8,128)(2,1)S(1)} %all-to-all-done.3.refs_1_, f32[1024,128]{1,0:T(8,128)} %back_mirror.1.refs_2_), custom_call_target="tpu_custom_call" | custom-call | tf_op jit(solution)/shard_map/last/pallas_call | solution.py:517
Async XLA Ops:
  5.1 25.6 %all-to-all-start = ((bf16[128,16,128]{2,1,0:T(8,128)(2,1)}), bf16[128,16,128]{2,1,0:T(8,128)(2,1)S(1)}, u32[]{:S(2)}, u32[]{:S(2)}) async-start(bf16[128,16,128]{2,1,0:T(8,128)(2,1)} %get-tuple-element.30), calls=%async_computation | async-start | bytes 1048576 | tf_op jit(solution)/shard_map/all_to_all | solution.py:530
  28.8 14.6 %copy-start.6 = (s32[1,128,8]{1,2,0:T(8,128)S(1)}, s32[1,128,8]{1,2,0:T(8,128)}, u32[]{:S(2)}) copy-start(s32[1,128,8]{1,2,0:T(8,128)} %param.17) | copy-start | bytes 12292
  28.9 14.8 %copy-start.2 = (bf16[1024,128]{1,0:T(8,128)(2,1)S(1)}, bf16[1024,128]{1,0:T(8,128)(2,1)}, u32[]{:S(2)}) copy-start(bf16[1024,128]{1,0:T(8,128)(2,1)} %refs_5_.1) | copy-start | bytes 786436
  30.7 13.0 %copy-start = (bf16[128,16,128]{2,1,0:T(8,128)(2,1)}, bf16[128,16,128]{2,1,0:T(8,128)(2,1)S(1)}, u32[]{:S(2)}) copy-start(bf16[128,16,128]{2,1,0:T(8,128)(2,1)S(1)} %all-to-all-done.refs_0_.refs_1_) | copy-start | bytes 1572868
  33.9 21.0 %all-to-all-start.1 = ((bf16[128,8,128]{2,1,0:T(8,128)(2,1)}), bf16[128,8,128]{2,1,0:T(8,128)(2,1)S(1)}, u32[]{:S(2)}, u32[]{:S(2)}) async-start(bf16[128,8,128]{2,1,0:T(8,128)(2,1)} %push.1), calls=%async_computation.1 | async-start | bytes 524288 | tf_op jit(solution)/shard_map/all_to_all | solution.py:530
  43.7 11.2 %copy-start.3 = (bf16[128,256]{1,0:T(8,128)(2,1)S(1)}, bf16[128,256]{1,0:T(8,128)(2,1)}, u32[]{:S(2)}) copy-start(bf16[128,256]{1,0:T(8,128)(2,1)} %refs_6_.1) | copy-start | bytes 196612
  43.7 11.2 %copy-start.4 = (bf16[128,256]{1,0:T(8,128)(2,1)S(1)}, bf16[128,256]{1,0:T(8,128)(2,1)}, u32[]{:S(2)}) copy-start(bf16[128,256]{1,0:T(8,128)(2,1)} %refs_7_.1) | copy-start | bytes 196612
  43.7 11.2 %copy-start.5 = (f32[256]{0:T(256)S(1)}, f32[256]{0:T(256)}, u32[]{:S(2)}) copy-start(f32[256]{0:T(256)} %param.13) | copy-start | bytes 3076
  59.1 18.2 %all-to-all-start.2 = ((bf16[128,16,128]{2,1,0:T(8,128)(2,1)}), bf16[128,16,128]{2,1,0:T(8,128)(2,1)S(1)}, u32[]{:S(2)}, u32[]{:S(2)}) async-start(bf16[128,16,128]{2,1,0:T(8,128)(2,1)} %get-tuple-element.43), calls=%async_computation.2 | async-start | bytes 1048576 | tf_op jit(solution)/shard_map/all_to_all | solution.py:530
  77.3 3.3 %copy-start.1 = (bf16[128,16,128]{2,1,0:T(8,128)(2,1)}, bf16[128,16,128]{2,1,0:T(8,128)(2,1)S(1)}, u32[]{:S(2)}) copy-start(bf16[128,16,128]{2,1,0:T(8,128)(2,1)S(1)} %all-to-all-done.2.refs_0_) | copy-start | bytes 1572868
  80.6 18.2 %all-to-all-start.3 = ((bf16[128,16,128]{2,1,0:T(8,128)(2,1)}), bf16[128,16,128]{2,1,0:T(8,128)(2,1)S(1)}, u32[]{:S(2)}, u32[]{:S(2)}) async-start(bf16[128,16,128]{2,1,0:T(8,128)(2,1)} %back_push.1), calls=%async_computation.3 | async-start | bytes 1048576 | tf_op jit(solution)/shard_map/all_to_all | solution.py:530

commit v8 on v7

--- a/solution.py
+++ b/solution.py
@@ -631,6 +631,7 @@
         (got3, gm, base),
         [rows_f32],
         "back_mirror",
+        room=55_000_000,
         flops=2_000_000_000,
         moved=6_000_000,
     )
@@ -640,7 +641,7 @@
         [rows_bf16, ((F, H), F32), ((F, H), F32), ((2, F), F32)],
         "last",
         near=(1,),
-        room=55_700_000,
+        room=55_000_000,
     )
     return act, grad_features, grad_self, grad_neigh, bias_out.reshape(H)
 

time: 102 us -> 101 us (level)
  Pallas kernels: 44.1 us -> 41.1 us
  waiting for transfers between devices: 26.4 us -> 28.4 us
    pallas_call x9, Pallas kernels: 44.1 us -> 41.1 us  [call(): pl.pallas_call(body, out_shape=[jax.ShapeDtypeStruct(s, t) for s, t in ou...]
    all_to_all x4, waiting for transfers between devices: 26.4 us -> 28.4 us  [exchange(): return lax.all_to_all(x, AXES, split_axis=0, concat_axis=0, tiled=True)]
  transfers between devices with their start and end apart: 4 -> 4, of which waited for: 4 -> 4; matrix products, arithmetic and copies ran while one was open for 0% -> 0% of each run, Pallas kernels for 27% -> 25%
where the time goes in v8:
time: 101 us; the launch traced here: 100 us
  Pallas kernels  41.1 us (41%)
  starting transfers between devices  28.9 us (29%)
  waiting for transfers between devices  28.4 us (28%)
  between operations  1.6 us (2%)
    pallas_call x9, Pallas kernels, call(): pl.pallas_call(body, out_shape=[jax.ShapeDtypeStruct(s, t) for s, t in ou...  41.1 us
    all_to_all x4, starting transfers between devices, exchange(): return lax.all_to_all(x, AXES, split_axis=0, concat_axis=0, tiled=True)  28.9 us
    all_to_all x4, waiting for transfers between devices, exchange(): return lax.all_to_all(x, AXES, split_axis=0, concat_axis=0, tiled=True)  28.4 us
  transfers between devices with their start and end apart: 4, of which 4 were waited for; matrix products, arithmetic and copies ran while one was open for 0% of the time, Pallas kernels for 25%

profile of v8, /device:TPU:1, one launch (start us, length us, event | category | flops | bytes accessed | tf_op | source)
XLA Modules:
  0.0 100.2 jit_solution(15376170800760586320)
XLA Ops:
  1.3 3.8 %pull.1 = (bf16[128,16,128]{2,1,0:T(8,128)(2,1)}, s32[64,128]{1,0:T(8,128)}) custom-call(s32[1]{0:T(128)S(6)} %copy.16.refs_0_, s32[8,128]{1,0:T(8,128)} %bitcast.10, s32[64,128]{1,0:T(8,128)} %bitcast.8, s32[64,128]{1,0:T(8,128)} %bitcast.9, bf16[1024,128]{1,0:T(8,128)(2,1)} %refs_5_.1), custom_call_target="tpu_custom_call" | custom-call | tf_op jit(solution)/shard_map/pull/pallas_call | solution.py:517
  5.1 11.5 %all-to-all-start = ((bf16[128,16,128]{2,1,0:T(8,128)(2,1)}), bf16[128,16,128]{2,1,0:T(8,128)(2,1)S(1)}, u32[]{:S(2)}, u32[]{:S(2)}) async-start(bf16[128,16,128]{2,1,0:T(8,128)(2,1)} %get-tuple-element.30), calls=%async_computation | async-start | bytes 1048576 | tf_op jit(solution)/shard_map/all_to_all | solution.py:530
  16.6 11.1 %build.1 = (s32[2048,128]{1,0:T(8,128)}, bf16[1024,1024]{1,0:T(8,128)(2,1)}, bf16[1024,1024]{1,0:T(8,128)(2,1)}, f32[1024,128]{1,0:T(8,128)}, s32[1]{0:T(128)}, ...) custom-call(s32[1]{0:T(128)S(6)} %copy.16.refs_0_, s32[64,128]{1,0:T(8,128)} %get-tuple-element.31.refs_1_, ...), custom_call_target="tpu_custom_call" | custom-call | flops 20000000000 | bytes 20000000 | tf_op jit(solution)/shard_map/build/pallas_call | solution.py:517
  27.7 0.0 copy-start.5
  27.7 0.0 copy-start.1
  27.7 3.0 %all-to-all-done.refs_0_.refs_1_ = bf16[128,16,128]{2,1,0:T(8,128)(2,1)S(1)} async-done(((bf16[128,16,128]{2,1,0:T(8,128)(2,1)}), bf16[128,16,128]{2,1,0:T(8,128)(2,1)S(1)}, u32[]{:S(2)}, u32[]{:S(2)}) %all-to-all-start) | async-done | bytes 524320 | tf_op jit(solution)/shard_map/all_to_all | solution.py:530
  30.7 0.0 copy-start
  30.7 3.2 %push.1 = bf16[128,8,128]{2,1,0:T(8,128)(2,1)} custom-call(bf16[128,16,128]{2,1,0:T(8,128)(2,1)S(1)} %all-to-all-done.refs_0_.refs_1_, f32[1024,128]{1,0:T(8,128)} %get-tuple-element.32.refs_1_, bf16[1024,1024]{1,0:T(8,128)(2,1)} %get-tuple-element.33.refs_2_.refs_1_), custom_call_target="tpu_custom_call" | custom-call | tf_op jit(solution)/shard_map/push/pallas_call | solution.py:517
  33.9 9.3 %all-to-all-start.1 = ((bf16[128,8,128]{2,1,0:T(8,128)(2,1)}), bf16[128,8,128]{2,1,0:T(8,128)(2,1)S(1)}, u32[]{:S(2)}, u32[]{:S(2)}) async-start(bf16[128,8,128]{2,1,0:T(8,128)(2,1)} %push.1), calls=%async_computation.1 | async-start | bytes 524288 | tf_op jit(solution)/shard_map/all_to_all | solution.py:530
  43.2 0.0 copy-done.5
  43.2 0.1 copy.15
  43.3 0.1 reshape.27.refs_1_.refs_0_
  43.4 0.0 copy-done
  43.4 0.0 copy-done.1
  43.4 0.0 copy-start.2
  43.4 0.0 copy-start.3
  43.5 0.0 copy-start.4
  43.5 5.5 %local.1 = (bf16[128,1024]{1,0:T(8,128)(2,1)S(1)}, bf16[1024,128]{1,0:T(8,128)(2,1)S(1)}, f32[1024,128]{1,0:T(8,128)}, bf16[1024,128]{1,0:T(8,128)(2,1)S(1)}) custom-call(s32[1]{0:T(128)} %get-tuple-element.34.refs_0_, bf16[128,16,128]{2,1,0:T(8,128)(2,1)} %copy-done, bf16[1024,128]{1,0:T(8,128)(2,1)S(1)} %copy-done.1, ...), custom_call_target="tpu_custom_call" | custom-call | flops 2000000000 | bytes 6000000 | tf_op jit(solution)/shard_map/local/pallas_call | solution.py:517
  48.9 5.7 %all-to-all-done.1.refs_0_ = bf16[128,8,128]{2,1,0:T(8,128)(2,1)S(1)} async-done(((bf16[128,8,128]{2,1,0:T(8,128)(2,1)}), bf16[128,8,128]{2,1,0:T(8,128)(2,1)S(1)}, u32[]{:S(2)}, u32[]{:S(2)}) %all-to-all-start.1) | async-done | bytes 262176 | tf_op jit(solution)/shard_map/all_to_all | solution.py:530
  54.7 0.0 copy-done.2
  54.7 0.0 copy-done.3
  54.7 0.0 copy-done.4
  54.7 4.2 %dense.1 = (bf16[1024,256]{1,0:T(8,128)(2,1)}, f32[1024,128]{1,0:T(8,128)}, f32[1024,128]{1,0:T(8,128)}, bf16[128,16,128]{2,1,0:T(8,128)(2,1)}, f32[8,128]{1,0:T(8,128)S(1)}) custom-call(bf16[128,8,128]{2,1,0:T(8,128)(2,1)S(1)} %all-to-all-done.1.refs_0_, s32[1,1024]{1,0:T(1,128)S(1)} %reshape.27.refs_1_.refs_0_, ...), custom_call_target="tpu_custom_call" | custom-call | tf_op jit(solution)/shard_map/dense/pallas_call | solution.py:517
  58.9 4.1 %all-to-all-start.2 = ((bf16[128,16,128]{2,1,0:T(8,128)(2,1)}), bf16[128,16,128]{2,1,0:T(8,128)(2,1)S(1)}, u32[]{:S(2)}, u32[]{:S(2)}) async-start(bf16[128,16,128]{2,1,0:T(8,128)(2,1)} %get-tuple-element.43), calls=%async_computation.2 | async-start | bytes 1048576 | tf_op jit(solution)/shard_map/all_to_all | solution.py:530
  63.0 6.2 %back_local.1 = (bf16[1024,1024]{1,0:T(8,128)(2,1)}, f32[1024,128]{1,0:T(8,128)}, f32[1024,128]{1,0:T(8,128)}) custom-call(s32[1]{0:T(128)} %get-tuple-element.34.refs_0_, bf16[1024,1024]{1,0:T(8,128)(2,1)} %get-tuple-element.33.refs_2_.refs_1_, f32[1024,128]{1,0:T(8,128)} %get-tuple-element.44.refs_2_, s32[2048,128]{1,0:T(8,128)} %get-tuple-element.35.refs_3_, ...), custom_call_target="tpu_custom_call" | custom-call | flops 2000000000 | bytes 6000000 | tf_op jit(solution)/shard_map/back_local/pallas_call | solution.py:517
  69.2 7.9 %all-to-all-done.2.refs_0_ = bf16[128,16,128]{2,1,0:T(8,128)(2,1)S(1)} async-done(((bf16[128,16,128]{2,1,0:T(8,128)(2,1)}), bf16[128,16,128]{2,1,0:T(8,128)(2,1)S(1)}, u32[]{:S(2)}, u32[]{:S(2)}) %all-to-all-start.2) | async-done | bytes 524320 | tf_op jit(solution)/shard_map/all_to_all | solution.py:530
  77.1 3.1 %back_push.1 = bf16[128,16,128]{2,1,0:T(8,128)(2,1)} custom-call(bf16[128,16,128]{2,1,0:T(8,128)(2,1)S(1)} %all-to-all-done.2.refs_0_, f32[1024,128]{1,0:T(8,128)} %get-tuple-element.46.refs_1_, f32[8,128]{1,0:T(8,128)S(1)} %get-tuple-element.47.refs_2_, bf16[1024,1024]{1,0:T(8,128)(2,1)} %get-tuple-element.48.refs_3_), custom_call_target="tpu_custom_call" | custom-call | tf_op jit(solution)/shard_map/back_push/pallas_call | solution.py:517
  80.1 4.0 %all-to-all-start.3 = ((bf16[128,16,128]{2,1,0:T(8,128)(2,1)}), bf16[128,16,128]{2,1,0:T(8,128)(2,1)S(1)}, u32[]{:S(2)}, u32[]{:S(2)}) async-start(bf16[128,16,128]{2,1,0:T(8,128)(2,1)} %back_push.1), calls=%async_computation.3 | async-start | bytes 1048576 | tf_op jit(solution)/shard_map/all_to_all | solution.py:530
  84.2 2.3 %back_mirror.1.refs_2_ = f32[1024,128]{1,0:T(8,128)S(1)} custom-call(bf16[128,16,128]{2,1,0:T(8,128)(2,1)S(1)} %all-to-all-done.2.refs_0_, bf16[1024,1024]{1,0:T(8,128)(2,1)} %get-tuple-element.49.refs_1_, f32[1024,128]{1,0:T(8,128)} %get-tuple-element.50.refs_2_), custom_call_target="tpu_custom_call" | custom-call | flops 2000000000 | bytes 6000000 | tf_op jit(solution)/shard_map/back_mirror/pallas_call | solution.py:517
  86.5 11.9 %all-to-all-done.3.refs_1_ = bf16[128,16,128]{2,1,0:T(8,128)(2,1)S(1)} async-done(((bf16[128,16,128]{2,1,0:T(8,128)(2,1)}), bf16[128,16,128]{2,1,0:T(8,128)(2,1)S(1)}, u32[]{:S(2)}, u32[]{:S(2)}) %all-to-all-start.3) | async-done | bytes 524320 | tf_op jit(solution)/shard_map/all_to_all | solution.py:530
  98.4 1.7 %last.1 = (bf16[1024,128]{1,0:T(8,128)(2,1)}, f32[128,256]{1,0:T(8,128)}, f32[128,256]{1,0:T(8,128)}, f32[2,128]{1,0:T(2,128)}) custom-call(s32[1,1024]{1,0:T(1,128)S(1)} %reshape.27.refs_1_.refs_0_, bf16[128,16,128]{2,1,0:T(8,128)(2,1)S(1)} %all-to-all-done.3.refs_1_, f32[1024,128]{1,0:T(8,128)S(1)} %back_mirror.1.refs_2_), custom_call_target="tpu_custom_call" | custom-call | tf_op jit(solution)/shard_map/last/pallas_call | solution.py:517
Async XLA Ops:
  5.1 25.6 %all-to-all-start = ((bf16[128,16,128]{2,1,0:T(8,128)(2,1)}), bf16[128,16,128]{2,1,0:T(8,128)(2,1)S(1)}, u32[]{:S(2)}, u32[]{:S(2)}) async-start(bf16[128,16,128]{2,1,0:T(8,128)(2,1)} %get-tuple-element.30), calls=%async_computation | async-start | bytes 1048576 | tf_op jit(solution)/shard_map/all_to_all | solution.py:530
  27.7 15.5 %copy-start.5 = (s32[1,128,8]{1,2,0:T(8,128)S(1)}, s32[1,128,8]{1,2,0:T(8,128)}, u32[]{:S(2)}) copy-start(s32[1,128,8]{1,2,0:T(8,128)} %param.17) | copy-start | bytes 12292
  27.7 15.7 %copy-start.1 = (bf16[1024,128]{1,0:T(8,128)(2,1)S(1)}, bf16[1024,128]{1,0:T(8,128)(2,1)}, u32[]{:S(2)}) copy-start(bf16[1024,128]{1,0:T(8,128)(2,1)} %refs_5_.1) | copy-start | bytes 786436
  30.7 12.7 %copy-start = (bf16[128,16,128]{2,1,0:T(8,128)(2,1)}, bf16[128,16,128]{2,1,0:T(8,128)(2,1)S(1)}, u32[]{:S(2)}) copy-start(bf16[128,16,128]{2,1,0:T(8,128)(2,1)S(1)} %all-to-all-done.refs_0_.refs_1_) | copy-start | bytes 1572868
  33.9 20.7 %all-to-all-start.1 = ((bf16[128,8,128]{2,1,0:T(8,128)(2,1)}), bf16[128,8,128]{2,1,0:T(8,128)(2,1)S(1)}, u32[]{:S(2)}, u32[]{:S(2)}) async-start(bf16[128,8,128]{2,1,0:T(8,128)(2,1)} %push.1), calls=%async_computation.1 | async-start | bytes 524288 | tf_op jit(solution)/shard_map/all_to_all | solution.py:530
  43.4 11.2 %copy-start.2 = (bf16[128,256]{1,0:T(8,128)(2,1)S(1)}, bf16[128,256]{1,0:T(8,128)(2,1)}, u32[]{:S(2)}) copy-start(bf16[128,256]{1,0:T(8,128)(2,1)} %refs_6_.1) | copy-start | bytes 196612
  43.4 11.2 %copy-start.3 = (bf16[128,256]{1,0:T(8,128)(2,1)S(1)}, bf16[128,256]{1,0:T(8,128)(2,1)}, u32[]{:S(2)}) copy-start(bf16[128,256]{1,0:T(8,128)(2,1)} %refs_7_.1) | copy-start | bytes 196612
  43.5 11.2 %copy-start.4 = (f32[256]{0:T(256)S(1)}, f32[256]{0:T(256)}, u32[]{:S(2)}) copy-start(f32[256]{0:T(256)} %param.13) | copy-start | bytes 3076
  58.9 18.2 %all-to-all-start.2 = ((bf16[128,16,128]{2,1,0:T(8,128)(2,1)}), bf16[128,16,128]{2,1,0:T(8,128)(2,1)S(1)}, u32[]{:S(2)}, u32[]{:S(2)}) async-start(bf16[128,16,128]{2,1,0:T(8,128)(2,1)} %get-tuple-element.43), calls=%async_computation.2 | async-start | bytes 1048576 | tf_op jit(solution)/shard_map/all_to_all | solution.py:530
  80.1 18.2 %all-to-all-start.3 = ((bf16[128,16,128]{2,1,0:T(8,128)(2,1)}), bf16[128,16,128]{2,1,0:T(8,128)(2,1)S(1)}, u32[]{:S(2)}, u32[]{:S(2)}) async-start(bf16[128,16,128]{2,1,0:T(8,128)(2,1)} %back_push.1), calls=%async_computation.3 | async-start | bytes 1048576 | tf_op jit(solution)/shard_map/all_to_all | solution.py:530
